TPU v7x, 32 devices: a whole 2x2x4 slice. The times are simulated.
32 devices in a mesh: beam: 2 (over x), freq: 8 (over z, y), tm: 2 (over core).
Axes of the slice: x: 2, y: 2, z: 4, core: 2. Of those that a mesh axis runs over, the one named last changes fastest.
Arguments:
- spectra: float32 [4096, 5120], P(('beam', 'freq'), 'tm'), parts along dimension 0, may hold values from -6 to 6
- delays: int32 [11, 2048], replicated, may hold values from 0 to 1024, as said below
- widths: int32 [8], replicated, may hold values from 1 to 128, as said below
Outputs:
- filtered: float32 [8, 4096, 5120], P(None, ('beam', 'freq'), 'tm'), parts along dimension 1
There are 2 independent parts, one for each index of `beam`. A program takes and returns all parts, laid end to end along the dimension named above; an argument that names none is the same for every part. Nothing has to cross between parts.
Inputs may be any that keep to these rules, and one draw needn't show every extreme that they name: delays[l, r] lies in 0 to 2 ** l, and every level l has some entry equal to 2 ** l. The widths include 1 and 128.
All inputs are finite; a program needn't handle non-finite values.
Results may differ from a plain program's by a relative error of at most 0.0003.
Values sent between devices are 32-bit elements; how exact they have to be, the bound alone decides.
No kernel may reach another device: no remote copies, remote signals or barrier semaphores. Data moves between devices by JAX's collectives and lax.ppermute only.
A program may use at most 192 MiB of HBM per device.

v0:
```python
import jax
import jax.numpy as jnp
from jax import lax
from jax.sharding import PartitionSpec as P

F = 2048
TAPS = 128


def passed_along(value, axis, steps):
    count = lax.axis_size(axis)
    initial, last = (max(0, -steps), min(count, count - steps))
    return lax.ppermute(value, axis, [(source, source + steps) for source in range(initial, last)])


def from_partner(value, axis, stride):
    mask = 2**stride
    pairs = [(source, source ^ mask) for source in range(lax.axis_size(axis))]
    return lax.ppermute(value, axis, pairs)


def delay_rows(source_rows, row_shifts, out_width):
    total_width = source_rows.shape[1]
    top_reach = total_width - out_width
    shift_col = row_shifts[:, None]
    low_part = shift_col % top_reach
    result = source_rows
    bit_value = 1
    while bit_value < top_reach:
        width_now = result.shape[1]
        chosen = low_part // bit_value % 2 == 1
        result = jnp.where(chosen, result[:, bit_value:], result[:, : width_now - bit_value])
        bit_value = bit_value * 2
    lower_shift = result[:, :out_width]
    top_shift = source_rows[:, top_reach : top_reach + out_width]
    return jnp.where(shift_col == top_reach, top_shift, lower_shift)


def delay_block(current, row_shifts, half_rows, out_width):
    row_count, total_width = current.shape
    group_count = row_count // (2 * half_rows)
    block_view = current.reshape(group_count, 2, half_rows, total_width)
    source_rows = jnp.broadcast_to(
        block_view[:, 1][:, None], (group_count, 2, half_rows, total_width)
    )
    delayed = delay_rows(source_rows.reshape(row_count, total_width), row_shifts, out_width)
    summed = block_view[:, 0, :, :out_width][:, None] + delayed.reshape(
        group_count, 2, half_rows, out_width
    )
    return summed.reshape(row_count, out_width)


def local(spectra, delays, widths):
    row_count, time_span = spectra.shape
    local_levels = row_count.bit_length() - 1
    freq_count = lax.axis_size("freq")
    cross_levels = freq_count.bit_length() - 1
    position = lax.axis_index("freq")

    def own_shifts(tree_level):
        return lax.dynamic_slice_in_dim(delays[tree_level], position * row_count, row_count)

    current = spectra
    rim_depth = 2**local_levels - 1
    leading = passed_along(current[:, :rim_depth], "tm", -1)
    current = jnp.concatenate([current, leading], axis=1)
    for tree_level in range(local_levels):
        current = delay_block(
            current, own_shifts(tree_level), 2**tree_level, current.shape[1] - 2**tree_level
        )
    for bit_index in range(cross_levels):
        tree_level = local_levels + bit_index
        reach = 2**tree_level
        leading = passed_along(current[:, :reach], "tm", -1)
        own_ext = jnp.concatenate([current, leading], axis=1)
        partner_ext = from_partner(own_ext, "freq", bit_index)
        is_lower = position // 2**bit_index % 2 == 0
        first_term = jnp.where(is_lower, own_ext[:, :time_span], partner_ext[:, :time_span])
        second_source = jnp.where(is_lower, partner_ext, own_ext)
        current = first_term + delay_rows(second_source, own_shifts(tree_level), time_span)
    leading = passed_along(current[:, :TAPS], "tm", -1)
    extended = jnp.concatenate([current, leading], axis=1)
    block_count = time_span // TAPS
    block_view = extended.reshape(row_count, block_count + 1, TAPS)
    paired = jnp.concatenate([block_view[:, :-1], block_view[:, 1:]], axis=2)
    filter_count = widths.shape[0]
    input_pos = lax.broadcasted_iota(jnp.int32, (2 * TAPS, filter_count, TAPS), 0)
    output_pos = lax.broadcasted_iota(jnp.int32, (2 * TAPS, filter_count, TAPS), 2)
    distance = input_pos - output_pos
    box_widths = widths[None, :, None]
    scaling = 1.0 / jnp.sqrt(widths.astype(jnp.float32) * F)
    filter_matrix = jnp.where(
        (distance >= 0) & (distance < box_widths), scaling[None, :, None], 0.0
    )
    filter_matrix = filter_matrix.reshape(2 * TAPS, filter_count * TAPS)
    product = jnp.einsum("rbj,jk->rbk", paired, filter_matrix, precision=lax.Precision.HIGHEST)
    product = product.reshape(row_count, block_count, filter_count, TAPS)
    return jnp.transpose(product, (2, 0, 1, 3)).reshape(filter_count, row_count, time_span)


def solution(mesh):
    return jax.shard_map(
        local,
        mesh=mesh,
        in_specs=(P(("beam", "freq"), "tm"), P(), P()),
        out_specs=P(None, ("beam", "freq"), "tm"),
        check_vma=False,
    )
```

profile of v0, /device:TPU:0, one launch (start us, length us, event | category | flops | bytes accessed | tf_op | source)
XLA Modules:
  0.0 525.4 jit_solution(16496791616469396781)
XLA Ops:
  6.6 3.5 pad_maximum_fusion.2
  10.1 3.5 reshape.3247
  16.1 4.8 slice_reduce_fusion
  21.0 3.1 add.1172
  26.8 3.6 broadcast_in_dim.600
  32.8 3.9 reshape.3248
  36.7 2.8 broadcast_add_fusion
  41.3 2.8 add.1178
  44.1 3.6 broadcast_in_dim.604
  47.8 3.6 reshape.3249
  52.3 2.7 fusion.6
  55.0 4.6 reshape.3250
  59.7 3.7 copy_add_fusion
  70.8 3.0 reshape.3251
  73.8 3.3 add.1183
  77.1 4.6 add.1184
  120.2 5.5 %add.1228 = f32[2,128,2560]{1,0,2:T(2,128)S(1)} broadcast(f32[128,2560]{0,1:T(8,128)S(1)} %copy.31), dimensions={1,2} | broadcast | bytes 3932160 | tf_op jit(solution)/shard_map/add | solution.py:47
  132.0 3.0 collective-permute-start.2
  135.0 63.0 %collective-permute-done.2 = f32[256,2816]{0,1:T(8,128)} collective-permute-done((f32[256,2816]{0,1:T(8,128)}, f32[256,2816]{0,1:T(8,128)}, u32[]{:S(2)}, u32[]{:S(2)}) %collective-permute-start.2) | collective-permute-done | bytes 2883616 | tf_op jit(solution)/shard_map/ppermute | solution.py:19
  203.6 2.8 fusion.13
  214.7 68.0 %collective-permute-done.4 = f32[256,3072]{0,1:T(8,128)} collective-permute-done((f32[256,3072]{0,1:T(8,128)}, f32[256,3072]{0,1:T(8,128)}, u32[]{:S(2)}, u32[]{:S(2)}) %collective-permute-start.4) | collective-permute-done | bytes 3145760 | tf_op jit(solution)/shard_map/ppermute | solution.py:19
  288.7 2.8 fusion.11
  293.1 3.0 collective-permute-done.5
  298.3 2.8 collective-permute-start.6
  301.1 157.7 %collective-permute-done.6 = f32[256,3584]{0,1:T(8,128)} collective-permute-done((f32[256,3584]{0,1:T(8,128)}, f32[256,3584]{0,1:T(8,128)}, u32[]{:S(2)}, u32[]{:S(2)}) %collective-permute-start.6) | collective-permute-done | bytes 3670048 | tf_op jit(solution)/shard_map/ppermute | solution.py:19
  458.8 2.8 broadcast_select_fusion
  464.5 2.8 fusion.9
  470.8 3.0 fusion.149
  475.9 3.2 copy.43
  479.1 18.6 %convolution_bitcast_fusion = f32[8,256,20,128]{1,3,0,2:T(8,128)S(1)} fusion(f32[256,20,128]{2,0,1:T(8,128)} %copy.43, f32[256,20,128]{2,0,1:T(8,128)S(1)} %copy.42, f32[8]{0:T(128)S(1)} %multiply_rsqrt_fusion, s32[8]{0:T(128)S(1)} %copy-done.14), kind=kOutput, calls=%fused_computation | convolution fusion | flops 16108748800 | bytes 26214464 | tf_op jit(solution)/shard_map/rbj,jk->rbk/dot_general | solution.py:96
  497.7 7.4 %copy.35 = f32[8,256,20,128]{1,3,2,0:T(8,128)} copy(f32[8,256,20,128]{1,3,0,2:T(8,128)S(1)} %convolution_bitcast_fusion) | data formatting | bytes 41943040 | tf_op jit(solution)/shard_map/transpose | solution.py:98
  505.1 19.9 %copy.36 = f32[8,256,2560]{2,1,0:T(8,128)} copy(f32[8,256,2560]{1,2,0:T(8,128)} %bitcast.83) | data formatting | bytes 41943040 | tf_op jit(solution)/shard_map/reshape | solution.py:98
  (180 shorter events, 100.6 us)
Async XLA Ops:
  1.0 5.6 %collective-permute-start = (f32[256,255]{1,0:T(8,128)S(1)}, f32[256,255]{1,0:T(8,128)S(1)}, u32[]{:S(2)}, u32[]{:S(2)}) collective-permute-start(f32[256,255]{1,0:T(8,128)S(1)} %slice.507), channel_id=1, source_target_pairs={{1,0},{3,2},{5,4},{7,6},{9,8},{11,10},{13,12},{15,14},{17,16},{19,... | collective-permute-start | bytes 783368 | tf_op jit(solution)/shard_map/ppermute | solution.py:13
  21.0 3.1 copy-start.6
  55.0 4.6 copy-start.4
  83.5 1.8 copy-start.5
  117.7 0.7 copy-start.11
  118.4 0.6 copy-start.10
  119.0 0.7 copy-start.9
  120.2 5.5 %copy-start.12 = (pred[256]{0:T(512)(128)(4,1)S(1)}, pred[256]{0:T(512)(128)(4,1)}, u32[]{:S(2)}) copy-start(pred[256]{0:T(512)(128)(4,1)} %get-tuple-element.14) | copy-start | bytes 772
  120.2 5.5 %copy-start.13 = (pred[256]{0:T(512)(128)(4,1)S(1)}, pred[256]{0:T(512)(128)(4,1)}, u32[]{:S(2)}) copy-start(pred[256]{0:T(512)(128)(4,1)} %get-tuple-element.101) | copy-start | bytes 772
  126.7 71.3 %copy-start.2 = (f32[256,2560]{0,1:T(8,128)}, f32[256,2560]{0,1:T(8,128)S(1)}, u32[]{:S(2)}) copy-start(f32[256,2560]{0,1:T(8,128)S(1)} %bitcast_add_fusion) | copy-start | bytes 7864324
  126.8 8.2 %copy-start.8 = (s32[1,256]{1,0:T(1,128)S(1)}, s32[1,256]{1,0:T(1,128)}, u32[]{:S(2)}) copy-start(s32[1,256]{1,0:T(1,128)} %get-tuple-element.119) | copy-start | bytes 3076
  126.8 3.4 collective-permute-start.1
  132.0 66.1 %collective-permute-start.2 = (f32[256,2816]{0,1:T(8,128)}, f32[256,2816]{0,1:T(8,128)}, u32[]{:S(2)}, u32[]{:S(2)}) collective-permute-start(f32[256,2816]{0,1:T(8,128)} %pad_maximum_fusion.3), channel_id=1, source_target_pairs={{0,2},{2,0},{4,6},{6,4},{8,10},{10,8},{12,14},{14,12},{1,3},{3,1},... | collective-permute-start | bytes 8650760 | tf_op jit(solution)/shard_map/ppermute | solution.py:19
  201.9 1.7 copy-start.3
  206.4 76.2 %copy-start = (f32[256,2560]{0,1:T(8,128)}, f32[256,2560]{0,1:T(8,128)S(1)}, u32[]{:S(2)}) copy-start(f32[256,2560]{0,1:T(8,128)S(1)} %fusion.13) | copy-start | bytes 7864324
  206.4 3.8 collective-permute-start.3
  212.1 70.5 %collective-permute-start.4 = (f32[256,3072]{0,1:T(8,128)}, f32[256,3072]{0,1:T(8,128)}, u32[]{:S(2)}, u32[]{:S(2)}) collective-permute-start(f32[256,3072]{0,1:T(8,128)} %pad_maximum_fusion.1), channel_id=1, source_target_pairs={{0,4},{2,6},{4,0},{6,2},{8,12},{10,14},{12,8},{14,10},{1,5},{3,7},... | collective-permute-start | bytes 9437192 | tf_op jit(solution)/shard_map/ppermute | solution.py:19
  287.0 1.7 copy-start.1
  291.5 4.6 collective-permute-start.5
  296.1 2.2 copy-start.7
  298.3 160.5 %collective-permute-start.6 = (f32[256,3584]{0,1:T(8,128)}, f32[256,3584]{0,1:T(8,128)}, u32[]{:S(2)}, u32[]{:S(2)}) collective-permute-start(f32[256,3584]{0,1:T(8,128)} %pad_maximum_fusion), channel_id=1, source_target_pairs={{0,8},{2,10},{4,12},{6,14},{8,0},{10,2},{12,4},{14,6},{1,9},{3,11}... | collective-permute-start | bytes 11010056 | tf_op jit(solution)/shard_map/ppermute | solution.py:19
  464.5 4.1 copy-start.14
  467.3 3.2 collective-permute-start.7
where the time goes:
time: 535 us; the launch traced here: 525 us
  waiting for transfers between devices  298 us (56%)
  local copies, waits for them, and re-layouts  124 us (23%)
  other arithmetic  69.2 us (13%)
  matrix products  18.6 us (3%)
  starting transfers between devices  14.4 us (3%)
    ppermute x3, waiting for transfers between devices, from_partner(): return lax.ppermute(value, axis, pairs)  289 us
    add x19, local copies, waits for them, and re-layouts, delay_block(): block_view[:, 0, :, :out_width][:, None]  26 us
    select_n x45, other arithmetic, delay_rows(): jnp.where(chosen, result[:, bit_value:], result[:, :width_now - bit_value])  20.9 us
    reshape x1, local copies, waits for them, and re-layouts, local(): jnp.transpose(product, (2, 0, 1, 3))  19.9 us
    dot_general x1, matrix products, local(): jnp.einsum('rbj,jk->rbk', paired, filter_matrix, precision=lax.Precision....  18.6 us
    broadcast_in_dim x17, local copies, waits for them, and re-layouts, delay_block(): jnp.broadcast_to(block_view[:, 1][:, None], (group_count, 2, half_rows, t...  16.8 us
    select_n x7, other arithmetic, delay_rows(): return jnp.where(shift_col == top_reach, top_shift, lower_shift)  12.1 us
  transfers between devices with their start and end apart: 8, of which 7 were waited for; matrix products, arithmetic and copies ran while one was open for 1% of the time, Pallas kernels for 0%

commit v1 on v0

--- a/solution.py
+++ b/solution.py
@@ -1,16 +1,448 @@
+import functools
+
 import jax
 import jax.numpy as jnp
 from jax import lax
+from jax.experimental import pallas as pl
+from jax.experimental.pallas import tpu as pltpu
 from jax.sharding import PartitionSpec as P
 
-F = 2048
+LANES = 128
+SUBLANES = 8
 TAPS = 128
+CHUNKS = 2
+VMEM_LIMIT = 48 * 2**20
+
+
+def lane_gather(block, index):
+    return jnp.take_along_axis(block, index, axis=1, mode="promise_in_bounds")
+
+
+def shift_plan(shifts, level):
+    block_choices = max(1, 2**level // LANES)
+    whole = jnp.minimum(shifts >> 7, block_choices - 1)
+    reach = lax.broadcasted_iota(jnp.int32, shifts.shape, 1) + shifts - (whole << 7)
+    return whole, reach & (LANES - 1), reach < LANES
+
+
+def add_delayed(load_a, load_b, stores, shift_pair, level, in_blocks, out_blocks):
+    block_choices = max(1, 2**level // LANES)
+    plans = [shift_plan(shifts, level) for shifts in shift_pair]
+    bits = block_choices.bit_length() - 1
+    wanted = [[(whole & 2**bit) != 0 for bit in range(bits)] for whole, _, _ in plans]
+    kept = {}
+
+    def source(side, stage, j):
+        if stage == 0:
+            side = 0
+        key = (side, stage, j)
+        if key not in kept:
+            if stage == 0:
+                kept[key] = load_b(j)
+            else:
+                step = 2 ** (stage - 1)
+                kept[key] = jnp.where(
+                    wanted[side][stage - 1],
+                    source(side, stage - 1, j + step),
+                    source(side, stage - 1, j),
+                )
+        return kept[key]
+
+    def turned(side, j):
+        if j + block_choices > in_blocks:
+            return jnp.zeros((SUBLANES, LANES), jnp.float32)
+        return lane_gather(source(side, bits, j), plans[side][1])
+
+    held = [turned(side, 0) for side in range(2)]
+    for j in range(out_blocks):
+        first = load_a(j)
+        following = [turned(side, j + 1) for side in range(2)]
+        for side in range(2):
+            stores[side](j, first + jnp.where(plans[side][2], held[side], following[side]))
+        held = following
+
+
+def column(table_rows, level):
+    return jnp.broadcast_to(table_rows[:, level : level + 1], (SUBLANES, LANES))
+
+
+def block_of(j):
+    return slice(j * LANES, (j + 1) * LANES)
+
+
+def local_tree_kernel(freq_count, chunks, place, spectra, rim, table, *refs):
+    rows, span = spectra.shape
+    blocks, rim_blocks = span // LANES, rim.shape[1] // LANES
+    total = blocks + rim_blocks
+    outs, (work, done, in_sem, out_sem) = refs[: freq_count * chunks], refs[freq_count * chunks :]
+    mine = place[0]
+    loads = [
+        pltpu.make_async_copy(
+            spectra.at[:, block_of(j)] if j < blocks else rim.at[:, block_of(j - blocks)],
+            work.at[j],
+            in_sem.at[j],
+        )
+        for j in range(total)
+    ]
+    for load in loads:
+        load.start()
+    for load in loads:
+        load.wait()
+    levels = rows.bit_length() - 1
+    pairs = rows // (2 * SUBLANES)
+    for level in range(levels):
+        half = 2**level
+        last = level == levels - 1
+
+        def step(pair, carry, level=level, half=half, last=last):
+            if half < SUBLANES:
+                group, member = pair // 4, pair % 4
+                member = (member // half) * 2 * half + member % half
+                starts = [group * 64 + member + e * half for e in range(2)]
+                spots = [pl.ds(start, SUBLANES, stride=SUBLANES) for start in starts]
+                from_table = [
+                    pl.ds(mine * rows + start, SUBLANES, stride=SUBLANES) for start in starts
+                ]
+            else:
+                tiles = half // SUBLANES
+                tile = (pair // tiles) * 2 * tiles + pair % tiles
+                starts = [
+                    pl.multiple_of((tile + e * tiles) * SUBLANES, SUBLANES) for e in range(2)
+                ]
+                spots = [pl.ds(start, SUBLANES) for start in starts]
+                from_table = [
+                    pl.ds(pl.multiple_of(mine * rows + start, SUBLANES), SUBLANES)
+                    for start in starts
+                ]
+            shifts = [column(table[spot, :], level) for spot in from_table]
+
+            def load(e):
+                return lambda j: work[j, spots[e], :]
+
+            def store(e):
+                def put(j, value):
+                    if last:
+                        done[spots[e], block_of(j)] = value
+                    else:
+                        work[j, spots[e], :] = value
+
+                return put
+
+            add_delayed(
+                load(0), load(1), [store(0), store(1)], shifts, level, total, blocks if last else total
+            )
+            return carry
+
+        lax.fori_loop(0, pairs, step, 0)
+    share = rows // chunks // freq_count
+    stores = []
+    for chunk in range(chunks):
+        for mask in range(freq_count):
+            n = chunk * freq_count + mask
+            start = chunk * (rows // chunks) + jnp.bitwise_xor(mine, mask) * share
+            stores.append(
+                pltpu.make_async_copy(
+                    done.at[pl.ds(pl.multiple_of(start, SUBLANES), share), :], outs[n], out_sem.at[n]
+                )
+            )
+    for store in stores:
+        store.start()
+    for store in stores:
+        store.wait()
+
+
+def local_tree(position, spectra, rim, table, freq_count, chunks):
+    rows, span = spectra.shape
+    count = freq_count * chunks
+    total = (span + rim.shape[1]) // LANES
+    share = jax.ShapeDtypeStruct((rows // count, span), jnp.float32)
+    hbm = pl.BlockSpec(memory_space=pl.ANY)
+    return pl.pallas_call(
+        functools.partial(local_tree_kernel, freq_count, chunks),
+        out_shape=[share] * count,
+        in_specs=[
+            pl.BlockSpec(memory_space=pltpu.SMEM),
+            hbm,
+            hbm,
+            pl.BlockSpec(memory_space=pltpu.VMEM),
+        ],
+        out_specs=[hbm] * count,
+        scratch_shapes=[
+            pltpu.VMEM((total, rows, LANES), jnp.float32),
+            pltpu.VMEM((rows, span), jnp.float32),
+            pltpu.SemaphoreType.DMA((total,)),
+            pltpu.SemaphoreType.DMA((count,)),
+        ],
+        compiler_params=pltpu.CompilerParams(vmem_limit_bytes=VMEM_LIMIT),
+        cost_estimate=pl.CostEstimate(
+            flops=8 * rows * span, bytes_accessed=8 * rows * span, transcendentals=0
+        ),
+        name="local_tree",
+    )(position, spectra, rim, table)
+
+
+def cross_tree_kernel(rows, chunk, chunks, place, table, rim, *refs):
+    freq_count = rim.shape[0]
+    parts, outs = refs[:freq_count], refs[freq_count : 2 * freq_count]
+    work, done, in_sem, out_sem = refs[2 * freq_count :]
+    share, span = parts[0].shape
+    rim_span = rim.shape[2]
+    blocks = (span + rim_span) // LANES
+    mine = place[0]
+    loads = []
+    for mask in range(freq_count):
+        owner = jnp.bitwise_xor(mine, mask)
+        loads.append(
+            pltpu.make_async_copy(
+                parts[mask], work.at[owner, :, pl.ds(0, span)], in_sem.at[0, mask]
+            )
+        )
+        loads.append(
+            pltpu.make_async_copy(
+                rim.at[mask], work.at[owner, :, pl.ds(span, rim_span)], in_sem.at[1, mask]
+            )
+        )
+    for load in loads:
+        load.start()
+    for load in loads:
+        load.wait()
+    base = chunk * (rows // chunks) + mine * share
+    levels = freq_count.bit_length() - 1
+    tiles = share // SUBLANES
+    for bit in range(levels):
+        level = rows.bit_length() - 1 + bit
+        out_blocks = blocks - 2**level // LANES
+        last = bit == levels - 1
+
+        def step(item, carry, bit=bit, level=level, blocks=blocks, out_blocks=out_blocks, last=last):
+            pair, tile = item // tiles, item % tiles
+            first = (pair // 2**bit) * 2 * 2**bit + pair % 2**bit
+            owners = [first, first + 2**bit]
+            spot = pl.ds(pl.multiple_of(tile * SUBLANES, SUBLANES), SUBLANES)
+            shifts = [
+                column(
+                    table[
+                        pl.ds(
+                            pl.multiple_of(owner * rows + base + tile * SUBLANES, SUBLANES), SUBLANES
+                        ),
+                        :,
+                    ],
+                    level,
+                )
+                for owner in owners
+            ]
+
+            def load(e):
+                return lambda j: work[owners[e], spot, block_of(j)]
+
+            def store(e):
+                def put(j, value):
+                    if last:
+                        done[owners[e], spot, block_of(j)] = value
+                    else:
+                        work[owners[e], spot, block_of(j)] = value
+
+                return put
+
+            add_delayed(
+                load(0), load(1), [store(0), store(1)], shifts, level, blocks, out_blocks
+            )
+            return carry
+
+        lax.fori_loop(0, freq_count // 2 * tiles, step, 0)
+        blocks = out_blocks
+    stores = [
+        pltpu.make_async_copy(done.at[jnp.bitwise_xor(mine, mask)], outs[mask], out_sem.at[mask])
+        for mask in range(freq_count)
+    ]
+    for store in stores:
+        store.start()
+    for store in stores:
+        store.wait()
+
+
+def cross_tree(position, table, rim, parts, rows, chunk, chunks):
+    freq_count = len(parts)
+    share, span = parts[0].shape
+    hbm = pl.BlockSpec(memory_space=pl.ANY)
+    return pl.pallas_call(
+        functools.partial(cross_tree_kernel, rows, chunk, chunks),
+        out_shape=[jax.ShapeDtypeStruct((share, span), jnp.float32)] * freq_count,
+        in_specs=[pl.BlockSpec(memory_space=pltpu.SMEM), pl.BlockSpec(memory_space=pltpu.VMEM), hbm]
+        + [hbm] * freq_count,
+        out_specs=[hbm] * freq_count,
+        scratch_shapes=[
+            pltpu.VMEM((freq_count, share, span + rim.shape[2]), jnp.float32),
+            pltpu.VMEM((freq_count, share, span), jnp.float32),
+            pltpu.SemaphoreType.DMA((2, freq_count)),
+            pltpu.SemaphoreType.DMA((freq_count,)),
+        ],
+        compiler_params=pltpu.CompilerParams(vmem_limit_bytes=VMEM_LIMIT),
+        cost_estimate=pl.CostEstimate(
+            flops=4 * freq_count * share * span,
+            bytes_accessed=8 * freq_count * share * span,
+            transcendentals=0,
+        ),
+        name="cross_tree",
+    )(position, table, rim, *parts)
+
+
+def filter_kernel(freq_count, chunk, with_base, place, scale, band, rim, *refs):
+    parts, refs = refs[:freq_count], refs[freq_count:]
+    if with_base:
+        refs = refs[1:]
+    out, values, wide, taps, results, in_sem, out_sem = refs
+    share, span = parts[0].shape
+    group = freq_count * share
+    blocks = span // LANES
+    mine = place[0]
+    loads = [pltpu.make_async_copy(band, taps, in_sem.at[2, 0])]
+    for mask in range(freq_count):
+        owner = jnp.bitwise_xor(mine, mask)
+        spot = pl.ds(pl.multiple_of(owner * share, share), share)
+        loads.append(
+            pltpu.make_async_copy(parts[mask], values.at[spot, pl.ds(0, span)], in_sem.at[0, mask])
+        )
+        loads.append(
+            pltpu.make_async_copy(
+                rim.at[mask], values.at[spot, pl.ds(span, LANES)], in_sem.at[1, mask]
+            )
+        )
+    for load in loads:
+        load.start()
+    for load in loads:
+        load.wait()
+    for j in range(blocks + 1):
+        exact = values[:, block_of(j)]
+        high = exact.astype(jnp.bfloat16)
+        low = (exact - high.astype(jnp.float32)).astype(jnp.bfloat16)
+        for half, value in ((0, high), (1, low)):
+            if j < blocks:
+                wide[j, :, pl.ds(2 * half * LANES, LANES)] = value
+            if j > 0:
+                wide[j - 1, :, pl.ds((2 * half + 1) * LANES, LANES)] = value
+    filters = out.shape[0]
+    per_dot = 2
+    copies = {}
+    for pair in range(filters // per_dot):
+        slot = pair % 2
+        if pair >= 2:
+            for copy in copies[pair - 2]:
+                copy.wait()
+        weights = taps[:, pl.ds(pair * per_dot * TAPS, per_dot * TAPS)]
+        scales = [scale[pair * per_dot + e] for e in range(per_dot)]
+
+        def step(j, carry, slot=slot, weights=weights, scales=scales):
+            product = jnp.dot(wide[j], weights, preferred_element_type=jnp.float32)
+            for e in range(per_dot):
+                results[slot, e, :, pl.ds(pl.multiple_of(j * LANES, LANES), LANES)] = (
+                    product[:, block_of(e)] * scales[e]
+                )
+            return carry
+
+        lax.fori_loop(0, blocks, step, 0, unroll=4)
+        copies[pair] = [
+            pltpu.make_async_copy(
+                results.at[slot, e],
+                out.at[pair * per_dot + e, pl.ds(chunk * group, group), :],
+                out_sem.at[slot, e],
+            )
+            for e in range(per_dot)
+        ]
+        for copy in copies[pair]:
+            copy.start()
+    for pair in range(max(0, filters // per_dot - 2), filters // per_dot):
+        for copy in copies[pair]:
+            copy.wait()
+
+
+def box_filters(position, scale, band, rim, parts, base, rows, chunk):
+    freq_count = len(parts)
+    share, span = parts[0].shape
+    group = freq_count * share
+    filters = scale.shape[0]
+    hbm = pl.BlockSpec(memory_space=pl.ANY)
+    smem = pl.BlockSpec(memory_space=pltpu.SMEM)
+    operands = [position, scale, band, rim, *parts]
+    aliases = {}
+    if base is not None:
+        aliases = {len(operands): 0}
+        operands.append(base)
+    return pl.pallas_call(
+        functools.partial(filter_kernel, freq_count, chunk, base is not None),
+        out_shape=jax.ShapeDtypeStruct((filters, rows, span), jnp.float32),
+        in_specs=[smem, smem] + [hbm] * (len(operands) - 2),
+        out_specs=hbm,
+        input_output_aliases=aliases,
+        scratch_shapes=[
+            pltpu.VMEM((group, span + LANES), jnp.float32),
+            pltpu.VMEM((span // LANES, group, 4 * LANES), jnp.bfloat16),
+            pltpu.VMEM(band.shape, jnp.bfloat16),
+            pltpu.VMEM((2, 2, group, span), jnp.float32),
+            pltpu.SemaphoreType.DMA((3, freq_count)),
+            pltpu.SemaphoreType.DMA((2, 2)),
+        ],
+        compiler_params=pltpu.CompilerParams(vmem_limit_bytes=VMEM_LIMIT),
+        cost_estimate=pl.CostEstimate(
+            flops=8 * group * span * LANES * filters,
+            bytes_accessed=4 * group * span * (filters + 1),
+            transcendentals=0,
+        ),
+        name="box_filters",
+    )(*operands)
+
+
+def band_matrix(widths):
+    count = widths.shape[0]
+    source = lax.broadcasted_iota(jnp.int32, (4 * TAPS, count * TAPS), 0) % (2 * TAPS)
+    start = lax.broadcasted_iota(jnp.int32, (4 * TAPS, count * TAPS), 1) % TAPS
+    distance = source - start
+    reach = jnp.repeat(widths, TAPS)[None, :]
+    return ((distance >= 0) & (distance < reach)).astype(jnp.bfloat16)
 
 
 def passed_along(value, axis, steps):
     count = lax.axis_size(axis)
     initial, last = (max(0, -steps), min(count, count - steps))
     return lax.ppermute(value, axis, [(source, source + steps) for source in range(initial, last)])
+
+
+def swapped(parts, freq_count):
+    order = sorted(range(1, freq_count), key=lambda mask: (-(mask.bit_length()), mask))
+    result = [parts[0]] + [None] * (freq_count - 1)
+    for mask in order:
+        pairs = [(source, source ^ mask) for source in range(freq_count)]
+        result[mask] = lax.ppermute(parts[mask], "freq", pairs)
+    return result
+
+
+def by_residues(spectra, delays, widths):
+    rows, span = spectra.shape
+    freq_count = lax.axis_size("freq")
+    channels = rows * freq_count
+    position = lax.axis_index("freq").astype(jnp.int32)[None]
+    local_rim = -(-(rows - 1) // LANES) * LANES
+    rim = passed_along(spectra[:, :local_rim], "tm", -1)
+    table = jnp.pad(delays.T, ((0, 0), (0, LANES - delays.shape[0])))
+    band = band_matrix(widths)
+    scale = 1.0 / jnp.sqrt(widths.astype(jnp.float32) * channels)
+    parts = local_tree(position, spectra, rim, table, freq_count, CHUNKS)
+    arrived = [
+        swapped(parts[chunk * freq_count : (chunk + 1) * freq_count], freq_count)
+        for chunk in range(CHUNKS)
+    ]
+    returned = []
+    for chunk in range(CHUNKS):
+        leading = jnp.stack([part[:, : channels - rows] for part in arrived[chunk]])
+        leading = passed_along(leading, "tm", -1)
+        summed = cross_tree(position, table, leading, arrived[chunk], rows, chunk, CHUNKS)
+        returned.append(swapped(summed, freq_count))
+    result = None
+    for chunk in range(CHUNKS):
+        leading = jnp.stack([part[:, :LANES] for part in returned[chunk]])
+        leading = passed_along(leading, "tm", -1)
+        result = box_filters(position, scale, band, leading, returned[chunk], result, rows, chunk)
+    return result
 
 
 def from_partner(value, axis, stride):
@@ -50,7 +482,7 @@
     return summed.reshape(row_count, out_width)
 
 
-def local(spectra, delays, widths):
+def by_levels(spectra, delays, widths):
     row_count, time_span = spectra.shape
     local_levels = row_count.bit_length() - 1
     freq_count = lax.axis_size("freq")
@@ -88,7 +520,7 @@
     output_pos = lax.broadcasted_iota(jnp.int32, (2 * TAPS, filter_count, TAPS), 2)
     distance = input_pos - output_pos
     box_widths = widths[None, :, None]
-    scaling = 1.0 / jnp.sqrt(widths.astype(jnp.float32) * F)
+    scaling = 1.0 / jnp.sqrt(widths.astype(jnp.float32) * (row_count * freq_count))
     filter_matrix = jnp.where(
         (distance >= 0) & (distance < box_widths), scaling[None, :, None], 0.0
     )
@@ -96,6 +528,26 @@
     product = jnp.einsum("rbj,jk->rbk", paired, filter_matrix, precision=lax.Precision.HIGHEST)
     product = product.reshape(row_count, block_count, filter_count, TAPS)
     return jnp.transpose(product, (2, 0, 1, 3)).reshape(filter_count, row_count, time_span)
+
+
+def fits(rows, span, freq_count, levels):
+    channels = rows * freq_count
+    return (
+        rows % 64 == 0
+        and LANES <= rows <= 2 * LANES
+        and rows & (rows - 1) == 0
+        and freq_count & (freq_count - 1) == 0
+        and channels == 2**levels
+        and rows % (CHUNKS * freq_count * 2 * SUBLANES) == 0
+        and span % LANES == 0
+        and channels - rows <= span
+    )
+
+
+def local(spectra, delays, widths):
+    if fits(*spectra.shape, lax.axis_size("freq"), delays.shape[0]):
+        return by_residues(spectra, delays, widths)
+    return by_levels(spectra, delays, widths)
 
 
 def solution(mesh):

time: 535 us -> 220 us (0.41)
  the two profiles are of different devices: /device:TPU:0 before, /device:TPU:10 now
where the time goes in v1:
time: 220 us; the launch traced here: 218 us
  Pallas kernels  77.5 us (35%)
  waiting for transfers between devices  77.3 us (35%)
  starting transfers between devices  59.8 us (27%)
  local copies, waits for them, and re-layouts  2.56 us (1%)
    ppermute x28, waiting for transfers between devices, swapped(): result[mask] = lax.ppermute(parts[mask], 'freq', pairs)  76.6 us
    ppermute x28, starting transfers between devices, swapped(): result[mask] = lax.ppermute(parts[mask], 'freq', pairs)  53.4 us
    pallas_call x1, Pallas kernels, local_tree(): pl.pallas_call(functools.partial(local_tree_kernel, freq_count, chunks),...  36.9 us
    pallas_call x2, Pallas kernels, box_filters(): pl.pallas_call(functools.partial(filter_kernel, freq_count, chunk, base i...  20.5 us
    pallas_call x2, Pallas kernels, cross_tree(): pl.pallas_call(functools.partial(cross_tree_kernel, rows, chunk, chunks),...  20.1 us
    ppermute x5, starting transfers between devices, passed_along(): lax.ppermute(value, axis, [(source, source + steps) for source in range(i...  6.44 us
  transfers between devices with their start and end apart: 33, of which 15 were waited for; matrix products, arithmetic and copies ran while one was open for 1% of the time, Pallas kernels for 14%

profile of v1, /device:TPU:10, one launch (start us, length us, event | category | flops | bytes accessed | tf_op | source)
XLA Modules:
  0.0 218.1 jit_solution(11278242867580752969)
XLA Ops:
  4.4 36.9 %local_tree.1 = (f32[16,2560]{1,0:T(8,128)S(1)}, f32[16,2560]{1,0:T(8,128)S(1)}, f32[16,2560]{1,0:T(8,128)S(1)}, f32[16,2560]{1,0:T(8,128)S(1)}, f32[16,2560]{1,...) custom-call(s32[1]{0:T(128)} %bitcast.place, ...), custom_call_target="tpu_custom_call" | custom-call | flops 5242880 | bytes 5242880 | tf_op jit(solution)/shard_map/local_tree/pallas_call | solution.py:160
  44.9 2.6 %collective-permute-start.4 = (f32[16,2560]{1,0:T(8,128)S(1)}, f32[16,2560]{1,0:T(8,128)S(1)}, u32[]{:S(2)}, u32[]{:S(2)}) collective-permute-start(f32[16,2560]{1,0:T(8,128)S(1)} %get-tuple-element.41), channel_id=1, source_target_pairs={{0,8},{2,10},{4,12},{6,14},{8,0},{10,2},{12,4},{14,6},{1,9},{3,11}... | collective-permute-start | bytes 491528 | tf_op jit(solution)/shard_map/ppermute | solution.py:415
  48.8 1.6 collective-permute-start.6
  50.5 3.5 %collective-permute-done.2.refs_2_ = f32[16,2560]{1,0:T(8,128)S(1)} collective-permute-done((f32[16,2560]{1,0:T(8,128)S(1)}, f32[16,2560]{1,0:T(8,128)S(1)}, u32[]{:S(2)}, u32[]{:S(2)}) %collective-permute-start.2) | collective-permute-done | bytes 163872 | tf_op jit(solution)/shard_map/ppermute | solution.py:415
  54.0 8.3 %collective-permute-done.17.refs_1_ = f32[16,2560]{1,0:T(8,128)S(1)} collective-permute-done((f32[16,2560]{1,0:T(8,128)S(1)}, f32[16,2560]{1,0:T(8,128)S(1)}, u32[]{:S(2)}, u32[]{:S(2)}) %collective-permute-start.17) | collective-permute-done | bytes 163872 | tf_op jit(solution)/shard_map/ppermute | solution.py:415
  62.4 5.3 %collective-permute-done.18.refs_2_ = f32[16,2560]{1,0:T(8,128)S(1)} collective-permute-done((f32[16,2560]{1,0:T(8,128)S(1)}, f32[16,2560]{1,0:T(8,128)S(1)}, u32[]{:S(2)}, u32[]{:S(2)}) %collective-permute-start.18) | collective-permute-done | bytes 163872 | tf_op jit(solution)/shard_map/ppermute | solution.py:415
  67.7 3.0 %collective-permute-start.19 = (f32[16,2560]{1,0:T(8,128)S(1)}, f32[16,2560]{1,0:T(8,128)S(1)}, u32[]{:S(2)}, u32[]{:S(2)}) collective-permute-start(f32[16,2560]{1,0:T(8,128)S(1)} %get-tuple-element.56), channel_id=1, source_target_pairs={{0,6},{2,4},{4,2},{6,0},{8,14},{10,12},{12,10},{14,8},{1,7},{3,5},... | collective-permute-start | bytes 491528 | tf_op jit(solution)/shard_map/ppermute | solution.py:415
  70.7 3.9 %collective-permute-done.19.refs_3_ = f32[16,2560]{1,0:T(8,128)S(1)} collective-permute-done((f32[16,2560]{1,0:T(8,128)S(1)}, f32[16,2560]{1,0:T(8,128)S(1)}, u32[]{:S(2)}, u32[]{:S(2)}) %collective-permute-start.19) | collective-permute-done | bytes 163872 | tf_op jit(solution)/shard_map/ppermute | solution.py:415
  74.6 4.1 %collective-permute-start.20 = (f32[16,2560]{1,0:T(8,128)S(1)}, f32[16,2560]{1,0:T(8,128)S(1)}, u32[]{:S(2)}, u32[]{:S(2)}) collective-permute-start(f32[16,2560]{1,0:T(8,128)S(1)} %get-tuple-element.57), channel_id=1, source_target_pairs={{0,8},{2,10},{4,12},{6,14},{8,0},{10,2},{12,4},{14,6},{1,9},{3,11}... | collective-permute-start | bytes 491528 | tf_op jit(solution)/shard_map/ppermute | solution.py:415
  78.7 6.3 %collective-permute-done.20.refs_4_ = f32[16,2560]{1,0:T(8,128)S(1)} collective-permute-done((f32[16,2560]{1,0:T(8,128)S(1)}, f32[16,2560]{1,0:T(8,128)S(1)}, u32[]{:S(2)}, u32[]{:S(2)}) %collective-permute-start.20) | collective-permute-done | bytes 163872 | tf_op jit(solution)/shard_map/ppermute | solution.py:415
  85.0 3.3 %collective-permute-start.21 = (f32[16,2560]{1,0:T(8,128)S(1)}, f32[16,2560]{1,0:T(8,128)S(1)}, u32[]{:S(2)}, u32[]{:S(2)}) collective-permute-start(f32[16,2560]{1,0:T(8,128)S(1)} %get-tuple-element.58), channel_id=1, source_target_pairs={{0,10},{2,8},{4,14},{6,12},{8,2},{10,0},{12,6},{14,4},{1,11},{3,9}... | collective-permute-start | bytes 491528 | tf_op jit(solution)/shard_map/ppermute | solution.py:415
  88.3 4.6 %collective-permute-done.21.refs_5_ = f32[16,2560]{1,0:T(8,128)S(1)} collective-permute-done((f32[16,2560]{1,0:T(8,128)S(1)}, f32[16,2560]{1,0:T(8,128)S(1)}, u32[]{:S(2)}, u32[]{:S(2)}) %collective-permute-start.21) | collective-permute-done | bytes 163872 | tf_op jit(solution)/shard_map/ppermute | solution.py:415
  94.0 5.1 %collective-permute-done.22.refs_6_ = f32[16,2560]{1,0:T(8,128)S(1)} collective-permute-done((f32[16,2560]{1,0:T(8,128)S(1)}, f32[16,2560]{1,0:T(8,128)S(1)}, u32[]{:S(2)}, u32[]{:S(2)}) %collective-permute-start.22) | collective-permute-done | bytes 163872 | tf_op jit(solution)/shard_map/ppermute | solution.py:415
  99.0 6.2 %collective-permute-start.23 = (f32[16,2560]{1,0:T(8,128)S(1)}, f32[16,2560]{1,0:T(8,128)S(1)}, u32[]{:S(2)}, u32[]{:S(2)}) collective-permute-start(f32[16,2560]{1,0:T(8,128)S(1)} %get-tuple-element.60), channel_id=1, source_target_pairs={{0,14},{2,12},{4,10},{6,8},{8,6},{10,4},{12,2},{14,0},{1,15},{3,13... | collective-permute-start | bytes 491528 | tf_op jit(solution)/shard_map/ppermute | solution.py:415
  105.2 7.6 %collective-permute-done.23.refs_7_ = f32[16,2560]{1,0:T(8,128)S(1)} collective-permute-done((f32[16,2560]{1,0:T(8,128)S(1)}, f32[16,2560]{1,0:T(8,128)S(1)}, u32[]{:S(2)}, u32[]{:S(2)}) %collective-permute-start.23) | collective-permute-done | bytes 163872 | tf_op jit(solution)/shard_map/ppermute | solution.py:415
  112.8 3.0 %collective-permute-start.7 = (f32[16,2560]{1,0:T(8,128)S(1)}, f32[16,2560]{1,0:T(8,128)S(1)}, u32[]{:S(2)}, u32[]{:S(2)}) collective-permute-start(f32[16,2560]{1,0:T(8,128)S(1)} %get-tuple-element.44), channel_id=1, source_target_pairs={{0,14},{2,12},{4,10},{6,8},{8,6},{10,4},{12,2},{14,0},{1,15},{3,13... | collective-permute-start | bytes 491528 | tf_op jit(solution)/shard_map/ppermute | solution.py:415
  117.2 3.6 %collective-permute-done.7.refs_7_ = f32[16,2560]{1,0:T(8,128)S(1)} collective-permute-done((f32[16,2560]{1,0:T(8,128)S(1)}, f32[16,2560]{1,0:T(8,128)S(1)}, u32[]{:S(2)}, u32[]{:S(2)}) %collective-permute-start.7) | collective-permute-done | bytes 163872 | tf_op jit(solution)/shard_map/ppermute | solution.py:415
  122.7 10.1 %cross_tree.3 = (f32[16,2560]{1,0:T(8,128)S(1)}, f32[16,2560]{1,0:T(8,128)S(1)}, f32[16,2560]{1,0:T(8,128)S(1)}, f32[16,2560]{1,0:T(8,128)S(1)}, f32[16,2560]{1,...) custom-call(s32[1]{0:T(128)} %bitcast.place, s32[2048,128]{1,0:T(8,128)S(1)} %pad.4.table, ...), custom_call_target="tpu_custom_call" | custom-call | flops 1310720 | bytes 2621440 | tf_op jit(solution)/shard_map/cross_tree/pallas_call | solution.py:268
  133.4 2.9 %collective-permute-start.27 = (f32[16,2560]{1,0:T(8,128)S(1)}, f32[16,2560]{1,0:T(8,128)S(1)}, u32[]{:S(2)}, u32[]{:S(2)}) collective-permute-start(f32[16,2560]{1,0:T(8,128)S(1)} %get-tuple-element.64), channel_id=1, source_target_pairs={{0,6},{2,4},{4,2},{6,0},{8,14},{10,12},{12,10},{14,8},{1,7},{3,5},... | collective-permute-start | bytes 491528 | tf_op jit(solution)/shard_map/ppermute | solution.py:415
  136.4 2.4 %collective-permute-start.29 = (f32[16,2560]{1,0:T(8,128)S(1)}, f32[16,2560]{1,0:T(8,128)S(1)}, u32[]{:S(2)}, u32[]{:S(2)}) collective-permute-start(f32[16,2560]{1,0:T(8,128)S(1)} %get-tuple-element.66), channel_id=1, source_target_pairs={{0,10},{2,8},{4,14},{6,12},{8,2},{10,0},{12,6},{14,4},{1,11},{3,9}... | collective-permute-start | bytes 491528 | tf_op jit(solution)/shard_map/ppermute | solution.py:415
  138.8 10.0 %cross_tree.2 = (f32[16,2560]{1,0:T(8,128)S(1)}, f32[16,2560]{1,0:T(8,128)S(1)}, f32[16,2560]{1,0:T(8,128)S(1)}, f32[16,2560]{1,0:T(8,128)S(1)}, f32[16,2560]{1,...) custom-call(s32[1]{0:T(128)} %bitcast.place, s32[2048,128]{1,0:T(8,128)S(1)} %pad.4.table, ...), custom_call_target="tpu_custom_call" | custom-call | flops 1310720 | bytes 2621440 | tf_op jit(solution)/shard_map/cross_tree/pallas_call | solution.py:268
  148.8 1.9 collective-permute-start.30
  150.7 1.6 collective-permute-start.31
  152.4 2.3 %collective-permute-start.10 = (f32[16,2560]{1,0:T(8,128)S(1)}, f32[16,2560]{1,0:T(8,128)S(1)}, u32[]{:S(2)}, u32[]{:S(2)}) collective-permute-start(f32[16,2560]{1,0:T(8,128)S(1)} %get-tuple-element.47), channel_id=1, source_target_pairs={{0,4},{2,6},{4,0},{6,2},{8,12},{10,14},{12,8},{14,10},{1,5},{3,7},... | collective-permute-start | bytes 491528 | tf_op jit(solution)/shard_map/ppermute | solution.py:415
  154.7 8.6 %collective-permute-start.11 = (f32[16,2560]{1,0:T(8,128)S(1)}, f32[16,2560]{1,0:T(8,128)S(1)}, u32[]{:S(2)}, u32[]{:S(2)}) collective-permute-start(f32[16,2560]{1,0:T(8,128)S(1)} %get-tuple-element.48), channel_id=1, source_target_pairs={{0,6},{2,4},{4,2},{6,0},{8,14},{10,12},{12,10},{14,8},{1,7},{3,5},... | collective-permute-start | bytes 491528 | tf_op jit(solution)/shard_map/ppermute | solution.py:415
  164.5 7.8 %collective-permute-done.31.refs_7_ = f32[16,2560]{1,0:T(8,128)S(1)} collective-permute-done((f32[16,2560]{1,0:T(8,128)S(1)}, f32[16,2560]{1,0:T(8,128)S(1)}, u32[]{:S(2)}, u32[]{:S(2)}) %collective-permute-start.31) | collective-permute-done | bytes 163872 | tf_op jit(solution)/shard_map/ppermute | solution.py:415
  173.4 2.1 collective-permute-start.15
  176.8 11.0 %collective-permute-done.13.refs_5_ = f32[16,2560]{1,0:T(8,128)S(1)} collective-permute-done((f32[16,2560]{1,0:T(8,128)S(1)}, f32[16,2560]{1,0:T(8,128)S(1)}, u32[]{:S(2)}, u32[]{:S(2)}) %collective-permute-start.13) | collective-permute-done | bytes 163872 | tf_op jit(solution)/shard_map/ppermute | solution.py:415
  187.9 5.7 %collective-permute-done.14.refs_6_ = f32[16,2560]{1,0:T(8,128)S(1)} collective-permute-done((f32[16,2560]{1,0:T(8,128)S(1)}, f32[16,2560]{1,0:T(8,128)S(1)}, u32[]{:S(2)}, u32[]{:S(2)}) %collective-permute-start.14) | collective-permute-done | bytes 163872 | tf_op jit(solution)/shard_map/ppermute | solution.py:415
  193.6 2.7 %collective-permute-done.15.refs_7_ = f32[16,2560]{1,0:T(8,128)S(1)} collective-permute-done((f32[16,2560]{1,0:T(8,128)S(1)}, f32[16,2560]{1,0:T(8,128)S(1)}, u32[]{:S(2)}, u32[]{:S(2)}) %collective-permute-start.15) | collective-permute-done | bytes 163872 | tf_op jit(solution)/shard_map/ppermute | solution.py:415
  197.6 10.2 %box_filters.2.refs_8_ = f32[8,256,2560]{2,1,0:T(8,128)} custom-call(s32[1]{0:T(128)} %bitcast.place, f32[8]{0:T(128)S(1)} %multiply_rsqrt_fusion.scale, bf16[512,1024]{1,0:T(8,128)(2,1)S(1)} %fusion.3.band, f32[8,16,128]{2,1,0:T(8,128)S(1)} %collective-permute-done.32.rim, f32[16,2560]{1,0:T(8,128)S(1)} %get-tuple-element.61.refs_0_, ...), custom_call_target="tpu_custom_call" | custom-call | flops 2684354560 | bytes 11796480 | tf_op jit(solution)/shard_map/box_filters/pallas_call | solution.py:371
  207.8 10.2 %box_filters.3 = f32[8,256,2560]{2,1,0:T(8,128)} custom-call(s32[1]{0:T(128)} %bitcast.place, f32[8]{0:T(128)S(1)} %multiply_rsqrt_fusion.scale, bf16[512,1024]{1,0:T(8,128)(2,1)S(1)} %fusion.3.band, f32[8,16,128]{2,1,0:T(8,128)S(1)} %collective-permute-done.16.rim, f32[16,2560]{1,0:T(8,128)S(1)} %get-tuple-element.45.refs_0_, ...), custom_call_target="tpu_custom_call", output_to_operand_aliasing={{}: (12, {})} | custom-call | flops 2684354560 | bytes 11796480 | tf_op jit(solution)/shard_map/box_filters/pallas_call | solution.py:371
  (83 shorter events, 19.2 us)
Async XLA Ops:
  41.3 7.5 %collective-permute-start.1 = (f32[16,2560]{1,0:T(8,128)S(1)}, f32[16,2560]{1,0:T(8,128)S(1)}, u32[]{:S(2)}, u32[]{:S(2)}) collective-permute-start(f32[16,2560]{1,0:T(8,128)S(1)} %get-tuple-element.38), channel_id=1, source_target_pairs={{0,2},{2,0},{4,6},{6,4},{8,10},{10,8},{12,14},{14,12},{1,3},{3,1},... | collective-permute-start | bytes 491528 | tf_op jit(solution)/shard_map/ppermute | solution.py:415
  42.9 11.1 %collective-permute-start.2 = (f32[16,2560]{1,0:T(8,128)S(1)}, f32[16,2560]{1,0:T(8,128)S(1)}, u32[]{:S(2)}, u32[]{:S(2)}) collective-permute-start(f32[16,2560]{1,0:T(8,128)S(1)} %get-tuple-element.39), channel_id=1, source_target_pairs={{0,4},{2,6},{4,0},{6,2},{8,12},{10,14},{12,8},{14,10},{1,5},{3,7},... | collective-permute-start | bytes 491528 | tf_op jit(solution)/shard_map/ppermute | solution.py:415
  43.4 72.4 %collective-permute-start.3 = (f32[16,2560]{1,0:T(8,128)S(1)}, f32[16,2560]{1,0:T(8,128)S(1)}, u32[]{:S(2)}, u32[]{:S(2)}) collective-permute-start(f32[16,2560]{1,0:T(8,128)S(1)} %get-tuple-element.40), channel_id=1, source_target_pairs={{0,6},{2,4},{4,2},{6,0},{8,14},{10,12},{12,10},{14,8},{1,7},{3,5},... | collective-permute-start | bytes 491528 | tf_op jit(solution)/shard_map/ppermute | solution.py:415
  44.9 72.2 %collective-permute-start.4 = (f32[16,2560]{1,0:T(8,128)S(1)}, f32[16,2560]{1,0:T(8,128)S(1)}, u32[]{:S(2)}, u32[]{:S(2)}) collective-permute-start(f32[16,2560]{1,0:T(8,128)S(1)} %get-tuple-element.41), channel_id=1, source_target_pairs={{0,8},{2,10},{4,12},{6,14},{8,0},{10,2},{12,4},{14,6},{1,9},{3,11}... | collective-permute-start | bytes 491528 | tf_op jit(solution)/shard_map/ppermute | solution.py:415
  47.5 69.7 %collective-permute-start.5 = (f32[16,2560]{1,0:T(8,128)S(1)}, f32[16,2560]{1,0:T(8,128)S(1)}, u32[]{:S(2)}, u32[]{:S(2)}) collective-permute-start(f32[16,2560]{1,0:T(8,128)S(1)} %get-tuple-element.42), channel_id=1, source_target_pairs={{0,10},{2,8},{4,14},{6,12},{8,2},{10,0},{12,6},{14,4},{1,11},{3,9}... | collective-permute-start | bytes 491528 | tf_op jit(solution)/shard_map/ppermute | solution.py:415
  48.8 68.4 %collective-permute-start.6 = (f32[16,2560]{1,0:T(8,128)S(1)}, f32[16,2560]{1,0:T(8,128)S(1)}, u32[]{:S(2)}, u32[]{:S(2)}) collective-permute-start(f32[16,2560]{1,0:T(8,128)S(1)} %get-tuple-element.43), channel_id=1, source_target_pairs={{0,12},{2,14},{4,8},{6,10},{8,4},{10,6},{12,0},{14,2},{1,13},{3,15... | collective-permute-start | bytes 491528 | tf_op jit(solution)/shard_map/ppermute | solution.py:415
  54.0 8.3 %collective-permute-start.17 = (f32[16,2560]{1,0:T(8,128)S(1)}, f32[16,2560]{1,0:T(8,128)S(1)}, u32[]{:S(2)}, u32[]{:S(2)}) collective-permute-start(f32[16,2560]{1,0:T(8,128)S(1)} %get-tuple-element.54), channel_id=1, source_target_pairs={{0,2},{2,0},{4,6},{6,4},{8,10},{10,8},{12,14},{14,12},{1,3},{3,1},... | collective-permute-start | bytes 491528 | tf_op jit(solution)/shard_map/ppermute | solution.py:415
  62.3 5.4 %collective-permute-start.18 = (f32[16,2560]{1,0:T(8,128)S(1)}, f32[16,2560]{1,0:T(8,128)S(1)}, u32[]{:S(2)}, u32[]{:S(2)}) collective-permute-start(f32[16,2560]{1,0:T(8,128)S(1)} %get-tuple-element.55), channel_id=1, source_target_pairs={{0,4},{2,6},{4,0},{6,2},{8,12},{10,14},{12,8},{14,10},{1,5},{3,7},... | collective-permute-start | bytes 491528 | tf_op jit(solution)/shard_map/ppermute | solution.py:415
  67.7 6.9 %collective-permute-start.19 = (f32[16,2560]{1,0:T(8,128)S(1)}, f32[16,2560]{1,0:T(8,128)S(1)}, u32[]{:S(2)}, u32[]{:S(2)}) collective-permute-start(f32[16,2560]{1,0:T(8,128)S(1)} %get-tuple-element.56), channel_id=1, source_target_pairs={{0,6},{2,4},{4,2},{6,0},{8,14},{10,12},{12,10},{14,8},{1,7},{3,5},... | collective-permute-start | bytes 491528 | tf_op jit(solution)/shard_map/ppermute | solution.py:415
  74.6 10.4 %collective-permute-start.20 = (f32[16,2560]{1,0:T(8,128)S(1)}, f32[16,2560]{1,0:T(8,128)S(1)}, u32[]{:S(2)}, u32[]{:S(2)}) collective-permute-start(f32[16,2560]{1,0:T(8,128)S(1)} %get-tuple-element.57), channel_id=1, source_target_pairs={{0,8},{2,10},{4,12},{6,14},{8,0},{10,2},{12,4},{14,6},{1,9},{3,11}... | collective-permute-start | bytes 491528 | tf_op jit(solution)/shard_map/ppermute | solution.py:415
  85.0 7.9 %collective-permute-start.21 = (f32[16,2560]{1,0:T(8,128)S(1)}, f32[16,2560]{1,0:T(8,128)S(1)}, u32[]{:S(2)}, u32[]{:S(2)}) collective-permute-start(f32[16,2560]{1,0:T(8,128)S(1)} %get-tuple-element.58), channel_id=1, source_target_pairs={{0,10},{2,8},{4,14},{6,12},{8,2},{10,0},{12,6},{14,4},{1,11},{3,9}... | collective-permute-start | bytes 491528 | tf_op jit(solution)/shard_map/ppermute | solution.py:415
  92.9 6.1 %collective-permute-start.22 = (f32[16,2560]{1,0:T(8,128)S(1)}, f32[16,2560]{1,0:T(8,128)S(1)}, u32[]{:S(2)}, u32[]{:S(2)}) collective-permute-start(f32[16,2560]{1,0:T(8,128)S(1)} %get-tuple-element.59), channel_id=1, source_target_pairs={{0,12},{2,14},{4,8},{6,10},{8,4},{10,6},{12,0},{14,2},{1,13},{3,15... | collective-permute-start | bytes 491528 | tf_op jit(solution)/shard_map/ppermute | solution.py:415
  99.0 13.8 %collective-permute-start.23 = (f32[16,2560]{1,0:T(8,128)S(1)}, f32[16,2560]{1,0:T(8,128)S(1)}, u32[]{:S(2)}, u32[]{:S(2)}) collective-permute-start(f32[16,2560]{1,0:T(8,128)S(1)} %get-tuple-element.60), channel_id=1, source_target_pairs={{0,14},{2,12},{4,10},{6,8},{8,6},{10,4},{12,2},{14,0},{1,15},{3,13... | collective-permute-start | bytes 491528 | tf_op jit(solution)/shard_map/ppermute | solution.py:415
  112.8 8.0 %collective-permute-start.7 = (f32[16,2560]{1,0:T(8,128)S(1)}, f32[16,2560]{1,0:T(8,128)S(1)}, u32[]{:S(2)}, u32[]{:S(2)}) collective-permute-start(f32[16,2560]{1,0:T(8,128)S(1)} %get-tuple-element.44), channel_id=1, source_target_pairs={{0,14},{2,12},{4,10},{6,8},{8,6},{10,4},{12,2},{14,0},{1,15},{3,13... | collective-permute-start | bytes 491528 | tf_op jit(solution)/shard_map/ppermute | solution.py:415
  115.8 6.9 %collective-permute-start.24 = (f32[8,16,1792]{2,1,0:T(8,128)S(1)}, f32[8,16,1792]{2,1,0:T(8,128)S(1)}, u32[]{:S(2)}, u32[]{:S(2)}) collective-permute-start(f32[8,16,1792]{2,1,0:T(8,128)S(1)} %fusion.4), channel_id=1, source_target_pairs={{1,0},{3,2},{5,4},{7,6},{9,8},{11,10},{13,12},{15,14},{17,16},{19,... | collective-permute-start | bytes 2752520 | tf_op jit(solution)/shard_map/ppermute | solution.py:407
  120.8 15.5 %collective-permute-start.8 = (f32[8,16,1792]{2,1,0:T(8,128)S(1)}, f32[8,16,1792]{2,1,0:T(8,128)S(1)}, u32[]{:S(2)}, u32[]{:S(2)}) collective-permute-start(f32[8,16,1792]{2,1,0:T(8,128)S(1)} %fusion.11), channel_id=1, source_target_pairs={{1,0},{3,2},{5,4},{7,6},{9,8},{11,10},{13,12},{15,14},{17,16},{19,... | collective-permute-start | bytes 2752520 | tf_op jit(solution)/shard_map/ppermute | solution.py:407
  132.8 16.0 %collective-permute-start.25 = (f32[16,2560]{1,0:T(8,128)S(1)}, f32[16,2560]{1,0:T(8,128)S(1)}, u32[]{:S(2)}, u32[]{:S(2)}) collective-permute-start(f32[16,2560]{1,0:T(8,128)S(1)} %get-tuple-element.62), channel_id=1, source_target_pairs={{0,2},{2,0},{4,6},{6,4},{8,10},{10,8},{12,14},{14,12},{1,3},{3,1},... | collective-permute-start | bytes 491528 | tf_op jit(solution)/shard_map/ppermute | solution.py:415
  132.9 17.8 %collective-permute-start.26 = (f32[16,2560]{1,0:T(8,128)S(1)}, f32[16,2560]{1,0:T(8,128)S(1)}, u32[]{:S(2)}, u32[]{:S(2)}) collective-permute-start(f32[16,2560]{1,0:T(8,128)S(1)} %get-tuple-element.63), channel_id=1, source_target_pairs={{0,4},{2,6},{4,0},{6,2},{8,12},{10,14},{12,8},{14,10},{1,5},{3,7},... | collective-permute-start | bytes 491528 | tf_op jit(solution)/shard_map/ppermute | solution.py:415
  133.4 18.9 %collective-permute-start.27 = (f32[16,2560]{1,0:T(8,128)S(1)}, f32[16,2560]{1,0:T(8,128)S(1)}, u32[]{:S(2)}, u32[]{:S(2)}) collective-permute-start(f32[16,2560]{1,0:T(8,128)S(1)} %get-tuple-element.64), channel_id=1, source_target_pairs={{0,6},{2,4},{4,2},{6,0},{8,14},{10,12},{12,10},{14,8},{1,7},{3,5},... | collective-permute-start | bytes 491528 | tf_op jit(solution)/shard_map/ppermute | solution.py:415
  136.3 16.1 %collective-permute-start.28 = (f32[16,2560]{1,0:T(8,128)S(1)}, f32[16,2560]{1,0:T(8,128)S(1)}, u32[]{:S(2)}, u32[]{:S(2)}) collective-permute-start(f32[16,2560]{1,0:T(8,128)S(1)} %get-tuple-element.65), channel_id=1, source_target_pairs={{0,8},{2,10},{4,12},{6,14},{8,0},{10,2},{12,4},{14,6},{1,9},{3,11}... | collective-permute-start | bytes 491528 | tf_op jit(solution)/shard_map/ppermute | solution.py:415
  136.4 18.4 %collective-permute-start.29 = (f32[16,2560]{1,0:T(8,128)S(1)}, f32[16,2560]{1,0:T(8,128)S(1)}, u32[]{:S(2)}, u32[]{:S(2)}) collective-permute-start(f32[16,2560]{1,0:T(8,128)S(1)} %get-tuple-element.66), channel_id=1, source_target_pairs={{0,10},{2,8},{4,14},{6,12},{8,2},{10,0},{12,6},{14,4},{1,11},{3,9}... | collective-permute-start | bytes 491528 | tf_op jit(solution)/shard_map/ppermute | solution.py:415
  148.8 15.6 %collective-permute-start.30 = (f32[16,2560]{1,0:T(8,128)S(1)}, f32[16,2560]{1,0:T(8,128)S(1)}, u32[]{:S(2)}, u32[]{:S(2)}) collective-permute-start(f32[16,2560]{1,0:T(8,128)S(1)} %get-tuple-element.67), channel_id=1, source_target_pairs={{0,12},{2,14},{4,8},{6,10},{8,4},{10,6},{12,0},{14,2},{1,13},{3,15... | collective-permute-start | bytes 491528 | tf_op jit(solution)/shard_map/ppermute | solution.py:415
  150.7 21.6 %collective-permute-start.31 = (f32[16,2560]{1,0:T(8,128)S(1)}, f32[16,2560]{1,0:T(8,128)S(1)}, u32[]{:S(2)}, u32[]{:S(2)}) collective-permute-start(f32[16,2560]{1,0:T(8,128)S(1)} %get-tuple-element.68), channel_id=1, source_target_pairs={{0,14},{2,12},{4,10},{6,8},{8,6},{10,4},{12,2},{14,0},{1,15},{3,13... | collective-permute-start | bytes 491528 | tf_op jit(solution)/shard_map/ppermute | solution.py:415
  152.3 19.9 %collective-permute-start.9 = (f32[16,2560]{1,0:T(8,128)S(1)}, f32[16,2560]{1,0:T(8,128)S(1)}, u32[]{:S(2)}, u32[]{:S(2)}) collective-permute-start(f32[16,2560]{1,0:T(8,128)S(1)} %get-tuple-element.46), channel_id=1, source_target_pairs={{0,2},{2,0},{4,6},{6,4},{8,10},{10,8},{12,14},{14,12},{1,3},{3,1},... | collective-permute-start | bytes 491528 | tf_op jit(solution)/shard_map/ppermute | solution.py:415
  152.4 21.0 %collective-permute-start.10 = (f32[16,2560]{1,0:T(8,128)S(1)}, f32[16,2560]{1,0:T(8,128)S(1)}, u32[]{:S(2)}, u32[]{:S(2)}) collective-permute-start(f32[16,2560]{1,0:T(8,128)S(1)} %get-tuple-element.47), channel_id=1, source_target_pairs={{0,4},{2,6},{4,0},{6,2},{8,12},{10,14},{12,8},{14,10},{1,5},{3,7},... | collective-permute-start | bytes 491528 | tf_op jit(solution)/shard_map/ppermute | solution.py:415
  154.7 20.8 %collective-permute-start.11 = (f32[16,2560]{1,0:T(8,128)S(1)}, f32[16,2560]{1,0:T(8,128)S(1)}, u32[]{:S(2)}, u32[]{:S(2)}) collective-permute-start(f32[16,2560]{1,0:T(8,128)S(1)} %get-tuple-element.48), channel_id=1, source_target_pairs={{0,6},{2,4},{4,2},{6,0},{8,14},{10,12},{12,10},{14,8},{1,7},{3,5},... | collective-permute-start | bytes 491528 | tf_op jit(solution)/shard_map/ppermute | solution.py:415
  164.5 12.3 %collective-permute-start.12 = (f32[16,2560]{1,0:T(8,128)S(1)}, f32[16,2560]{1,0:T(8,128)S(1)}, u32[]{:S(2)}, u32[]{:S(2)}) collective-permute-start(f32[16,2560]{1,0:T(8,128)S(1)} %get-tuple-element.49), channel_id=1, source_target_pairs={{0,8},{2,10},{4,12},{6,14},{8,0},{10,2},{12,4},{14,6},{1,9},{3,11}... | collective-permute-start | bytes 491528 | tf_op jit(solution)/shard_map/ppermute | solution.py:415
  172.3 15.6 %collective-permute-start.13 = (f32[16,2560]{1,0:T(8,128)S(1)}, f32[16,2560]{1,0:T(8,128)S(1)}, u32[]{:S(2)}, u32[]{:S(2)}) collective-permute-start(f32[16,2560]{1,0:T(8,128)S(1)} %get-tuple-element.50), channel_id=1, source_target_pairs={{0,10},{2,8},{4,14},{6,12},{8,2},{10,0},{12,6},{14,4},{1,11},{3,9}... | collective-permute-start | bytes 491528 | tf_op jit(solution)/shard_map/ppermute | solution.py:415
  172.3 21.3 %collective-permute-start.14 = (f32[16,2560]{1,0:T(8,128)S(1)}, f32[16,2560]{1,0:T(8,128)S(1)}, u32[]{:S(2)}, u32[]{:S(2)}) collective-permute-start(f32[16,2560]{1,0:T(8,128)S(1)} %get-tuple-element.51), channel_id=1, source_target_pairs={{0,12},{2,14},{4,8},{6,10},{8,4},{10,6},{12,0},{14,2},{1,13},{3,15... | collective-permute-start | bytes 491528 | tf_op jit(solution)/shard_map/ppermute | solution.py:415
  173.4 22.9 %collective-permute-start.15 = (f32[16,2560]{1,0:T(8,128)S(1)}, f32[16,2560]{1,0:T(8,128)S(1)}, u32[]{:S(2)}, u32[]{:S(2)}) collective-permute-start(f32[16,2560]{1,0:T(8,128)S(1)} %get-tuple-element.52), channel_id=1, source_target_pairs={{0,14},{2,12},{4,10},{6,8},{8,6},{10,4},{12,2},{14,0},{1,15},{3,13... | collective-permute-start | bytes 491528 | tf_op jit(solution)/shard_map/ppermute | solution.py:415
  175.5 22.1 %collective-permute-start.32 = (f32[8,16,128]{2,1,0:T(8,128)S(1)}, f32[8,16,128]{2,1,0:T(8,128)S(1)}, u32[]{:S(2)}, u32[]{:S(2)}) collective-permute-start(f32[8,16,128]{2,1,0:T(8,128)S(1)} %constant_dynamic-update-slice_fusion.8), channel_id=1, source_target_pairs={{1,0},{3,2},{5,4},{7,6},{9,8},{11,10},{13,12},{15,14},{17,16},{19,... | collective-permute-start | bytes 196616 | tf_op jit(solution)/shard_map/ppermute | solution.py:407
  196.3 11.5 %collective-permute-start.16 = (f32[8,16,128]{2,1,0:T(8,128)S(1)}, f32[8,16,128]{2,1,0:T(8,128)S(1)}, u32[]{:S(2)}, u32[]{:S(2)}) collective-permute-start(f32[8,16,128]{2,1,0:T(8,128)S(1)} %constant_dynamic-update-slice_fusion), channel_id=1, source_target_pairs={{1,0},{3,2},{5,4},{7,6},{9,8},{11,10},{13,12},{15,14},{17,16},{19,... | collective-permute-start | bytes 196616 | tf_op jit(solution)/shard_map/ppermute | solution.py:407
  (2 other events, 84.2 us)

commit v2 on v0

--- a/solution.py
+++ b/solution.py
@@ -1,16 +1,483 @@
+import functools
+
 import jax
 import jax.numpy as jnp
 from jax import lax
+from jax.experimental import pallas as pl
+from jax.experimental.pallas import tpu as pltpu
 from jax.sharding import PartitionSpec as P
 
-F = 2048
+LANES = 128
+SUBLANES = 8
 TAPS = 128
+VMEM_LIMIT = 48 * 2**20
+
+
+def lane_gather(block, index):
+    return jnp.take_along_axis(block, index, axis=1, mode="promise_in_bounds")
+
+
+def add_delayed(load_a, load_b, store, shifts, level, in_blocks, out_blocks):
+    block_choices = max(1, 2**level // LANES)
+    bits = block_choices.bit_length() - 1
+    whole = jnp.minimum(shifts >> 7, block_choices - 1)
+    reach = lax.broadcasted_iota(jnp.int32, shifts.shape, 1) + shifts - (whole << 7)
+    index, stays = reach & (LANES - 1), reach < LANES
+    wanted = [(whole & 2**bit) != 0 for bit in range(bits)]
+    kept = {}
+
+    def source(stage, j):
+        if (stage, j) not in kept:
+            if stage == 0:
+                kept[stage, j] = load_b(j)
+            else:
+                later = source(stage - 1, j + 2 ** (stage - 1))
+                kept[stage, j] = jnp.where(wanted[stage - 1], later, source(stage - 1, j))
+        return kept[stage, j]
+
+    def turned(j):
+        if j + block_choices > in_blocks:
+            return jnp.zeros((SUBLANES, LANES), jnp.float32)
+        return lane_gather(source(bits, j), index)
+
+    held = turned(0)
+    for j in range(out_blocks):
+        following = turned(j + 1)
+        store(j, load_a(j) + jnp.where(stays, held, following))
+        held = following
+
+
+def block_of(j):
+    return slice(j * LANES, (j + 1) * LANES)
+
+
+def spread_shifts(table, spread, rows_at, count, levels):
+    per_step = max(n for n in (1, 2, 4) if count % n == 0)
+
+    def step(item, carry):
+        for e in range(per_step):
+            tile = item * per_step + e
+            values = table[pl.ds(pl.multiple_of(rows_at(tile), SUBLANES), SUBLANES), :]
+            for n, level in enumerate(levels):
+                spread[n, pl.ds(pl.multiple_of(tile * SUBLANES, SUBLANES), SUBLANES), :] = (
+                    jnp.broadcast_to(values[:, level : level + 1], (SUBLANES, LANES))
+                )
+        return carry
+
+    lax.fori_loop(0, count // per_step, step, 0)
+
+
+def local_tree_kernel(freq_count, place, spectra, rim, table, *refs):
+    rows, span = spectra.shape
+    levels = rows.bit_length() - 1
+    outs, (even, odd, done, spread, in_sem, out_sem) = refs[:freq_count], refs[freq_count:]
+    total, out_blocks = even.shape[0], span // LANES
+    mine = place[0]
+    loads = []
+    for j in range(total):
+        at = j - out_blocks
+        source = rim.at[:, block_of(at)] if at >= 0 else spectra.at[:, block_of(j)]
+        loads.append(pltpu.make_async_copy(source, even.at[j], in_sem.at[j]))
+    for load in loads:
+        load.start()
+    spread_shifts(
+        table, spread, lambda tile: mine * rows + tile * SUBLANES, rows // SUBLANES, range(levels)
+    )
+    for load in loads:
+        load.wait()
+    pairs = rows // (2 * SUBLANES)
+    per_step = max(n for n in (1, 2, 4) if pairs % n == 0)
+    for level in range(levels - 1):
+        half = 2**level
+        source, target = (even, odd) if level % 2 == 0 else (odd, even)
+
+        def step(item, carry, level=level, half=half, source=source, target=target):
+            for n in range(per_step):
+                pair = item * per_step + n
+                if half < SUBLANES:
+                    group, member = pair // 4, pair % 4
+                    start = group * 64 + (member // half) * 2 * half + member % half
+                    spots = [
+                        pl.ds(start + e * half, SUBLANES, stride=SUBLANES) for e in range(2)
+                    ]
+                else:
+                    tiles = half // SUBLANES
+                    tile = (pair // tiles) * 2 * tiles + pair % tiles
+                    spots = [
+                        pl.ds(pl.multiple_of((tile + e * tiles) * SUBLANES, SUBLANES), SUBLANES)
+                        for e in range(2)
+                    ]
+                for spot in spots:
+
+                    def put(j, value, spot=spot):
+                        target[j, spot, :] = value
+
+                    add_delayed(
+                        lambda j: source[j, spots[0], :],
+                        lambda j: source[j, spots[1], :],
+                        put,
+                        spread[level, spot, :],
+                        level,
+                        total,
+                        total,
+                    )
+            return carry
+
+        lax.fori_loop(0, pairs // per_step, step, 0)
+    level = levels - 1
+    source = even if level % 2 == 0 else odd
+    half = freq_count // 2
+    share = rows // freq_count
+    tiles = share // SUBLANES
+    stores = []
+    for mask in range(half):
+        lower = jnp.bitwise_and(jnp.bitwise_xor(mine, mask), half - 1)
+        starts = [lower * share, (lower + half) * share]
+        for tile in range(tiles):
+            spots = [
+                pl.ds(pl.multiple_of(start + tile * SUBLANES, SUBLANES), SUBLANES)
+                for start in starts
+            ]
+            for spot in spots:
+
+                def put(j, value, spot=spot):
+                    done[spot, block_of(j)] = value
+
+                add_delayed(
+                    lambda j: source[j, spots[0], :],
+                    lambda j: source[j, spots[1], :],
+                    put,
+                    spread[level, spot, :],
+                    level,
+                    total,
+                    out_blocks,
+                )
+        for n in (mask, mask + half):
+            at = pl.multiple_of(jnp.bitwise_xor(mine, n) * share, SUBLANES)
+            stores.append(
+                pltpu.make_async_copy(done.at[pl.ds(at, share), :], outs[n], out_sem.at[n])
+            )
+            stores[-1].start()
+    for store in stores:
+        store.wait()
+
+
+def local_tree(position, spectra, rim, table, freq_count):
+    rows, span = spectra.shape
+    total = (span + rim.shape[1]) // LANES
+    hbm = pl.BlockSpec(memory_space=pl.ANY)
+    return pl.pallas_call(
+        functools.partial(local_tree_kernel, freq_count),
+        out_shape=[jax.ShapeDtypeStruct((rows // freq_count, span), jnp.float32)] * freq_count,
+        in_specs=[
+            pl.BlockSpec(memory_space=pltpu.SMEM),
+            hbm,
+            hbm,
+            pl.BlockSpec(memory_space=pltpu.VMEM),
+        ],
+        out_specs=[hbm] * freq_count,
+        scratch_shapes=[
+            pltpu.VMEM((total, rows, LANES), jnp.float32),
+            pltpu.VMEM((total, rows, LANES), jnp.float32),
+            pltpu.VMEM((rows, span), jnp.float32),
+            pltpu.VMEM((rows.bit_length() - 1, rows, LANES), jnp.int32),
+            pltpu.SemaphoreType.DMA((total,)),
+            pltpu.SemaphoreType.DMA((freq_count,)),
+        ],
+        compiler_params=pltpu.CompilerParams(vmem_limit_bytes=VMEM_LIMIT),
+        cost_estimate=pl.CostEstimate(
+            flops=8 * rows * span, bytes_accessed=8 * rows * span, transcendentals=0
+        ),
+        name="local_tree",
+    )(position, spectra, rim, table)
+
+
+def cross_tree_kernel(rows, masks, rim_count, place, table, *refs):
+    freq_count = len(masks)
+    rims, refs = refs[:rim_count], refs[rim_count:]
+    parts, outs = refs[:freq_count], refs[freq_count : 2 * freq_count]
+    even, odd, done, spread, in_sem, out_sem = refs[2 * freq_count :]
+    share, span = parts[0].shape
+    rim_span = rims[0].shape[2]
+    blocks = (span + rim_span) // LANES
+    mine = place[0]
+    loads = [None] * freq_count
+    edges = [rim.at[n] for rim in rims for n in range(rim.shape[0])]
+    for mask, part, edge in zip(masks, parts, edges):
+        spot = pl.ds(pl.multiple_of(jnp.bitwise_xor(mine, mask) * share, SUBLANES), share)
+        loads[mask] = [
+            pltpu.make_async_copy(part, even.at[spot, pl.ds(0, span)], in_sem.at[0, mask]),
+            pltpu.make_async_copy(edge, even.at[spot, pl.ds(span, rim_span)], in_sem.at[1, mask]),
+        ]
+        for load in loads[mask]:
+            load.start()
+    first_level = rows.bit_length() - 1
+    levels = freq_count.bit_length() - 1
+    tiles = share // SUBLANES
+    spread_shifts(
+        table,
+        spread,
+        lambda n: (n // tiles) * rows + mine * share + (n % tiles) * SUBLANES,
+        freq_count * tiles,
+        range(first_level, first_level + levels),
+    )
+    per_step = 2 if tiles % 2 == 0 else 1
+    stores = []
+    for bit in range(levels):
+        level = first_level + bit
+        out_blocks = blocks - 2**level // LANES
+        last = bit == levels - 1
+        source, target = (even, odd) if bit % 2 == 0 else (odd, even)
+        target = done if last else target
+        for mask in range(freq_count):
+            other = mask + 2**bit
+            if mask & 2**bit:
+                continue
+            if bit == 0:
+                for load in loads[mask] + loads[other]:
+                    load.wait()
+            lower = jnp.bitwise_and(jnp.bitwise_xor(mine, mask), freq_count - 1 - 2**bit)
+            starts = [lower * share, (lower + 2**bit) * share]
+
+            def step(item, carry, bit=bit, level=level, blocks=blocks, out_blocks=out_blocks, source=source, target=target, starts=starts):
+                for n in range(per_step):
+                    at = (item * per_step + n) * SUBLANES
+                    spots = [pl.ds(pl.multiple_of(start + at, SUBLANES), SUBLANES) for start in starts]
+                    for spot in spots:
+
+                        def put(j, value, spot=spot):
+                            target[spot, block_of(j)] = value
+
+                        add_delayed(
+                            lambda j: source[spots[0], block_of(j)],
+                            lambda j: source[spots[1], block_of(j)],
+                            put,
+                            spread[bit, spot, :],
+                            level,
+                            blocks,
+                            out_blocks,
+                        )
+                return carry
+
+            lax.fori_loop(0, tiles // per_step, step, 0)
+            if last:
+                for n in (mask, other):
+                    spot = pl.ds(pl.multiple_of(jnp.bitwise_xor(mine, n) * share, SUBLANES), share)
+                    stores.append(pltpu.make_async_copy(done.at[spot, :], outs[n], out_sem.at[n]))
+                    stores[-1].start()
+        blocks = out_blocks
+    for store in stores:
+        store.wait()
+
+
+def cross_tree(position, table, rims, parts, masks, rows):
+    freq_count = len(parts)
+    share, span = parts[0].shape
+    total = span + rims[0].shape[2]
+    group = freq_count * share
+    hbm = pl.BlockSpec(memory_space=pl.ANY)
+    operands = [*rims, *parts]
+    return pl.pallas_call(
+        functools.partial(cross_tree_kernel, rows, tuple(masks), len(rims)),
+        out_shape=[jax.ShapeDtypeStruct((share, span + LANES), jnp.float32)] * freq_count,
+        in_specs=[pl.BlockSpec(memory_space=pltpu.SMEM), pl.BlockSpec(memory_space=pltpu.VMEM)]
+        + [hbm] * len(operands),
+        out_specs=[hbm] * freq_count,
+        scratch_shapes=[
+            pltpu.VMEM((group, total), jnp.float32),
+            pltpu.VMEM((group, total), jnp.float32),
+            pltpu.VMEM((group, span + LANES), jnp.float32),
+            pltpu.VMEM((freq_count.bit_length() - 1, group, LANES), jnp.int32),
+            pltpu.SemaphoreType.DMA((2, freq_count)),
+            pltpu.SemaphoreType.DMA((freq_count,)),
+        ],
+        compiler_params=pltpu.CompilerParams(vmem_limit_bytes=VMEM_LIMIT),
+        cost_estimate=pl.CostEstimate(
+            flops=4 * group * span, bytes_accessed=8 * group * span, transcendentals=0
+        ),
+        name="cross_tree",
+    )(position, table, *operands)
+
+
+def filter_kernel(masks, place, widths, scale, earlier, *refs):
+    count = len(masks)
+    parts = refs[:count]
+    out, mark, values, halves, before, whole, results, in_sem, out_sem = refs[-9:]
+    mark[...] = jnp.zeros_like(mark)
+    share = parts[0].shape[0]
+    blocks = out.shape[2] // LANES
+    filters = out.shape[0]
+    mine = place[0]
+    loads = [pltpu.make_async_copy(parts[n], values.at[n], in_sem.at[n]) for n in range(count)]
+    for load in loads:
+        load.start()
+    row = lax.broadcasted_iota(jnp.int32, (2 * LANES, 2 * LANES), 0) & (LANES - 1)
+    col = lax.broadcasted_iota(jnp.int32, (2 * LANES, 2 * LANES), 1)
+    ones = ((row < col) | (col >= LANES)).astype(jnp.bfloat16)
+    per_dot = max(n for n in (1, 2, 3, 4, 5, 6, 7) if (blocks + 1) % n == 0)
+    lane = lax.broadcasted_iota(jnp.int32, (SUBLANES, LANES), 1)
+    copies = {}
+    for n, mask in enumerate(masks):
+        slot = n % 2
+        loads[n].wait()
+        for j in range(blocks + 1):
+            exact = values[n, :, block_of(j)]
+            high = exact.astype(jnp.bfloat16)
+            low = (exact - high.astype(jnp.float32)).astype(jnp.bfloat16)
+            halves[j, :, pl.ds(0, LANES)] = high
+            halves[j, :, pl.ds(LANES, LANES)] = low
+        for item in range((blocks + 1) // per_dot):
+            taken = halves[item * per_dot : (item + 1) * per_dot]
+            product = jnp.dot(
+                taken.reshape(per_dot * share, 2 * LANES), ones, preferred_element_type=jnp.float32
+            )
+            for e in range(per_dot):
+                rows = slice(e * share, (e + 1) * share)
+                before[item * per_dot + e] = product[rows, :LANES]
+                whole[item * per_dot + e] = product[rows, LANES:]
+        if n >= 2:
+            for copy in copies[n - 2]:
+                copy.wait()
+
+        def step(item, carry, slot=slot):
+            which, tile = item // (share // SUBLANES), item % (share // SUBLANES)
+            width = widths[which]
+            factor = scale[which]
+            stays = lane < LANES - width
+            at = pl.ds(pl.multiple_of(tile * SUBLANES, SUBLANES), SUBLANES)
+            first = before[0, at, :]
+            turned = pltpu.roll(first, LANES - width, 1)
+            for j in range(blocks):
+                second = before[j + 1, at, :]
+                following = pltpu.roll(second, LANES - width, 1)
+                upper = jnp.where(stays, turned, following + whole[j, at, :])
+                results[slot, which, at, block_of(j)] = (upper - first) * factor
+                first, turned = second, following
+            return carry
+
+        lax.fori_loop(0, filters * share // SUBLANES, step, 0, unroll=8)
+        start = pl.multiple_of(jnp.bitwise_xor(mine, mask) * share, SUBLANES)
+        copies[n] = [
+            pltpu.make_async_copy(
+                results.at[slot, which],
+                out.at[which, pl.ds(start, share), :],
+                out_sem.at[slot, which],
+            )
+            for which in range(filters)
+        ]
+        for copy in copies[n]:
+            copy.start()
+    for n in range(max(0, count - 2), count):
+        for copy in copies[n]:
+            copy.wait()
+
+
+def box_filters(position, widths, scale, earlier, masks, parts, result, rows):
+    share, reach = parts[0].shape
+    span = reach - LANES
+    blocks = span // LANES
+    count = len(masks)
+    filters = scale.shape[0]
+    hbm = pl.BlockSpec(memory_space=pl.ANY)
+    smem = pl.BlockSpec(memory_space=pltpu.SMEM)
+    operands = [position, widths, scale, earlier, *parts]
+    aliases = {}
+    if result is not None:
+        aliases = {len(operands): 0}
+        operands.append(result)
+    return pl.pallas_call(
+        functools.partial(filter_kernel, masks),
+        out_shape=[
+            jax.ShapeDtypeStruct((filters, rows, span), jnp.float32),
+            jax.ShapeDtypeStruct((SUBLANES, LANES), jnp.float32),
+        ],
+        in_specs=[smem] * 3 + [hbm] * (len(operands) - 3),
+        out_specs=[hbm, pl.BlockSpec(memory_space=pltpu.VMEM)],
+        input_output_aliases=aliases,
+        scratch_shapes=[
+            pltpu.VMEM((count, share, reach), jnp.float32),
+            pltpu.VMEM((blocks + 1, share, 2 * LANES), jnp.bfloat16),
+            pltpu.VMEM((blocks + 1, share, LANES), jnp.float32),
+            pltpu.VMEM((blocks + 1, share, LANES), jnp.float32),
+            pltpu.VMEM((2, filters, share, span), jnp.float32),
+            pltpu.SemaphoreType.DMA((count,)),
+            pltpu.SemaphoreType.DMA((2, filters)),
+        ],
+        compiler_params=pltpu.CompilerParams(vmem_limit_bytes=VMEM_LIMIT),
+        cost_estimate=pl.CostEstimate(
+            flops=8 * count * share * span * filters,
+            bytes_accessed=4 * count * share * span * (filters + 1),
+            transcendentals=0,
+        ),
+        name="box_filters",
+    )(*operands)
 
 
 def passed_along(value, axis, steps):
     count = lax.axis_size(axis)
     initial, last = (max(0, -steps), min(count, count - steps))
     return lax.ppermute(value, axis, [(source, source + steps) for source in range(initial, last)])
+
+
+def exchanged(part, mask, freq_count):
+    pairs = [(source, source ^ mask) for source in range(freq_count)]
+    return lax.ppermute(part, "freq", pairs)
+
+
+def by_residues(spectra, delays, widths):
+    rows, span = spectra.shape
+    freq_count = lax.axis_size("freq")
+    channels = rows * freq_count
+    position = lax.axis_index("freq").astype(jnp.int32)[None]
+    local_rim = -(-(rows - 1) // LANES) * LANES
+    rim = passed_along(spectra[:, :local_rim], "tm", -1)
+    table = jnp.pad(delays.T, ((0, 0), (0, LANES - delays.shape[0])))
+    scale = 1.0 / jnp.sqrt(widths.astype(jnp.float32) * channels)
+    half = freq_count // 2
+    near, far = list(range(half)), list(range(half, freq_count))
+    early, late = far[: half // 2], far[half // 2 :]
+    sent = {}
+
+    def ready(value, *keys):
+        for key in keys:
+            value, sent[key] = lax.optimization_barrier((value, sent[key]))
+        return value
+
+    def swap(name, parts, masks, *keys):
+        sent[name, 0] = parts[0]
+        for mask in masks:
+            sent[name, mask] = exchanged(ready(parts[mask], *keys), mask, freq_count)
+
+    def leading(name, masks, length):
+        return passed_along(jnp.stack([sent[name, mask][:, :length] for mask in masks]), "tm", -1)
+
+    parts = local_tree(position, spectra, rim, table, freq_count)
+    name = "out"
+    swap(name, parts, early + near[1:])
+    for before, mask in zip(early, late):
+        swap(name, parts, [mask], (name, before))
+    rims = [leading(name, masks, channels - rows + LANES) for masks in (near, far)]
+    arrived = [sent[name, mask] for mask in near + far]
+    summed = cross_tree(position, table, rims, arrived, near + far, rows)
+    result = None
+    sent["mark"] = jnp.zeros((SUBLANES, LANES), jnp.float32)
+
+    def filters(name, masks):
+        nonlocal result
+        parts = [sent[name, mask] for mask in masks]
+        result, sent["mark"] = box_filters(
+            position, widths, scale, sent["mark"], masks, parts, result, rows
+        )
+
+    name = "back"
+    swap(name, summed, early + near[1:])
+    filters(name, near[:1])
+    swap(name, summed, late[:1], "mark")
+    filters(name, near[1:])
+    swap(name, summed, late[1:], "mark")
+    filters(name, early)
+    filters(name, late)
+    return result
 
 
 def from_partner(value, axis, stride):
@@ -50,7 +517,7 @@
     return summed.reshape(row_count, out_width)
 
 
-def local(spectra, delays, widths):
+def by_levels(spectra, delays, widths):
     row_count, time_span = spectra.shape
     local_levels = row_count.bit_length() - 1
     freq_count = lax.axis_size("freq")
@@ -88,7 +555,7 @@
     output_pos = lax.broadcasted_iota(jnp.int32, (2 * TAPS, filter_count, TAPS), 2)
     distance = input_pos - output_pos
     box_widths = widths[None, :, None]
-    scaling = 1.0 / jnp.sqrt(widths.astype(jnp.float32) * F)
+    scaling = 1.0 / jnp.sqrt(widths.astype(jnp.float32) * (row_count * freq_count))
     filter_matrix = jnp.where(
         (distance >= 0) & (distance < box_widths), scaling[None, :, None], 0.0
     )
@@ -96,6 +563,27 @@
     product = jnp.einsum("rbj,jk->rbk", paired, filter_matrix, precision=lax.Precision.HIGHEST)
     product = product.reshape(row_count, block_count, filter_count, TAPS)
     return jnp.transpose(product, (2, 0, 1, 3)).reshape(filter_count, row_count, time_span)
+
+
+def fits(rows, span, freq_count, levels):
+    channels = rows * freq_count
+    return (
+        rows % 64 == 0
+        and LANES <= rows <= 2 * LANES
+        and rows & (rows - 1) == 0
+        and freq_count & (freq_count - 1) == 0
+        and channels == 2**levels
+        and rows % (freq_count * 2 * SUBLANES) == 0
+        and freq_count >= 4
+        and span % LANES == 0
+        and channels - rows + LANES <= span
+    )
+
+
+def local(spectra, delays, widths):
+    if fits(*spectra.shape, lax.axis_size("freq"), delays.shape[0]):
+        return by_residues(spectra, delays, widths)
+    return by_levels(spectra, delays, widths)
 
 
 def solution(mesh):

time: 535 us -> 166 us (0.31)
  the two profiles are of different devices: /device:TPU:0 before, /device:TPU:10 now
where the time goes in v2:
time: 166 us; the launch traced here: 165 us
  waiting for transfers between devices  95.3 us (57%)
  Pallas kernels  42.5 us (26%)
  starting transfers between devices  23.7 us (14%)
  local copies, waits for them, and re-layouts  3.43 us (2%)
    ppermute x14, waiting for transfers between devices, exchanged(): return lax.ppermute(part, 'freq', pairs)  91.6 us
    pallas_call x4, Pallas kernels, box_filters(): pl.pallas_call(functools.partial(filter_kernel, masks), out_shape=[jax.Sh...  21.5 us
    ppermute x14, starting transfers between devices, exchanged(): return lax.ppermute(part, 'freq', pairs)  19.7 us
    pallas_call x1, Pallas kernels, local_tree(): pl.pallas_call(functools.partial(local_tree_kernel, freq_count), out_shap...  12.3 us
    pallas_call x1, Pallas kernels, cross_tree(): pl.pallas_call(functools.partial(cross_tree_kernel, rows, tuple(masks), l...  8.66 us
    ppermute x3, starting transfers between devices, passed_along(): lax.ppermute(value, axis, [(source, source + steps) for source in range(i...  4.06 us
    ppermute x3, waiting for transfers between devices, passed_along(): lax.ppermute(value, axis, [(source, source + steps) for source in range(i...  3.73 us
  transfers between devices with their start and end apart: 17, of which 11 were waited for; matrix products, arithmetic and copies ran while one was open for 1% of the time, Pallas kernels for 9%

profile of v2, /device:TPU:10, one launch (start us, length us, event | category | flops | bytes accessed | tf_op | source)
XLA Modules:
  0.0 165.4 jit_solution(9415612021258066351)
XLA Ops:
  0.0 1.0 slice.27
  1.0 1.3 collective-permute-start
  2.3 1.3 copy.7
  4.4 12.3 %local_tree.1 = (f32[32,2560]{1,0:T(8,128)S(1)}, f32[32,2560]{1,0:T(8,128)S(1)}, f32[32,2560]{1,0:T(8,128)S(1)}, f32[32,2560]{1,0:T(8,128)S(1)}, f32[32,2560]{1,...) custom-call(s32[1]{0:T(128)} %bitcast.place, f32[256,2560]{1,0:T(8,128)} %spectra.1, ...), custom_call_target="tpu_custom_call" | custom-call | flops 5242880 | bytes 5242880 | tf_op jit(solution)/shard_map/local_tree/pallas_call | solution.py:169
  16.7 1.6 collective-permute-start.1
  18.8 1.5 collective-permute-start.3
  20.3 2.6 %collective-permute-start.5 = (f32[32,2560]{1,0:T(8,128)S(1)}, f32[32,2560]{1,0:T(8,128)S(1)}, u32[]{:S(2)}, u32[]{:S(2)}) collective-permute-start(f32[32,2560]{1,0:T(8,128)S(1)} %get-tuple-element.41), channel_id=1, source_target_pairs={{0,8},{2,10},{4,12},{6,14},{8,0},{10,2},{12,4},{14,6},{1,9},{3,11}... | collective-permute-start | bytes 983048 | tf_op jit(solution)/shard_map/ppermute | solution.py:424
  22.9 1.3 collective-permute-start.6
  24.2 19.8 %collective-permute-done.5.refs_6_ = f32[32,2560]{1,0:T(8,128)S(1)} collective-permute-done((f32[32,2560]{1,0:T(8,128)S(1)}, f32[32,2560]{1,0:T(8,128)S(1)}, u32[]{:S(2)}, u32[]{:S(2)}) %collective-permute-start.5) | collective-permute-done | bytes 327712 | tf_op jit(solution)/shard_map/ppermute | solution.py:424
  44.4 14.6 %collective-permute-done.6.refs_7_ = f32[32,2560]{1,0:T(8,128)S(1)} collective-permute-done((f32[32,2560]{1,0:T(8,128)S(1)}, f32[32,2560]{1,0:T(8,128)S(1)}, u32[]{:S(2)}, u32[]{:S(2)}) %collective-permute-start.6) | collective-permute-done | bytes 327712 | tf_op jit(solution)/shard_map/ppermute | solution.py:424
  59.5 1.3 collective-permute-start.4
  60.9 12.2 %collective-permute-done.7.refs_8_ = f32[32,2560]{1,0:T(8,128)S(1)} collective-permute-done((f32[32,2560]{1,0:T(8,128)S(1)}, f32[32,2560]{1,0:T(8,128)S(1)}, u32[]{:S(2)}, u32[]{:S(2)}) %collective-permute-start.7) | collective-permute-done | bytes 327712 | tf_op jit(solution)/shard_map/ppermute | solution.py:424
  73.1 6.7 %collective-permute-done.8.refs_9_ = f32[32,2560]{1,0:T(8,128)S(1)} collective-permute-done((f32[32,2560]{1,0:T(8,128)S(1)}, f32[32,2560]{1,0:T(8,128)S(1)}, u32[]{:S(2)}, u32[]{:S(2)}) %collective-permute-start.8) | collective-permute-done | bytes 327712 | tf_op jit(solution)/shard_map/ppermute | solution.py:424
  80.0 1.5 collective-permute-start.9
  81.5 3.0 %collective-permute-done.9.refs_1_ = f32[4,32,1920]{2,1,0:T(8,128)S(1)} collective-permute-done((f32[4,32,1920]{2,1,0:T(8,128)S(1)}, f32[4,32,1920]{2,1,0:T(8,128)S(1)}, u32[]{:S(2)}, u32[]{:S(2)}) %collective-permute-start.9) | collective-permute-done | bytes 983072 | tf_op jit(solution)/shard_map/ppermute | solution.py:419
  84.4 1.0 copy-done.3
  85.4 8.7 %cross_tree.1 = (f32[32,2688]{1,0:T(8,128)S(1)}, f32[32,2688]{1,0:T(8,128)S(1)}, f32[32,2688]{1,0:T(8,128)S(1)}, f32[32,2688]{1,0:T(8,128)S(1)}, f32[32,2688]{1,...) custom-call(s32[1]{0:T(128)} %bitcast.place, s32[2048,128]{1,0:T(8,128)} %copy-done, ...), custom_call_target="tpu_custom_call" | custom-call | flops 2621440 | bytes 5242880 | tf_op jit(solution)/shard_map/cross_tree/pallas_call | solution.py:280
  94.1 0.8 collective-permute-start.10
  94.9 2.7 %collective-permute-start.12 = (f32[32,2688]{1,0:T(8,128)S(1)}, f32[32,2688]{1,0:T(8,128)S(1)}, u32[]{:S(2)}, u32[]{:S(2)}) collective-permute-start(f32[32,2688]{1,0:T(8,128)S(1)} %get-tuple-element.55), channel_id=1, source_target_pairs={{0,6},{2,4},{4,2},{6,0},{8,14},{10,12},{12,10},{14,8},{1,7},{3,5},... | collective-permute-start | bytes 1032200 | tf_op jit(solution)/shard_map/ppermute | solution.py:424
  97.6 2.1 %collective-permute-start.13 = (f32[32,2688]{1,0:T(8,128)S(1)}, f32[32,2688]{1,0:T(8,128)S(1)}, u32[]{:S(2)}, u32[]{:S(2)}) collective-permute-start(f32[32,2688]{1,0:T(8,128)S(1)} %get-tuple-element.59), channel_id=1, source_target_pairs={{0,8},{2,10},{4,12},{6,14},{8,0},{10,2},{12,4},{14,6},{1,9},{3,11}... | collective-permute-start | bytes 1032200 | tf_op jit(solution)/shard_map/ppermute | solution.py:424
  99.8 1.0 collective-permute-start.14
  100.8 3.7 %box_filters.4 = (f32[8,256,2560]{2,1,0:T(8,128)}, f32[8,128]{1,0:T(8,128)S(1)}) custom-call(s32[1]{0:T(128)} %bitcast.place, s32[8]{0:T(128)S(1)} %copy-done.1, f32[8]{0:T(128)S(1)} %multiply_rsqrt_fusion.scale, f32[8,128]{1,0:T(8,128)S(1)} %broadcast_in_dim.7.earlier, f32[32,2688]{1,0:T(8,128)S(1)} %get-tuple-element.50.refs_0_), custom_call_target="tpu_custom_call" | custom-call | flops 5242880 | bytes 2949120 | tf_op jit(solution)/shard_map/box_filters/pallas_call | solution.py:388
  104.5 2.5 %collective-permute-start.15 = (f32[32,2688]{1,0:T(8,128)S(1)}, f32[32,2688]{1,0:T(8,128)S(1)}, u32[]{:S(2)}, u32[]{:S(2)}) collective-permute-start(f32[32,2688]{1,0:T(8,128)S(1)} %get-tuple-element.63), channel_id=1, source_target_pairs={{0,12},{2,14},{4,8},{6,10},{8,4},{10,6},{12,0},{14,2},{1,13},{3,15... | collective-permute-start | bytes 1032200 | tf_op jit(solution)/shard_map/ppermute | solution.py:424
  107.0 9.8 %collective-permute-done.11.refs_1_ = f32[32,2688]{1,0:T(8,128)S(1)} collective-permute-done((f32[32,2688]{1,0:T(8,128)S(1)}, f32[32,2688]{1,0:T(8,128)S(1)}, u32[]{:S(2)}, u32[]{:S(2)}) %collective-permute-start.11) | collective-permute-done | bytes 344096 | tf_op jit(solution)/shard_map/ppermute | solution.py:424
  116.8 6.6 %collective-permute-done.12.refs_2_ = f32[32,2688]{1,0:T(8,128)S(1)} collective-permute-done((f32[32,2688]{1,0:T(8,128)S(1)}, f32[32,2688]{1,0:T(8,128)S(1)}, u32[]{:S(2)}, u32[]{:S(2)}) %collective-permute-start.12) | collective-permute-done | bytes 344096 | tf_op jit(solution)/shard_map/ppermute | solution.py:424
  123.4 6.8 %box_filters.5 = (f32[8,256,2560]{2,1,0:T(8,128)}, f32[8,128]{1,0:T(8,128)S(1)}) custom-call(s32[1]{0:T(128)} %bitcast.place, s32[8]{0:T(128)S(1)} %copy-done.1, f32[8]{0:T(128)S(1)} %multiply_rsqrt_fusion.scale, f32[8,128]{1,0:T(8,128)S(1)} %get-tuple-element.52.earlier, ...), custom_call_target="tpu_custom_call", output_to_operand_aliasing={{0}: (7, {})} | custom-call | flops 15728640 | bytes 8847360 | tf_op jit(solution)/shard_map/box_filters/pallas_call | solution.py:388
  130.1 2.3 %collective-permute-start.16 = (f32[32,2688]{1,0:T(8,128)S(1)}, f32[32,2688]{1,0:T(8,128)S(1)}, u32[]{:S(2)}, u32[]{:S(2)}) collective-permute-start(f32[32,2688]{1,0:T(8,128)S(1)} %get-tuple-element.64), channel_id=1, source_target_pairs={{0,14},{2,12},{4,10},{6,8},{8,6},{10,4},{12,2},{14,0},{1,15},{3,13... | collective-permute-start | bytes 1032200 | tf_op jit(solution)/shard_map/ppermute | solution.py:424
  132.4 12.7 %collective-permute-done.14.refs_1_ = f32[32,2688]{1,0:T(8,128)S(1)} collective-permute-done((f32[32,2688]{1,0:T(8,128)S(1)}, f32[32,2688]{1,0:T(8,128)S(1)}, u32[]{:S(2)}, u32[]{:S(2)}) %collective-permute-start.14) | collective-permute-done | bytes 344096 | tf_op jit(solution)/shard_map/ppermute | solution.py:424
  145.1 5.3 %box_filters.6 = (f32[8,256,2560]{2,1,0:T(8,128)}, f32[8,128]{1,0:T(8,128)S(1)}) custom-call(s32[1]{0:T(128)} %bitcast.place, s32[8]{0:T(128)S(1)} %copy-done.1, f32[8]{0:T(128)S(1)} %multiply_rsqrt_fusion.scale, f32[8,128]{1,0:T(8,128)S(1)} %get-tuple-element.58.earlier, ...), custom_call_target="tpu_custom_call", output_to_operand_aliasing={{0}: (6, {})} | custom-call | flops 10485760 | bytes 5898240 | tf_op jit(solution)/shard_map/box_filters/pallas_call | solution.py:388
  150.4 3.1 %collective-permute-done.15.refs_0_ = f32[32,2688]{1,0:T(8,128)S(1)} collective-permute-done((f32[32,2688]{1,0:T(8,128)S(1)}, f32[32,2688]{1,0:T(8,128)S(1)}, u32[]{:S(2)}, u32[]{:S(2)}) %collective-permute-start.15) | collective-permute-done | bytes 344096 | tf_op jit(solution)/shard_map/ppermute | solution.py:424
  153.5 5.9 %collective-permute-done.16.refs_1_ = f32[32,2688]{1,0:T(8,128)S(1)} collective-permute-done((f32[32,2688]{1,0:T(8,128)S(1)}, f32[32,2688]{1,0:T(8,128)S(1)}, u32[]{:S(2)}, u32[]{:S(2)}) %collective-permute-start.16) | collective-permute-done | bytes 344096 | tf_op jit(solution)/shard_map/ppermute | solution.py:424
  159.5 5.8 %box_filters.7 = (f32[8,256,2560]{2,1,0:T(8,128)}, f32[8,128]{1,0:T(8,128)}) custom-call(s32[1]{0:T(128)} %bitcast.place, s32[8]{0:T(128)S(1)} %copy-done.1, f32[8]{0:T(128)S(1)} %multiply_rsqrt_fusion.scale, f32[8,128]{1,0:T(8,128)S(1)} %get-tuple-element.62.earlier, ...), custom_call_target="tpu_custom_call", output_to_operand_aliasing={{0}: (6, {})} | custom-call | flops 10485760 | bytes 5898240 | tf_op jit(solution)/shard_map/box_filters/pallas_call | solution.py:388
  (30 shorter events, 2.3 us)
Async XLA Ops:
  0.0 97.6 %copy-start.1 = (s32[8]{0:T(128)S(1)}, s32[8]{0:T(128)}, u32[]{:S(2)}) copy-start(s32[8]{0:T(128)} %widths.7) | copy-start | bytes 100
  1.0 3.4 %collective-permute-start = (f32[256,256]{1,0:T(8,128)S(1)}, f32[256,256]{1,0:T(8,128)S(1)}, u32[]{:S(2)}, u32[]{:S(2)}) collective-permute-start(f32[256,256]{1,0:T(8,128)S(1)} %slice.27), channel_id=1, source_target_pairs={{1,0},{3,2},{5,4},{7,6},{9,8},{11,10},{13,12},{15,14},{17,16},{19,... | collective-permute-start | bytes 786440 | tf_op jit(solution)/shard_map/ppermute | solution.py:419
  3.6 80.8 %copy-start = (s32[2048,128]{1,0:T(8,128)}, s32[2048,128]{1,0:T(8,128)S(1)}, u32[]{:S(2)}) copy-start(s32[2048,128]{1,0:T(8,128)S(1)} %pad.4.table) | copy-start | bytes 3145732
  16.7 42.6 %collective-permute-start.1 = (f32[32,2560]{1,0:T(8,128)S(1)}, f32[32,2560]{1,0:T(8,128)S(1)}, u32[]{:S(2)}, u32[]{:S(2)}) collective-permute-start(f32[32,2560]{1,0:T(8,128)S(1)} %get-tuple-element.37), channel_id=1, source_target_pairs={{0,2},{2,0},{4,6},{6,4},{8,10},{10,8},{12,14},{14,12},{1,3},{3,1},... | collective-permute-start | bytes 983048 | tf_op jit(solution)/shard_map/ppermute | solution.py:424
  18.3 41.1 %collective-permute-start.2 = (f32[32,2560]{1,0:T(8,128)S(1)}, f32[32,2560]{1,0:T(8,128)S(1)}, u32[]{:S(2)}, u32[]{:S(2)}) collective-permute-start(f32[32,2560]{1,0:T(8,128)S(1)} %get-tuple-element.38), channel_id=1, source_target_pairs={{0,4},{2,6},{4,0},{6,2},{8,12},{10,14},{12,8},{14,10},{1,5},{3,7},... | collective-permute-start | bytes 983048 | tf_op jit(solution)/shard_map/ppermute | solution.py:424
  18.8 40.7 %collective-permute-start.3 = (f32[32,2560]{1,0:T(8,128)S(1)}, f32[32,2560]{1,0:T(8,128)S(1)}, u32[]{:S(2)}, u32[]{:S(2)}) collective-permute-start(f32[32,2560]{1,0:T(8,128)S(1)} %get-tuple-element.39), channel_id=1, source_target_pairs={{0,6},{2,4},{4,2},{6,0},{8,14},{10,12},{12,10},{14,8},{1,7},{3,5},... | collective-permute-start | bytes 983048 | tf_op jit(solution)/shard_map/ppermute | solution.py:424
  20.3 23.7 %collective-permute-start.5 = (f32[32,2560]{1,0:T(8,128)S(1)}, f32[32,2560]{1,0:T(8,128)S(1)}, u32[]{:S(2)}, u32[]{:S(2)}) collective-permute-start(f32[32,2560]{1,0:T(8,128)S(1)} %get-tuple-element.41), channel_id=1, source_target_pairs={{0,8},{2,10},{4,12},{6,14},{8,0},{10,2},{12,4},{14,6},{1,9},{3,11}... | collective-permute-start | bytes 983048 | tf_op jit(solution)/shard_map/ppermute | solution.py:424
  22.9 36.2 %collective-permute-start.6 = (f32[32,2560]{1,0:T(8,128)S(1)}, f32[32,2560]{1,0:T(8,128)S(1)}, u32[]{:S(2)}, u32[]{:S(2)}) collective-permute-start(f32[32,2560]{1,0:T(8,128)S(1)} %get-tuple-element.44), channel_id=1, source_target_pairs={{0,10},{2,8},{4,14},{6,12},{8,2},{10,0},{12,6},{14,4},{1,11},{3,9}... | collective-permute-start | bytes 983048 | tf_op jit(solution)/shard_map/ppermute | solution.py:424
  44.0 29.1 %collective-permute-start.7 = (f32[32,2560]{1,0:T(8,128)S(1)}, f32[32,2560]{1,0:T(8,128)S(1)}, u32[]{:S(2)}, u32[]{:S(2)}) collective-permute-start(f32[32,2560]{1,0:T(8,128)S(1)} %get-tuple-element.46), channel_id=1, source_target_pairs={{0,12},{2,14},{4,8},{6,10},{8,4},{10,6},{12,0},{14,2},{1,13},{3,15... | collective-permute-start | bytes 983048 | tf_op jit(solution)/shard_map/ppermute | solution.py:424
  59.1 20.8 %collective-permute-start.8 = (f32[32,2560]{1,0:T(8,128)S(1)}, f32[32,2560]{1,0:T(8,128)S(1)}, u32[]{:S(2)}, u32[]{:S(2)}) collective-permute-start(f32[32,2560]{1,0:T(8,128)S(1)} %get-tuple-element.47), channel_id=1, source_target_pairs={{0,14},{2,12},{4,10},{6,8},{8,6},{10,4},{12,2},{14,0},{1,15},{3,13... | collective-permute-start | bytes 983048 | tf_op jit(solution)/shard_map/ppermute | solution.py:424
  59.5 21.9 %collective-permute-start.4 = (f32[4,32,1920]{2,1,0:T(8,128)S(1)}, f32[4,32,1920]{2,1,0:T(8,128)S(1)}, u32[]{:S(2)}, u32[]{:S(2)}) collective-permute-start(f32[4,32,1920]{2,1,0:T(8,128)S(1)} %pad_maximum_fusion), channel_id=1, source_target_pairs={{1,0},{3,2},{5,4},{7,6},{9,8},{11,10},{13,12},{15,14},{17,16},{19,... | collective-permute-start | bytes 2949128 | tf_op jit(solution)/shard_map/ppermute | solution.py:419
  80.0 4.5 %collective-permute-start.9 = (f32[4,32,1920]{2,1,0:T(8,128)S(1)}, f32[4,32,1920]{2,1,0:T(8,128)S(1)}, u32[]{:S(2)}, u32[]{:S(2)}) collective-permute-start(f32[4,32,1920]{2,1,0:T(8,128)S(1)} %pad_maximum_fusion.1), channel_id=1, source_target_pairs={{1,0},{3,2},{5,4},{7,6},{9,8},{11,10},{13,12},{15,14},{17,16},{19,... | collective-permute-start | bytes 2949128 | tf_op jit(solution)/shard_map/ppermute | solution.py:419
  81.5 3.0 %copy-start.2 = (f32[4,32,1920]{2,1,0:T(8,128)}, f32[4,32,1920]{2,1,0:T(8,128)S(1)}, u32[]{:S(2)}) copy-start(f32[4,32,1920]{2,1,0:T(8,128)S(1)} %collective-permute-done.4.refs_0_) | copy-start | bytes 2949124
  84.4 1.0 copy-start.3
  94.1 10.4 %collective-permute-start.10 = (f32[32,2688]{1,0:T(8,128)S(1)}, f32[32,2688]{1,0:T(8,128)S(1)}, u32[]{:S(2)}, u32[]{:S(2)}) collective-permute-start(f32[32,2688]{1,0:T(8,128)S(1)} %get-tuple-element.53), channel_id=1, source_target_pairs={{0,2},{2,0},{4,6},{6,4},{8,10},{10,8},{12,14},{14,12},{1,3},{3,1},... | collective-permute-start | bytes 1032200 | tf_op jit(solution)/shard_map/ppermute | solution.py:424
  94.9 21.9 %collective-permute-start.11 = (f32[32,2688]{1,0:T(8,128)S(1)}, f32[32,2688]{1,0:T(8,128)S(1)}, u32[]{:S(2)}, u32[]{:S(2)}) collective-permute-start(f32[32,2688]{1,0:T(8,128)S(1)} %get-tuple-element.54), channel_id=1, source_target_pairs={{0,4},{2,6},{4,0},{6,2},{8,12},{10,14},{12,8},{14,10},{1,5},{3,7},... | collective-permute-start | bytes 1032200 | tf_op jit(solution)/shard_map/ppermute | solution.py:424
  94.9 28.4 %collective-permute-start.12 = (f32[32,2688]{1,0:T(8,128)S(1)}, f32[32,2688]{1,0:T(8,128)S(1)}, u32[]{:S(2)}, u32[]{:S(2)}) collective-permute-start(f32[32,2688]{1,0:T(8,128)S(1)} %get-tuple-element.55), channel_id=1, source_target_pairs={{0,6},{2,4},{4,2},{6,0},{8,14},{10,12},{12,10},{14,8},{1,7},{3,5},... | collective-permute-start | bytes 1032200 | tf_op jit(solution)/shard_map/ppermute | solution.py:424
  97.6 34.8 %collective-permute-start.13 = (f32[32,2688]{1,0:T(8,128)S(1)}, f32[32,2688]{1,0:T(8,128)S(1)}, u32[]{:S(2)}, u32[]{:S(2)}) collective-permute-start(f32[32,2688]{1,0:T(8,128)S(1)} %get-tuple-element.59), channel_id=1, source_target_pairs={{0,8},{2,10},{4,12},{6,14},{8,0},{10,2},{12,4},{14,6},{1,9},{3,11}... | collective-permute-start | bytes 1032200 | tf_op jit(solution)/shard_map/ppermute | solution.py:424
  99.8 45.4 %collective-permute-start.14 = (f32[32,2688]{1,0:T(8,128)S(1)}, f32[32,2688]{1,0:T(8,128)S(1)}, u32[]{:S(2)}, u32[]{:S(2)}) collective-permute-start(f32[32,2688]{1,0:T(8,128)S(1)} %get-tuple-element.60), channel_id=1, source_target_pairs={{0,10},{2,8},{4,14},{6,12},{8,2},{10,0},{12,6},{14,4},{1,11},{3,9}... | collective-permute-start | bytes 1032200 | tf_op jit(solution)/shard_map/ppermute | solution.py:424
  104.5 49.1 %collective-permute-start.15 = (f32[32,2688]{1,0:T(8,128)S(1)}, f32[32,2688]{1,0:T(8,128)S(1)}, u32[]{:S(2)}, u32[]{:S(2)}) collective-permute-start(f32[32,2688]{1,0:T(8,128)S(1)} %get-tuple-element.63), channel_id=1, source_target_pairs={{0,12},{2,14},{4,8},{6,10},{8,4},{10,6},{12,0},{14,2},{1,13},{3,15... | collective-permute-start | bytes 1032200 | tf_op jit(solution)/shard_map/ppermute | solution.py:424
  130.1 29.3 %collective-permute-start.16 = (f32[32,2688]{1,0:T(8,128)S(1)}, f32[32,2688]{1,0:T(8,128)S(1)}, u32[]{:S(2)}, u32[]{:S(2)}) collective-permute-start(f32[32,2688]{1,0:T(8,128)S(1)} %get-tuple-element.64), channel_id=1, source_target_pairs={{0,14},{2,12},{4,10},{6,8},{8,6},{10,4},{12,2},{14,0},{1,15},{3,13... | collective-permute-start | bytes 1032200 | tf_op jit(solution)/shard_map/ppermute | solution.py:424

commit v3 on v2

--- a/solution.py
+++ b/solution.py
@@ -10,7 +10,8 @@
 LANES = 128
 SUBLANES = 8
 TAPS = 128
-VMEM_LIMIT = 48 * 2**20
+LATER = 0.5
+LOCAL_VMEM, CROSS_VMEM, FILTER_VMEM = 60 * 2**20, 24 * 2**20, 16 * 2**20
 
 
 def lane_gather(block, index):
@@ -51,13 +52,13 @@
     return slice(j * LANES, (j + 1) * LANES)
 
 
-def spread_shifts(table, spread, rows_at, count, levels):
+def spread_shifts(table, spread, count, levels):
     per_step = max(n for n in (1, 2, 4) if count % n == 0)
 
     def step(item, carry):
         for e in range(per_step):
             tile = item * per_step + e
-            values = table[pl.ds(pl.multiple_of(rows_at(tile), SUBLANES), SUBLANES), :]
+            values = table[pl.ds(pl.multiple_of(tile * SUBLANES, SUBLANES), SUBLANES), :]
             for n, level in enumerate(levels):
                 spread[n, pl.ds(pl.multiple_of(tile * SUBLANES, SUBLANES), SUBLANES), :] = (
                     jnp.broadcast_to(values[:, level : level + 1], (SUBLANES, LANES))
@@ -67,31 +68,42 @@
     lax.fori_loop(0, count // per_step, step, 0)
 
 
-def local_tree_kernel(freq_count, place, spectra, rim, table, *refs):
+def views(parts, count, mine, share):
+    if len(parts) == 1:
+        return [(parts[0], pl.ds(0, count))]
+    return [
+        (part, pl.ds(pl.multiple_of(jnp.bitwise_xor(mine, mask) * share, SUBLANES), share))
+        for mask, part in enumerate(parts)
+    ]
+
+
+def local_tree_kernel(chunks, freq_count, place, spectra, rim, table, *refs):
     rows, span = spectra.shape
     levels = rows.bit_length() - 1
-    outs, (even, odd, done, spread, in_sem, out_sem) = refs[:freq_count], refs[freq_count:]
+    outs, (even, odd, done, spread, held, in_sem, out_sem) = refs[:-7], refs[-7:]
     total, out_blocks = even.shape[0], span // LANES
     mine = place[0]
+    own = table.at[pl.ds(pl.multiple_of(mine * rows, SUBLANES), rows), :]
+    shifts = pltpu.make_async_copy(own, held, in_sem.at[total])
     loads = []
     for j in range(total):
         at = j - out_blocks
         source = rim.at[:, block_of(at)] if at >= 0 else spectra.at[:, block_of(j)]
         loads.append(pltpu.make_async_copy(source, even.at[j], in_sem.at[j]))
-    for load in loads:
+    for load in [shifts, *loads]:
         load.start()
-    spread_shifts(
-        table, spread, lambda tile: mine * rows + tile * SUBLANES, rows // SUBLANES, range(levels)
-    )
+    shifts.wait()
+    spread_shifts(held, spread, rows // SUBLANES, range(levels))
     for load in loads:
         load.wait()
     pairs = rows // (2 * SUBLANES)
     per_step = max(n for n in (1, 2, 4) if pairs % n == 0)
-    for level in range(levels - 1):
+    for level in range(levels):
         half = 2**level
+        last = level == levels - 1
         source, target = (even, odd) if level % 2 == 0 else (odd, even)
 
-        def step(item, carry, level=level, half=half, source=source, target=target):
+        def step(item, carry, level=level, half=half, last=last, source=source, target=target):
             for n in range(per_step):
                 pair = item * per_step + n
                 if half < SUBLANES:
@@ -110,7 +122,10 @@
                 for spot in spots:
 
                     def put(j, value, spot=spot):
-                        target[j, spot, :] = value
+                        if last:
+                            done[spot, block_of(j)] = value
+                        else:
+                            target[j, spot, :] = value
 
                     add_delayed(
                         lambda j: source[j, spots[0], :],
@@ -119,72 +134,47 @@
                         spread[level, spot, :],
                         level,
                         total,
-                        total,
+                        out_blocks if last else total,
                     )
             return carry
 
         lax.fori_loop(0, pairs // per_step, step, 0)
-    level = levels - 1
-    source = even if level % 2 == 0 else odd
-    half = freq_count // 2
-    share = rows // freq_count
-    tiles = share // SUBLANES
     stores = []
-    for mask in range(half):
-        lower = jnp.bitwise_and(jnp.bitwise_xor(mine, mask), half - 1)
-        starts = [lower * share, (lower + half) * share]
-        for tile in range(tiles):
-            spots = [
-                pl.ds(pl.multiple_of(start + tile * SUBLANES, SUBLANES), SUBLANES)
-                for start in starts
-            ]
-            for spot in spots:
-
-                def put(j, value, spot=spot):
-                    done[spot, block_of(j)] = value
-
-                add_delayed(
-                    lambda j: source[j, spots[0], :],
-                    lambda j: source[j, spots[1], :],
-                    put,
-                    spread[level, spot, :],
-                    level,
-                    total,
-                    out_blocks,
-                )
-        for n in (mask, mask + half):
-            at = pl.multiple_of(jnp.bitwise_xor(mine, n) * share, SUBLANES)
-            stores.append(
-                pltpu.make_async_copy(done.at[pl.ds(at, share), :], outs[n], out_sem.at[n])
-            )
-            stores[-1].start()
+    for start, count, parts in chunks:
+        targets, outs = outs[:parts], outs[parts:]
+        for target, spot in views(targets, count, mine, count // freq_count):
+            source = done.at[pl.ds(start, count), :].at[spot, :]
+            stores.append(pltpu.make_async_copy(source, target, out_sem.at[len(stores)]))
+    for store in stores:
+        store.start()
     for store in stores:
         store.wait()
 
 
-def local_tree(position, spectra, rim, table, freq_count):
+def local_tree(position, spectra, rim, table, chunks, freq_count):
+    count = sum(parts for _, _, parts in chunks)
     rows, span = spectra.shape
     total = (span + rim.shape[1]) // LANES
     hbm = pl.BlockSpec(memory_space=pl.ANY)
     return pl.pallas_call(
-        functools.partial(local_tree_kernel, freq_count),
-        out_shape=[jax.ShapeDtypeStruct((rows // freq_count, span), jnp.float32)] * freq_count,
-        in_specs=[
-            pl.BlockSpec(memory_space=pltpu.SMEM),
-            hbm,
-            hbm,
-            pl.BlockSpec(memory_space=pltpu.VMEM),
+        functools.partial(local_tree_kernel, tuple(chunks), freq_count),
+        out_shape=[
+            jax.ShapeDtypeStruct((size // parts, span), jnp.float32)
+            for _, size, parts in chunks
+            for _ in range(parts)
         ],
-        out_specs=[hbm] * freq_count,
+        in_specs=[pl.BlockSpec(memory_space=pltpu.SMEM), hbm, hbm, hbm],
+        out_specs=[pl.BlockSpec(memory_space=pltpu.HBM)] * count,
         scratch_shapes=[
             pltpu.VMEM((total, rows, LANES), jnp.float32),
             pltpu.VMEM((total, rows, LANES), jnp.float32),
             pltpu.VMEM((rows, span), jnp.float32),
             pltpu.VMEM((rows.bit_length() - 1, rows, LANES), jnp.int32),
-            pltpu.SemaphoreType.DMA((total,)),
-            pltpu.SemaphoreType.DMA((freq_count,)),
+            pltpu.VMEM((rows, LANES), jnp.int32),
+            pltpu.SemaphoreType.DMA((total + 1,)),
+            pltpu.SemaphoreType.DMA((count,)),
         ],
-        compiler_params=pltpu.CompilerParams(vmem_limit_bytes=VMEM_LIMIT),
+        compiler_params=pltpu.CompilerParams(vmem_limit_bytes=LOCAL_VMEM),
         cost_estimate=pl.CostEstimate(
             flops=8 * rows * span, bytes_accessed=8 * rows * span, transcendentals=0
         ),
@@ -192,123 +182,128 @@
     )(position, spectra, rim, table)
 
 
-def cross_tree_kernel(rows, masks, rim_count, place, table, *refs):
-    freq_count = len(masks)
-    rims, refs = refs[:rim_count], refs[rim_count:]
-    parts, outs = refs[:freq_count], refs[freq_count : 2 * freq_count]
-    even, odd, done, spread, in_sem, out_sem = refs[2 * freq_count :]
-    share, span = parts[0].shape
-    rim_span = rims[0].shape[2]
-    blocks = (span + rim_span) // LANES
+def cross_tree_kernel(rows, freq_count, base, count, place, table, rim, *refs):
+    parts, outs, refs = refs[:count], refs[count : 2 * count], refs[2 * count :]
+    even, odd, done, spread, held, in_sem, out_sem = refs
+    group, span = even.shape[0], parts[0].shape[1]
+    share = group // freq_count
+    blocks = even.shape[1] // LANES
     mine = place[0]
-    loads = [None] * freq_count
-    edges = [rim.at[n] for rim in rims for n in range(rim.shape[0])]
-    for mask, part, edge in zip(masks, parts, edges):
-        spot = pl.ds(pl.multiple_of(jnp.bitwise_xor(mine, mask) * share, SUBLANES), share)
-        loads[mask] = [
-            pltpu.make_async_copy(part, even.at[spot, pl.ds(0, span)], in_sem.at[0, mask]),
-            pltpu.make_async_copy(edge, even.at[spot, pl.ds(span, rim_span)], in_sem.at[1, mask]),
-        ]
-        for load in loads[mask]:
-            load.start()
+    loads = []
+    for owner in range(freq_count):
+        start = pl.multiple_of(owner * rows + base + mine * share, SUBLANES)
+        spot = pl.ds(owner * share, share)
+        loads.append(
+            pltpu.make_async_copy(
+                table.at[pl.ds(start, share), :], held.at[spot, :], in_sem.at[owner]
+            )
+        )
+    sources = [(0, pair) for pair in views(parts, group, mine, share)]
+    edges = [rim] if count == 1 else [rim.at[n] for n in range(count)]
+    sources += [(span, pair) for pair in views(edges, group, mine, share)]
+    for start, (source, spot) in sources:
+        target = even.at[spot, pl.ds(start, source.shape[1])]
+        loads.append(pltpu.make_async_copy(source, target, in_sem.at[len(loads)]))
+    for load in loads:
+        load.start()
+    for load in loads[:freq_count]:
+        load.wait()
     first_level = rows.bit_length() - 1
     levels = freq_count.bit_length() - 1
     tiles = share // SUBLANES
-    spread_shifts(
-        table,
-        spread,
-        lambda n: (n // tiles) * rows + mine * share + (n % tiles) * SUBLANES,
-        freq_count * tiles,
-        range(first_level, first_level + levels),
-    )
-    per_step = 2 if tiles % 2 == 0 else 1
-    stores = []
+    spread_shifts(held, spread, freq_count * tiles, range(first_level, first_level + levels))
+    for load in loads[freq_count:]:
+        load.wait()
+    items = freq_count // 2 * tiles
+    per_step = 2 if items % 2 == 0 else 1
     for bit in range(levels):
         level = first_level + bit
         out_blocks = blocks - 2**level // LANES
-        last = bit == levels - 1
         source, target = (even, odd) if bit % 2 == 0 else (odd, even)
-        target = done if last else target
-        for mask in range(freq_count):
-            other = mask + 2**bit
-            if mask & 2**bit:
-                continue
-            if bit == 0:
-                for load in loads[mask] + loads[other]:
-                    load.wait()
-            lower = jnp.bitwise_and(jnp.bitwise_xor(mine, mask), freq_count - 1 - 2**bit)
-            starts = [lower * share, (lower + 2**bit) * share]
-
-            def step(item, carry, bit=bit, level=level, blocks=blocks, out_blocks=out_blocks, source=source, target=target, starts=starts):
-                for n in range(per_step):
-                    at = (item * per_step + n) * SUBLANES
-                    spots = [pl.ds(pl.multiple_of(start + at, SUBLANES), SUBLANES) for start in starts]
-                    for spot in spots:
-
-                        def put(j, value, spot=spot):
-                            target[spot, block_of(j)] = value
-
-                        add_delayed(
-                            lambda j: source[spots[0], block_of(j)],
-                            lambda j: source[spots[1], block_of(j)],
-                            put,
-                            spread[bit, spot, :],
-                            level,
-                            blocks,
-                            out_blocks,
-                        )
-                return carry
-
-            lax.fori_loop(0, tiles // per_step, step, 0)
-            if last:
-                for n in (mask, other):
-                    spot = pl.ds(pl.multiple_of(jnp.bitwise_xor(mine, n) * share, SUBLANES), share)
-                    stores.append(pltpu.make_async_copy(done.at[spot, :], outs[n], out_sem.at[n]))
-                    stores[-1].start()
+        target = done if bit == levels - 1 else target
+
+        def step(
+            item, carry, bit=bit, level=level, blocks=blocks, out_blocks=out_blocks, source=source, target=target
+        ):
+            for n in range(per_step):
+                pair, tile = (item * per_step + n) // tiles, (item * per_step + n) % tiles
+                first = (pair // 2**bit) * 2 * 2**bit + pair % 2**bit
+                spots = [
+                    pl.ds(
+                        pl.multiple_of((first + e * 2**bit) * share + tile * SUBLANES, SUBLANES),
+                        SUBLANES,
+                    )
+                    for e in range(2)
+                ]
+                for spot in spots:
+
+                    def put(j, value, spot=spot):
+                        target[spot, block_of(j)] = value
+
+                    add_delayed(
+                        lambda j: source[spots[0], block_of(j)],
+                        lambda j: source[spots[1], block_of(j)],
+                        put,
+                        spread[bit, spot, :],
+                        level,
+                        blocks,
+                        out_blocks,
+                    )
+            return carry
+
+        lax.fori_loop(0, items // per_step, step, 0)
         blocks = out_blocks
+    stores = [
+        pltpu.make_async_copy(done.at[spot, :], target, out_sem.at[n])
+        for n, (target, spot) in enumerate(views(outs, group, mine, share))
+    ]
+    for store in stores:
+        store.start()
     for store in stores:
         store.wait()
 
 
-def cross_tree(position, table, rims, parts, masks, rows):
-    freq_count = len(parts)
-    share, span = parts[0].shape
-    total = span + rims[0].shape[2]
-    group = freq_count * share
+def cross_tree(position, table, parts, rim, rows, freq_count, base):
+    count = len(parts)
+    size, span = parts[0].shape
+    group = size * count
+    total = span + rim.shape[-1]
     hbm = pl.BlockSpec(memory_space=pl.ANY)
-    operands = [*rims, *parts]
     return pl.pallas_call(
-        functools.partial(cross_tree_kernel, rows, tuple(masks), len(rims)),
-        out_shape=[jax.ShapeDtypeStruct((share, span + LANES), jnp.float32)] * freq_count,
-        in_specs=[pl.BlockSpec(memory_space=pltpu.SMEM), pl.BlockSpec(memory_space=pltpu.VMEM)]
-        + [hbm] * len(operands),
-        out_specs=[hbm] * freq_count,
+        functools.partial(cross_tree_kernel, rows, freq_count, base, count),
+        out_shape=[jax.ShapeDtypeStruct((size, span + LANES), jnp.float32)] * count,
+        in_specs=[pl.BlockSpec(memory_space=pltpu.SMEM)] + [hbm] * (2 + count),
+        out_specs=[pl.BlockSpec(memory_space=pltpu.HBM if count == 1 else pl.ANY)] * count,
         scratch_shapes=[
             pltpu.VMEM((group, total), jnp.float32),
             pltpu.VMEM((group, total), jnp.float32),
             pltpu.VMEM((group, span + LANES), jnp.float32),
             pltpu.VMEM((freq_count.bit_length() - 1, group, LANES), jnp.int32),
-            pltpu.SemaphoreType.DMA((2, freq_count)),
-            pltpu.SemaphoreType.DMA((freq_count,)),
+            pltpu.VMEM((group, LANES), jnp.int32),
+            pltpu.SemaphoreType.DMA((freq_count + 2 * count,)),
+            pltpu.SemaphoreType.DMA((count,)),
         ],
-        compiler_params=pltpu.CompilerParams(vmem_limit_bytes=VMEM_LIMIT),
+        compiler_params=pltpu.CompilerParams(vmem_limit_bytes=CROSS_VMEM),
         cost_estimate=pl.CostEstimate(
             flops=4 * group * span, bytes_accessed=8 * group * span, transcendentals=0
         ),
         name="cross_tree",
-    )(position, table, *operands)
-
-
-def filter_kernel(masks, place, widths, scale, earlier, *refs):
-    count = len(masks)
-    parts = refs[:count]
+    )(position, table, rim, *parts)
+
+
+def filter_kernel(base, masks, place, widths, scale, earlier, *refs):
     out, mark, values, halves, before, whole, results, in_sem, out_sem = refs[-9:]
     mark[...] = jnp.zeros_like(mark)
-    share = parts[0].shape[0]
+    count, share = values.shape[:2]
+    if masks:
+        pieces = refs[:count]
+        starts = [jnp.bitwise_xor(place[0], mask) * share for mask in masks]
+    else:
+        pieces = [refs[0].at[pl.ds(n * share, share), :] for n in range(count)]
+        starts = [n * share for n in range(count)]
     blocks = out.shape[2] // LANES
     filters = out.shape[0]
-    mine = place[0]
-    loads = [pltpu.make_async_copy(parts[n], values.at[n], in_sem.at[n]) for n in range(count)]
+    loads = [pltpu.make_async_copy(pieces[n], values.at[n], in_sem.at[n]) for n in range(count)]
     for load in loads:
         load.start()
     row = lax.broadcasted_iota(jnp.int32, (2 * LANES, 2 * LANES), 0) & (LANES - 1)
@@ -317,7 +312,7 @@
     per_dot = max(n for n in (1, 2, 3, 4, 5, 6, 7) if (blocks + 1) % n == 0)
     lane = lax.broadcasted_iota(jnp.int32, (SUBLANES, LANES), 1)
     copies = {}
-    for n, mask in enumerate(masks):
+    for n in range(count):
         slot = n % 2
         loads[n].wait()
         for j in range(blocks + 1):
@@ -356,11 +351,10 @@
             return carry
 
         lax.fori_loop(0, filters * share // SUBLANES, step, 0, unroll=8)
-        start = pl.multiple_of(jnp.bitwise_xor(mine, mask) * share, SUBLANES)
         copies[n] = [
             pltpu.make_async_copy(
                 results.at[slot, which],
-                out.at[which, pl.ds(start, share), :],
+                out.at[which, pl.ds(pl.multiple_of(base + starts[n], SUBLANES), share), :],
                 out_sem.at[slot, which],
             )
             for which in range(filters)
@@ -372,11 +366,12 @@
             copy.wait()
 
 
-def box_filters(position, widths, scale, earlier, masks, parts, result, rows):
-    share, reach = parts[0].shape
+def box_filters(position, widths, scale, earlier, parts, masks, result, rows, base):
+    size, reach = parts[0].shape
+    share = size if masks else max(n for n in (16, 32) if size % n == 0)
+    count = len(parts) * size // share
     span = reach - LANES
     blocks = span // LANES
-    count = len(masks)
     filters = scale.shape[0]
     hbm = pl.BlockSpec(memory_space=pl.ANY)
     smem = pl.BlockSpec(memory_space=pltpu.SMEM)
@@ -386,7 +381,7 @@
         aliases = {len(operands): 0}
         operands.append(result)
     return pl.pallas_call(
-        functools.partial(filter_kernel, masks),
+        functools.partial(filter_kernel, base, tuple(masks)),
         out_shape=[
             jax.ShapeDtypeStruct((filters, rows, span), jnp.float32),
             jax.ShapeDtypeStruct((SUBLANES, LANES), jnp.float32),
@@ -403,7 +398,7 @@
             pltpu.SemaphoreType.DMA((count,)),
             pltpu.SemaphoreType.DMA((2, filters)),
         ],
-        compiler_params=pltpu.CompilerParams(vmem_limit_bytes=VMEM_LIMIT),
+        compiler_params=pltpu.CompilerParams(vmem_limit_bytes=FILTER_VMEM),
         cost_estimate=pl.CostEstimate(
             flops=8 * count * share * span * filters,
             bytes_accessed=4 * count * share * span * (filters + 1),
@@ -419,9 +414,21 @@
     return lax.ppermute(value, axis, [(source, source + steps) for source in range(initial, last)])
 
 
-def exchanged(part, mask, freq_count):
-    pairs = [(source, source ^ mask) for source in range(freq_count)]
-    return lax.ppermute(part, "freq", pairs)
+def exchanged(parts, freq_count):
+    if len(parts) == 1:
+        return [lax.all_to_all(parts[0], "freq", 0, 0, tiled=True)]
+    result = list(parts)
+    for mask in range(1, freq_count):
+        pairs = [(source, source ^ mask) for source in range(freq_count)]
+        result[mask] = lax.ppermute(parts[mask], "freq", pairs)
+    return result
+
+
+def chunks_of(rows, freq_count):
+    tiles = rows // freq_count // SUBLANES
+    first = tiles - max(1, int(tiles * LATER))
+    counts = [first * SUBLANES * freq_count, (tiles - first) * SUBLANES * freq_count]
+    return [(0, counts[0], freq_count), (counts[0], counts[1], 1)]
 
 
 def by_residues(spectra, delays, widths):
@@ -433,50 +440,28 @@
     rim = passed_along(spectra[:, :local_rim], "tm", -1)
     table = jnp.pad(delays.T, ((0, 0), (0, LANES - delays.shape[0])))
     scale = 1.0 / jnp.sqrt(widths.astype(jnp.float32) * channels)
+    reach = channels - rows + LANES
+    chunks = chunks_of(rows, freq_count)
+    made = local_tree(position, spectra, rim, table, chunks, freq_count)
+    arrived = []
+    for _, _, count in chunks:
+        arrived.append(exchanged(made[:count], freq_count))
+        made = made[count:]
+    back = []
+    for (base, _, count), parts in zip(chunks, arrived):
+        edges = [part[:, :reach] for part in parts]
+        rim = passed_along(jnp.stack(edges) if count > 1 else edges[0], "tm", -1)
+        back.append(cross_tree(position, table, parts, rim, rows, freq_count, base))
+    back = [exchanged(parts, freq_count) for parts in back]
+    result, mark = None, jnp.zeros((SUBLANES, LANES), jnp.float32)
     half = freq_count // 2
-    near, far = list(range(half)), list(range(half, freq_count))
-    early, late = far[: half // 2], far[half // 2 :]
-    sent = {}
-
-    def ready(value, *keys):
-        for key in keys:
-            value, sent[key] = lax.optimization_barrier((value, sent[key]))
-        return value
-
-    def swap(name, parts, masks, *keys):
-        sent[name, 0] = parts[0]
-        for mask in masks:
-            sent[name, mask] = exchanged(ready(parts[mask], *keys), mask, freq_count)
-
-    def leading(name, masks, length):
-        return passed_along(jnp.stack([sent[name, mask][:, :length] for mask in masks]), "tm", -1)
-
-    parts = local_tree(position, spectra, rim, table, freq_count)
-    name = "out"
-    swap(name, parts, early + near[1:])
-    for before, mask in zip(early, late):
-        swap(name, parts, [mask], (name, before))
-    rims = [leading(name, masks, channels - rows + LANES) for masks in (near, far)]
-    arrived = [sent[name, mask] for mask in near + far]
-    summed = cross_tree(position, table, rims, arrived, near + far, rows)
-    result = None
-    sent["mark"] = jnp.zeros((SUBLANES, LANES), jnp.float32)
-
-    def filters(name, masks):
-        nonlocal result
-        parts = [sent[name, mask] for mask in masks]
-        result, sent["mark"] = box_filters(
-            position, widths, scale, sent["mark"], masks, parts, result, rows
+    turns = [(0, range(half)), (1, ()), (0, range(half, freq_count))]
+    for chunk, masks in turns:
+        base, parts = chunks[chunk][0], back[chunk]
+        some = [parts[mask] for mask in masks] or parts
+        result, mark = box_filters(
+            position, widths, scale, mark, some, tuple(masks), result, rows, base
         )
-
-    name = "back"
-    swap(name, summed, early + near[1:])
-    filters(name, near[:1])
-    swap(name, summed, late[:1], "mark")
-    filters(name, near[1:])
-    swap(name, summed, late[1:], "mark")
-    filters(name, early)
-    filters(name, late)
     return result
 
 

time: 166 us -> 153 us (0.922)
  waiting for transfers between devices: 95.3 us -> 59.3 us
  starting transfers between devices: 23.7 us -> 37.3 us
  local copies, waits for them, and re-layouts: 3.43 us -> 12.2 us
    ppermute x14, waiting for transfers between devices: 91.6 us -> 43.1 us  [exchanged(): result[mask] = lax.ppermute(parts[mask], 'freq', pairs)]
    all_to_all x0 -> x2, starting transfers between devices: none -> 12.8 us  [exchanged(): return [lax.all_to_all(parts[0], 'freq', 0, 0, tiled=True)]]
    all_to_all x0 -> x2, waiting for transfers between devices: none -> 12.8 us  [exchanged(): return [lax.all_to_all(parts[0], 'freq', 0, 0, tiled=True)]]
    unnamed x9 -> x18, local copies, waits for them, and re-layouts: 2.23 us -> 8.57 us
  transfers between devices with their start and end apart: 17 -> 19, of which waited for: 11 -> 12; matrix products, arithmetic and copies ran while one was open for 1% -> 6% of each run, Pallas kernels for 9% -> 16%
where the time goes in v3:
time: 153 us
  waiting for transfers between devices  59.3 us (39%)
  Pallas kernels  43.6 us (28%)
  starting transfers between devices  37.3 us (24%)
  local copies, waits for them, and re-layouts  12.2 us (8%)
    ppermute x14, waiting for transfers between devices, exchanged(): result[mask] = lax.ppermute(parts[mask], 'freq', pairs)  43.1 us
    ppermute x14, starting transfers between devices, exchanged(): result[mask] = lax.ppermute(parts[mask], 'freq', pairs)  20.7 us
    pallas_call x3, Pallas kernels, box_filters(): pl.pallas_call(functools.partial(filter_kernel, base, tuple(masks)), out_...  20.4 us
    pallas_call x1, Pallas kernels, local_tree(): pl.pallas_call(functools.partial(local_tree_kernel, tuple(chunks), freq_c...  13.1 us
    all_to_all x2, starting transfers between devices, exchanged(): return [lax.all_to_all(parts[0], 'freq', 0, 0, tiled=True)]  12.8 us
    all_to_all x2, waiting for transfers between devices, exchanged(): return [lax.all_to_all(parts[0], 'freq', 0, 0, tiled=True)]  12.8 us
    pallas_call x2, Pallas kernels, cross_tree(): pl.pallas_call(functools.partial(cross_tree_kernel, rows, freq_count, bas...  10.1 us
    unnamed x18, local copies, waits for them, and re-layouts  8.57 us
  transfers between devices with their start and end apart: 19, of which 12 were waited for; matrix products, arithmetic and copies ran while one was open for 6% of the time, Pallas kernels for 16%

profile of v3, /device:TPU:10, one launch (start us, length us, event | category | flops | bytes accessed | tf_op | source)
XLA Modules:
  0.0 152.6 jit_solution(3384748985205233392)
XLA Ops:
  5.3 13.1 %local_tree.1 = (f32[16,2560]{1,0:T(8,128)}, f32[16,2560]{1,0:T(8,128)}, f32[16,2560]{1,0:T(8,128)}, f32[16,2560]{1,0:T(8,128)}, f32[16,2560]{1,0:T(8,128)}, /*i...) custom-call(s32[1]{0:T(128)} %bitcast.place, f32[256,2560]{1,0:T(8,128)} %spectra.1, ...), custom_call_target="tpu_custom_call" | custom-call | flops 5242880 | bytes 5242880 | tf_op jit(solution)/shard_map/local_tree/pallas_call | solution.py:159
  18.5 6.4 %all-to-all-start = ((f32[8,16,2560]{2,1,0:T(8,128)}), f32[8,16,2560]{2,1,0:T(8,128)S(1)}, u32[]{:S(2)}, u32[]{:S(2)}) async-start(f32[8,16,2560]{2,1,0:T(8,128)} %bitcast.41), calls=%async_computation | async-start | bytes 2621440 | tf_op jit(solution)/shard_map/all_to_all | solution.py:419
  24.9 1.5 collective-permute-start.1
  26.9 1.5 collective-permute-start.3
  28.4 2.4 %collective-permute-start.4 = (f32[16,2560]{1,0:T(8,128)}, f32[16,2560]{1,0:T(8,128)S(1)}, u32[]{:S(2)}, u32[]{:S(2)}) collective-permute-start(f32[16,2560]{1,0:T(8,128)} %get-tuple-element.31), channel_id=1, source_target_pairs={{0,8},{2,10},{4,12},{6,14},{8,0},{10,2},{12,4},{14,6},{1,9},{3,11}... | collective-permute-start | bytes 491528 | tf_op jit(solution)/shard_map/ppermute | solution.py:423
  30.7 1.5 collective-permute-start.5
  32.9 7.3 %collective-permute-done.1.refs_1_ = f32[16,2560]{1,0:T(8,128)S(1)} collective-permute-done((f32[16,2560]{1,0:T(8,128)}, f32[16,2560]{1,0:T(8,128)S(1)}, u32[]{:S(2)}, u32[]{:S(2)}) %collective-permute-start.1) | collective-permute-done | bytes 163872 | tf_op jit(solution)/shard_map/ppermute | solution.py:423
  40.2 1.5 collective-permute-start.6
  42.3 12.8 %all-to-all-done = f32[8,16,2560]{2,1,0:T(8,128)S(1)} async-done(((f32[8,16,2560]{2,1,0:T(8,128)}), f32[8,16,2560]{2,1,0:T(8,128)S(1)}, u32[]{:S(2)}, u32[]{:S(2)}) %all-to-all-start) | async-done | bytes 1310752 | tf_op jit(solution)/shard_map/all_to_all | solution.py:419
  57.3 1.7 %collective-permute-start.7 = (f32[16,2560]{1,0:T(8,128)}, f32[16,2560]{1,0:T(8,128)}, u32[]{:S(2)}, u32[]{:S(2)}) collective-permute-start(f32[16,2560]{1,0:T(8,128)} %get-tuple-element.34), channel_id=1, source_target_pairs={{0,14},{2,12},{4,10},{6,8},{8,6},{10,4},{12,2},{14,0},{1,15},{3,13... | collective-permute-start | bytes 491528 | tf_op jit(solution)/shard_map/ppermute | solution.py:423
  59.6 13.0 %collective-permute-done.4.refs_4_ = f32[16,2560]{1,0:T(8,128)S(1)} collective-permute-done((f32[16,2560]{1,0:T(8,128)}, f32[16,2560]{1,0:T(8,128)S(1)}, u32[]{:S(2)}, u32[]{:S(2)}) %collective-permute-start.4) | collective-permute-done | bytes 163872 | tf_op jit(solution)/shard_map/ppermute | solution.py:423
  73.3 3.4 %cross_tree.3 = f32[128,2688]{1,0:T(8,128)S(1)} custom-call(s32[1]{0:T(128)} %bitcast.place, s32[2048,128]{1,0:T(8,128)S(1)} %copy-done, f32[128,1920]{1,0:T(8,128)S(1)} %collective-permute-done.12.rim, f32[128,2560]{1,0:T(8,128)S(1)} %bitcast.37), custom_call_target="tpu_custom_call" | custom-call | flops 1310720 | bytes 2621440 | tf_op jit(solution)/shard_map/cross_tree/pallas_call | solution.py:272
  77.9 6.4 %all-to-all-start.1 = ((f32[8,16,2688]{2,1,0:T(8,128)}), f32[8,16,2688]{2,1,0:T(8,128)S(1)}, u32[]{:S(2)}, u32[]{:S(2)}) async-start(f32[8,16,2688]{2,1,0:T(8,128)} %bitcast.38), calls=%async_computation.1 | async-start | bytes 2752512 | tf_op jit(solution)/shard_map/all_to_all | solution.py:419
  84.9 1.5 %fusion.1 = f32[8,16,1920]{2,1,0:T(8,128)} fusion(f32[8,16,1920]{2,1,0:T(8,128)} %fusion.2, f32[16,2560]{1,0:T(8,128)} %collective-permute-done.6.refs_6_), kind=kLoop, calls=%fused_computation.3 | loop fusion | bytes 245760
  86.5 1.6 %fusion = f32[8,16,1920]{2,1,0:T(8,128)} fusion(f32[8,16,1920]{2,1,0:T(8,128)} %fusion.1, f32[16,2560]{1,0:T(8,128)} %collective-permute-done.7.refs_7_), kind=kLoop, calls=%fused_computation.1 | loop fusion | bytes 245760 | tf_op jit(solution)/shard_map/stack | solution.py:453
  89.3 3.4 %collective-permute-done.8.rim = f32[8,16,1920]{2,1,0:T(8,128)S(1)} collective-permute-done((f32[8,16,1920]{2,1,0:T(8,128)}, f32[8,16,1920]{2,1,0:T(8,128)S(1)}, u32[]{:S(2)}, u32[]{:S(2)}) %collective-permute-start.8) | collective-permute-done | bytes 983072 | tf_op jit(solution)/shard_map/ppermute | solution.py:414
  92.7 6.6 %cross_tree.2 = (f32[16,2688]{1,0:T(8,128)S(1)}, f32[16,2688]{1,0:T(8,128)S(1)}, f32[16,2688]{1,0:T(8,128)S(1)}, f32[16,2688]{1,0:T(8,128)S(1)}, f32[16,2688]{1,...) custom-call(s32[1]{0:T(128)} %bitcast.place, s32[2048,128]{1,0:T(8,128)S(1)} %copy-done, ...), custom_call_target="tpu_custom_call" | custom-call | flops 1310720 | bytes 2621440 | tf_op jit(solution)/shard_map/cross_tree/pallas_call | solution.py:272
  99.3 1.5 %collective-permute-start.9 = (f32[16,2688]{1,0:T(8,128)S(1)}, f32[16,2688]{1,0:T(8,128)S(1)}, u32[]{:S(2)}, u32[]{:S(2)}) collective-permute-start(f32[16,2688]{1,0:T(8,128)S(1)} %get-tuple-element.36), channel_id=1, source_target_pairs={{0,2},{2,0},{4,6},{6,4},{8,10},{10,8},{12,14},{14,12},{1,3},{3,1},... | collective-permute-start | bytes 516104 | tf_op jit(solution)/shard_map/ppermute | solution.py:423
  101.4 1.5 collective-permute-start.11
  102.9 2.4 %collective-permute-start.13 = (f32[16,2688]{1,0:T(8,128)}, f32[16,2688]{1,0:T(8,128)S(1)}, u32[]{:S(2)}, u32[]{:S(2)}) collective-permute-start(f32[16,2688]{1,0:T(8,128)} %get-tuple-element.43), channel_id=1, source_target_pairs={{0,8},{2,10},{4,12},{6,14},{8,0},{10,2},{12,4},{14,6},{1,9},{3,11}... | collective-permute-start | bytes 516104 | tf_op jit(solution)/shard_map/ppermute | solution.py:423
  105.3 1.4 collective-permute-start.14
  106.7 2.4 %collective-permute-done.9.refs_1_ = f32[16,2688]{1,0:T(8,128)S(1)} collective-permute-done((f32[16,2688]{1,0:T(8,128)S(1)}, f32[16,2688]{1,0:T(8,128)S(1)}, u32[]{:S(2)}, u32[]{:S(2)}) %collective-permute-start.9) | collective-permute-done | bytes 172064 | tf_op jit(solution)/shard_map/ppermute | solution.py:423
  109.1 3.9 %collective-permute-done.10.refs_2_ = f32[16,2688]{1,0:T(8,128)S(1)} collective-permute-done((f32[16,2688]{1,0:T(8,128)S(1)}, f32[16,2688]{1,0:T(8,128)S(1)}, u32[]{:S(2)}, u32[]{:S(2)}) %collective-permute-start.10) | collective-permute-done | bytes 172064 | tf_op jit(solution)/shard_map/ppermute | solution.py:423
  112.9 2.8 %collective-permute-start.16 = (f32[16,2688]{1,0:T(8,128)}, f32[16,2688]{1,0:T(8,128)S(1)}, u32[]{:S(2)}, u32[]{:S(2)}) collective-permute-start(f32[16,2688]{1,0:T(8,128)} %get-tuple-element.46), channel_id=1, source_target_pairs={{0,14},{2,12},{4,10},{6,8},{8,6},{10,4},{12,2},{14,0},{1,15},{3,13... | collective-permute-start | bytes 516104 | tf_op jit(solution)/shard_map/ppermute | solution.py:423
  115.8 2.0 %collective-permute-done.11.refs_3_ = f32[16,2688]{1,0:T(8,128)S(1)} collective-permute-done((f32[16,2688]{1,0:T(8,128)S(1)}, f32[16,2688]{1,0:T(8,128)S(1)}, u32[]{:S(2)}, u32[]{:S(2)}) %collective-permute-start.11) | collective-permute-done | bytes 172064 | tf_op jit(solution)/shard_map/ppermute | solution.py:423
  117.7 5.7 %box_filters.3 = (f32[8,256,2560]{2,1,0:T(8,128)}, f32[8,128]{1,0:T(8,128)S(1)}) custom-call(s32[1]{0:T(128)} %bitcast.place, s32[8]{0:T(128)S(1)} %copy-done.3, f32[8]{0:T(128)S(1)} %multiply_rsqrt_fusion.scale, f32[8,128]{1,0:T(8,128)S(1)} %broadcast_in_dim.7.earlier, f32[16,2688]{1,0:T(8,128)S(1)} %get-tuple-element.35.refs_0_, ...), custom_call_target="tpu_custom_call" | custom-call | flops 10485760 | bytes 5898240 | tf_op jit(solution)/shard_map/box_filters/pallas_call | solution.py:383
  123.5 8.4 %box_filters.4 = (f32[8,256,2560]{2,1,0:T(8,128)}, f32[8,128]{1,0:T(8,128)S(1)}) custom-call(s32[1]{0:T(128)} %bitcast.place, s32[8]{0:T(128)S(1)} %copy-done.3, f32[8]{0:T(128)S(1)} %multiply_rsqrt_fusion.scale, f32[8,128]{1,0:T(8,128)S(1)} %get-tuple-element.39.earlier, f32[128,2688]{1,0:T(8,128)S(1)} %bitcast.39, ...), custom_call_target="tpu_custom_call", output_to_operand_aliasing={{0}: (5, {})} | custom-call | flops 20971520 | bytes 11796480 | tf_op jit(solution)/shard_map/box_filters/pallas_call | solution.py:383
  131.9 1.6 %collective-permute-done.13.refs_0_ = f32[16,2688]{1,0:T(8,128)S(1)} collective-permute-done((f32[16,2688]{1,0:T(8,128)}, f32[16,2688]{1,0:T(8,128)S(1)}, u32[]{:S(2)}, u32[]{:S(2)}) %collective-permute-start.13) | collective-permute-done | bytes 172064 | tf_op jit(solution)/shard_map/ppermute | solution.py:423
  133.5 3.7 %collective-permute-done.14.refs_1_ = f32[16,2688]{1,0:T(8,128)S(1)} collective-permute-done((f32[16,2688]{1,0:T(8,128)}, f32[16,2688]{1,0:T(8,128)S(1)}, u32[]{:S(2)}, u32[]{:S(2)}) %collective-permute-start.14) | collective-permute-done | bytes 172064 | tf_op jit(solution)/shard_map/ppermute | solution.py:423
  137.2 5.6 %collective-permute-done.15.refs_2_ = f32[16,2688]{1,0:T(8,128)S(1)} collective-permute-done((f32[16,2688]{1,0:T(8,128)}, f32[16,2688]{1,0:T(8,128)S(1)}, u32[]{:S(2)}, u32[]{:S(2)}) %collective-permute-start.15) | collective-permute-done | bytes 172064 | tf_op jit(solution)/shard_map/ppermute | solution.py:423
  142.8 3.5 %collective-permute-done.16.refs_3_ = f32[16,2688]{1,0:T(8,128)S(1)} collective-permute-done((f32[16,2688]{1,0:T(8,128)}, f32[16,2688]{1,0:T(8,128)S(1)}, u32[]{:S(2)}, u32[]{:S(2)}) %collective-permute-start.16) | collective-permute-done | bytes 172064 | tf_op jit(solution)/shard_map/ppermute | solution.py:423
  146.3 6.3 %box_filters.5 = (f32[8,256,2560]{2,1,0:T(8,128)}, f32[8,128]{1,0:T(8,128)}) custom-call(s32[1]{0:T(128)} %bitcast.place, s32[8]{0:T(128)S(1)} %copy-done.3, f32[8]{0:T(128)S(1)} %multiply_rsqrt_fusion.scale, f32[8,128]{1,0:T(8,128)S(1)} %get-tuple-element.42.earlier, ...), custom_call_target="tpu_custom_call", output_to_operand_aliasing={{0}: (8, {})} | custom-call | flops 10485760 | bytes 5898240 | tf_op jit(solution)/shard_map/box_filters/pallas_call | solution.py:383
  (36 shorter events, 14.3 us)
Async XLA Ops:
  1.0 3.6 %collective-permute-start = (f32[256,256]{1,0:T(8,128)S(1)}, f32[256,256]{1,0:T(8,128)S(1)}, u32[]{:S(2)}, u32[]{:S(2)}) collective-permute-start(f32[256,256]{1,0:T(8,128)S(1)} %slice.30), channel_id=1, source_target_pairs={{1,0},{3,2},{5,4},{7,6},{9,8},{11,10},{13,12},{15,14},{17,16},{19,... | collective-permute-start | bytes 786440 | tf_op jit(solution)/shard_map/ppermute | solution.py:414
  4.6 0.7 copy-start.4
  18.4 13.8 %copy-start.2 = (f32[16,2560]{1,0:T(8,128)S(1)}, f32[16,2560]{1,0:T(8,128)}, u32[]{:S(2)}) copy-start(f32[16,2560]{1,0:T(8,128)} %get-tuple-element.27.refs_0_) | copy-start | bytes 491524
  18.4 54.9 %copy-start = (s32[2048,128]{1,0:T(8,128)S(1)}, s32[2048,128]{1,0:T(8,128)}, u32[]{:S(2)}) copy-start(s32[2048,128]{1,0:T(8,128)} %pad.4.table) | copy-start | bytes 3145732
  18.5 36.7 %all-to-all-start = ((f32[8,16,2560]{2,1,0:T(8,128)}), f32[8,16,2560]{2,1,0:T(8,128)S(1)}, u32[]{:S(2)}, u32[]{:S(2)}) async-start(f32[8,16,2560]{2,1,0:T(8,128)} %bitcast.41), calls=%async_computation | async-start | bytes 2621440 | tf_op jit(solution)/shard_map/all_to_all | solution.py:419
  24.9 15.3 %collective-permute-start.1 = (f32[16,2560]{1,0:T(8,128)}, f32[16,2560]{1,0:T(8,128)S(1)}, u32[]{:S(2)}, u32[]{:S(2)}) collective-permute-start(f32[16,2560]{1,0:T(8,128)} %get-tuple-element.28), channel_id=1, source_target_pairs={{0,2},{2,0},{4,6},{6,4},{8,10},{10,8},{12,14},{14,12},{1,3},{3,1},... | collective-permute-start | bytes 491528 | tf_op jit(solution)/shard_map/ppermute | solution.py:423
  26.3 28.8 %collective-permute-start.2 = (f32[16,2560]{1,0:T(8,128)}, f32[16,2560]{1,0:T(8,128)S(1)}, u32[]{:S(2)}, u32[]{:S(2)}) collective-permute-start(f32[16,2560]{1,0:T(8,128)} %get-tuple-element.29), channel_id=1, source_target_pairs={{0,4},{2,6},{4,0},{6,2},{8,12},{10,14},{12,8},{14,10},{1,5},{3,7},... | collective-permute-start | bytes 491528 | tf_op jit(solution)/shard_map/ppermute | solution.py:423
  26.9 30.4 %collective-permute-start.3 = (f32[16,2560]{1,0:T(8,128)}, f32[16,2560]{1,0:T(8,128)S(1)}, u32[]{:S(2)}, u32[]{:S(2)}) collective-permute-start(f32[16,2560]{1,0:T(8,128)} %get-tuple-element.30), channel_id=1, source_target_pairs={{0,6},{2,4},{4,2},{6,0},{8,14},{10,12},{12,10},{14,8},{1,7},{3,5},... | collective-permute-start | bytes 491528 | tf_op jit(solution)/shard_map/ppermute | solution.py:423
  28.4 44.3 %collective-permute-start.4 = (f32[16,2560]{1,0:T(8,128)}, f32[16,2560]{1,0:T(8,128)S(1)}, u32[]{:S(2)}, u32[]{:S(2)}) collective-permute-start(f32[16,2560]{1,0:T(8,128)} %get-tuple-element.31), channel_id=1, source_target_pairs={{0,8},{2,10},{4,12},{6,14},{8,0},{10,2},{12,4},{14,6},{1,9},{3,11}... | collective-permute-start | bytes 491528 | tf_op jit(solution)/shard_map/ppermute | solution.py:423
  30.7 53.5 %collective-permute-start.5 = (f32[16,2560]{1,0:T(8,128)}, f32[16,2560]{1,0:T(8,128)S(1)}, u32[]{:S(2)}, u32[]{:S(2)}) collective-permute-start(f32[16,2560]{1,0:T(8,128)} %get-tuple-element.32), channel_id=1, source_target_pairs={{0,10},{2,8},{4,14},{6,12},{8,2},{10,0},{12,6},{14,4},{1,11},{3,9}... | collective-permute-start | bytes 491528 | tf_op jit(solution)/shard_map/ppermute | solution.py:423
  40.2 44.7 %collective-permute-start.6 = (f32[16,2560]{1,0:T(8,128)}, f32[16,2560]{1,0:T(8,128)}, u32[]{:S(2)}, u32[]{:S(2)}) collective-permute-start(f32[16,2560]{1,0:T(8,128)} %get-tuple-element.33), channel_id=1, source_target_pairs={{0,12},{2,14},{4,8},{6,10},{8,4},{10,6},{12,0},{14,2},{1,13},{3,15... | collective-permute-start | bytes 491528 | tf_op jit(solution)/shard_map/ppermute | solution.py:423
  55.2 18.1 %collective-permute-start.12 = (f32[128,1920]{1,0:T(8,128)S(1)}, f32[128,1920]{1,0:T(8,128)S(1)}, u32[]{:S(2)}, u32[]{:S(2)}) collective-permute-start(f32[128,1920]{1,0:T(8,128)S(1)} %slice.47), channel_id=1, source_target_pairs={{1,0},{3,2},{5,4},{7,6},{9,8},{11,10},{13,12},{15,14},{17,16},{19,... | collective-permute-start | bytes 2949128 | tf_op jit(solution)/shard_map/ppermute | solution.py:414
  57.3 29.2 %collective-permute-start.7 = (f32[16,2560]{1,0:T(8,128)}, f32[16,2560]{1,0:T(8,128)}, u32[]{:S(2)}, u32[]{:S(2)}) collective-permute-start(f32[16,2560]{1,0:T(8,128)} %get-tuple-element.34), channel_id=1, source_target_pairs={{0,14},{2,12},{4,10},{6,8},{8,6},{10,4},{12,2},{14,0},{1,15},{3,13... | collective-permute-start | bytes 491528 | tf_op jit(solution)/shard_map/ppermute | solution.py:423
  76.8 1.1 copy-start.1
  77.9 45.6 %all-to-all-start.1 = ((f32[8,16,2688]{2,1,0:T(8,128)}), f32[8,16,2688]{2,1,0:T(8,128)S(1)}, u32[]{:S(2)}, u32[]{:S(2)}) async-start(f32[8,16,2688]{2,1,0:T(8,128)} %bitcast.38), calls=%async_computation.1 | async-start | bytes 2752512 | tf_op jit(solution)/shard_map/all_to_all | solution.py:419
  84.3 31.5 %copy-start.3 = (s32[8]{0:T(128)S(1)}, s32[8]{0:T(128)}, u32[]{:S(2)}) copy-start(s32[8]{0:T(128)} %widths.5) | copy-start | bytes 100
  88.0 4.7 %collective-permute-start.8 = (f32[8,16,1920]{2,1,0:T(8,128)}, f32[8,16,1920]{2,1,0:T(8,128)S(1)}, u32[]{:S(2)}, u32[]{:S(2)}) collective-permute-start(f32[8,16,1920]{2,1,0:T(8,128)} %fusion), channel_id=1, source_target_pairs={{1,0},{3,2},{5,4},{7,6},{9,8},{11,10},{13,12},{15,14},{17,16},{19,... | collective-permute-start | bytes 2949128 | tf_op jit(solution)/shard_map/ppermute | solution.py:414
  99.3 9.8 %collective-permute-start.9 = (f32[16,2688]{1,0:T(8,128)S(1)}, f32[16,2688]{1,0:T(8,128)S(1)}, u32[]{:S(2)}, u32[]{:S(2)}) collective-permute-start(f32[16,2688]{1,0:T(8,128)S(1)} %get-tuple-element.36), channel_id=1, source_target_pairs={{0,2},{2,0},{4,6},{6,4},{8,10},{10,8},{12,14},{14,12},{1,3},{3,1},... | collective-permute-start | bytes 516104 | tf_op jit(solution)/shard_map/ppermute | solution.py:423
  100.9 12.1 %collective-permute-start.10 = (f32[16,2688]{1,0:T(8,128)S(1)}, f32[16,2688]{1,0:T(8,128)S(1)}, u32[]{:S(2)}, u32[]{:S(2)}) collective-permute-start(f32[16,2688]{1,0:T(8,128)S(1)} %get-tuple-element.37), channel_id=1, source_target_pairs={{0,4},{2,6},{4,0},{6,2},{8,12},{10,14},{12,8},{14,10},{1,5},{3,7},... | collective-permute-start | bytes 516104 | tf_op jit(solution)/shard_map/ppermute | solution.py:423
  101.4 16.3 %collective-permute-start.11 = (f32[16,2688]{1,0:T(8,128)S(1)}, f32[16,2688]{1,0:T(8,128)S(1)}, u32[]{:S(2)}, u32[]{:S(2)}) collective-permute-start(f32[16,2688]{1,0:T(8,128)S(1)} %get-tuple-element.38), channel_id=1, source_target_pairs={{0,6},{2,4},{4,2},{6,0},{8,14},{10,12},{12,10},{14,8},{1,7},{3,5},... | collective-permute-start | bytes 516104 | tf_op jit(solution)/shard_map/ppermute | solution.py:423
  102.9 30.6 %collective-permute-start.13 = (f32[16,2688]{1,0:T(8,128)}, f32[16,2688]{1,0:T(8,128)S(1)}, u32[]{:S(2)}, u32[]{:S(2)}) collective-permute-start(f32[16,2688]{1,0:T(8,128)} %get-tuple-element.43), channel_id=1, source_target_pairs={{0,8},{2,10},{4,12},{6,14},{8,0},{10,2},{12,4},{14,6},{1,9},{3,11}... | collective-permute-start | bytes 516104 | tf_op jit(solution)/shard_map/ppermute | solution.py:423
  105.3 31.9 %collective-permute-start.14 = (f32[16,2688]{1,0:T(8,128)}, f32[16,2688]{1,0:T(8,128)S(1)}, u32[]{:S(2)}, u32[]{:S(2)}) collective-permute-start(f32[16,2688]{1,0:T(8,128)} %get-tuple-element.44), channel_id=1, source_target_pairs={{0,10},{2,8},{4,14},{6,12},{8,2},{10,0},{12,6},{14,4},{1,11},{3,9}... | collective-permute-start | bytes 516104 | tf_op jit(solution)/shard_map/ppermute | solution.py:423
  109.1 33.8 %collective-permute-start.15 = (f32[16,2688]{1,0:T(8,128)}, f32[16,2688]{1,0:T(8,128)S(1)}, u32[]{:S(2)}, u32[]{:S(2)}) collective-permute-start(f32[16,2688]{1,0:T(8,128)} %get-tuple-element.45), channel_id=1, source_target_pairs={{0,12},{2,14},{4,8},{6,10},{8,4},{10,6},{12,0},{14,2},{1,13},{3,15... | collective-permute-start | bytes 516104 | tf_op jit(solution)/shard_map/ppermute | solution.py:423
  112.9 33.3 %collective-permute-start.16 = (f32[16,2688]{1,0:T(8,128)}, f32[16,2688]{1,0:T(8,128)S(1)}, u32[]{:S(2)}, u32[]{:S(2)}) collective-permute-start(f32[16,2688]{1,0:T(8,128)} %get-tuple-element.46), channel_id=1, source_target_pairs={{0,14},{2,12},{4,10},{6,8},{8,6},{10,4},{12,2},{14,0},{1,15},{3,13... | collective-permute-start | bytes 516104 | tf_op jit(solution)/shard_map/ppermute | solution.py:423

commit v4 on v3

--- a/solution.py
+++ b/solution.py
@@ -11,7 +11,7 @@
 SUBLANES = 8
 TAPS = 128
 LATER = 0.5
-LOCAL_VMEM, CROSS_VMEM, FILTER_VMEM = 60 * 2**20, 24 * 2**20, 16 * 2**20
+LOCAL_VMEM, CROSS_VMEM, FILTER_VMEM = 60 * 2**20, 24 * 2**20, 12 * 2**20
 
 
 def lane_gather(block, index):
@@ -97,7 +97,7 @@
     for load in loads:
         load.wait()
     pairs = rows // (2 * SUBLANES)
-    per_step = max(n for n in (1, 2, 4) if pairs % n == 0)
+    per_step = max(n for n in (1, 2, 4, 8) if pairs % n == 0)
     for level in range(levels):
         half = 2**level
         last = level == levels - 1
@@ -182,7 +182,7 @@
     )(position, spectra, rim, table)
 
 
-def cross_tree_kernel(rows, freq_count, base, count, place, table, rim, *refs):
+def cross_tree_kernel(rows, freq_count, count, place, table, rim, *refs):
     parts, outs, refs = refs[:count], refs[count : 2 * count], refs[2 * count :]
     even, odd, done, spread, held, in_sem, out_sem = refs
     group, span = even.shape[0], parts[0].shape[1]
@@ -190,14 +190,7 @@
     blocks = even.shape[1] // LANES
     mine = place[0]
     loads = []
-    for owner in range(freq_count):
-        start = pl.multiple_of(owner * rows + base + mine * share, SUBLANES)
-        spot = pl.ds(owner * share, share)
-        loads.append(
-            pltpu.make_async_copy(
-                table.at[pl.ds(start, share), :], held.at[spot, :], in_sem.at[owner]
-            )
-        )
+    loads.append(pltpu.make_async_copy(table, held, in_sem.at[0]))
     sources = [(0, pair) for pair in views(parts, group, mine, share)]
     edges = [rim] if count == 1 else [rim.at[n] for n in range(count)]
     sources += [(span, pair) for pair in views(edges, group, mine, share)]
@@ -206,13 +199,12 @@
         loads.append(pltpu.make_async_copy(source, target, in_sem.at[len(loads)]))
     for load in loads:
         load.start()
-    for load in loads[:freq_count]:
-        load.wait()
+    loads[0].wait()
     first_level = rows.bit_length() - 1
     levels = freq_count.bit_length() - 1
     tiles = share // SUBLANES
     spread_shifts(held, spread, freq_count * tiles, range(first_level, first_level + levels))
-    for load in loads[freq_count:]:
+    for load in loads[1:]:
         load.wait()
     items = freq_count // 2 * tiles
     per_step = 2 if items % 2 == 0 else 1
@@ -263,14 +255,14 @@
         store.wait()
 
 
-def cross_tree(position, table, parts, rim, rows, freq_count, base):
+def cross_tree(position, table, parts, rim, rows, freq_count):
     count = len(parts)
     size, span = parts[0].shape
     group = size * count
     total = span + rim.shape[-1]
     hbm = pl.BlockSpec(memory_space=pl.ANY)
     return pl.pallas_call(
-        functools.partial(cross_tree_kernel, rows, freq_count, base, count),
+        functools.partial(cross_tree_kernel, rows, freq_count, count),
         out_shape=[jax.ShapeDtypeStruct((size, span + LANES), jnp.float32)] * count,
         in_specs=[pl.BlockSpec(memory_space=pltpu.SMEM)] + [hbm] * (2 + count),
         out_specs=[pl.BlockSpec(memory_space=pltpu.HBM if count == 1 else pl.ANY)] * count,
@@ -280,7 +272,7 @@
             pltpu.VMEM((group, span + LANES), jnp.float32),
             pltpu.VMEM((freq_count.bit_length() - 1, group, LANES), jnp.int32),
             pltpu.VMEM((group, LANES), jnp.int32),
-            pltpu.SemaphoreType.DMA((freq_count + 2 * count,)),
+            pltpu.SemaphoreType.DMA((1 + 2 * count,)),
             pltpu.SemaphoreType.DMA((count,)),
         ],
         compiler_params=pltpu.CompilerParams(vmem_limit_bytes=CROSS_VMEM),
@@ -443,6 +435,13 @@
     reach = channels - rows + LANES
     chunks = chunks_of(rows, freq_count)
     made = local_tree(position, spectra, rim, table, chunks, freq_count)
+    tables = {}
+    for base, size, _ in chunks:
+        share = size // freq_count
+        mine = lax.dynamic_slice_in_dim(
+            table.reshape(freq_count, rows, LANES), base + position[0] * share, share, axis=1
+        )
+        tables[base] = mine.reshape(size, LANES)
     arrived = []
     for _, _, count in chunks:
         arrived.append(exchanged(made[:count], freq_count))
@@ -451,11 +450,12 @@
     for (base, _, count), parts in zip(chunks, arrived):
         edges = [part[:, :reach] for part in parts]
         rim = passed_along(jnp.stack(edges) if count > 1 else edges[0], "tm", -1)
-        back.append(cross_tree(position, table, parts, rim, rows, freq_count, base))
+        back.append(cross_tree(position, tables[base], parts, rim, rows, freq_count))
     back = [exchanged(parts, freq_count) for parts in back]
     result, mark = None, jnp.zeros((SUBLANES, LANES), jnp.float32)
     half = freq_count // 2
-    turns = [(0, range(half)), (1, ()), (0, range(half, freq_count))]
+    turns = [(0, range(half)), (1, ()), (0, range(half, freq_count - 2))]
+    turns += [(0, (mask,)) for mask in range(freq_count - 2, freq_count)]
     for chunk, masks in turns:
         base, parts = chunks[chunk][0], back[chunk]
         some = [parts[mask] for mask in masks] or parts

time: 153 us -> 151 us (0.987); the launches traced: 153 us -> 148 us
  waiting for transfers between devices: 59.3 us -> 51.4 us
  Pallas kernels: 43.6 us -> 46.9 us
    ppermute x14, waiting for transfers between devices: 43.1 us -> 35.4 us  [exchanged(): result[mask] = lax.ppermute(parts[mask], 'freq', pairs)]
    pallas_call x3 -> x5, Pallas kernels: 20.4 us -> 23.8 us  [box_filters(): pl.pallas_call(functools.partial(filter_kernel, base, tuple(masks)), out_...]
    unnamed x18 -> x14, local copies, waits for them, and re-layouts: 8.57 us -> 8.39 us
  transfers between devices with their start and end apart: 19 -> 19, of which waited for: 12 -> 12; matrix products, arithmetic and copies ran while one was open for 6% -> 6% of each run, Pallas kernels for 16% -> 21%
where the time goes in v4:
time: 151 us; the launch traced here: 148 us
  waiting for transfers between devices  51.4 us (34%)
  Pallas kernels  46.9 us (31%)
  starting transfers between devices  37.5 us (25%)
  local copies, waits for them, and re-layouts  12.1 us (8%)
    ppermute x14, waiting for transfers between devices, exchanged(): result[mask] = lax.ppermute(parts[mask], 'freq', pairs)  35.4 us
    pallas_call x5, Pallas kernels, box_filters(): pl.pallas_call(functools.partial(filter_kernel, base, tuple(masks)), out_...  23.8 us
    ppermute x14, starting transfers between devices, exchanged(): result[mask] = lax.ppermute(parts[mask], 'freq', pairs)  20.8 us
    all_to_all x2, waiting for transfers between devices, exchanged(): return [lax.all_to_all(parts[0], 'freq', 0, 0, tiled=True)]  12.8 us
    all_to_all x2, starting transfers between devices, exchanged(): return [lax.all_to_all(parts[0], 'freq', 0, 0, tiled=True)]  12.7 us
    pallas_call x1, Pallas kernels, local_tree(): pl.pallas_call(functools.partial(local_tree_kernel, tuple(chunks), freq_c...  11.9 us
    pallas_call x2, Pallas kernels, cross_tree(): pl.pallas_call(functools.partial(cross_tree_kernel, rows, freq_count, cou...  11.2 us
    unnamed x14, local copies, waits for them, and re-layouts  8.39 us
  transfers between devices with their start and end apart: 19, of which 12 were waited for; matrix products, arithmetic and copies ran while one was open for 6% of the time, Pallas kernels for 21%

profile of v4, /device:TPU:10, one launch (start us, length us, event | category | flops | bytes accessed | tf_op | source)
XLA Modules:
  0.0 148.1 jit_solution(1028611268833648092)
XLA Ops:
  5.3 11.9 %local_tree.1 = (f32[16,2560]{1,0:T(8,128)}, f32[16,2560]{1,0:T(8,128)}, f32[16,2560]{1,0:T(8,128)}, f32[16,2560]{1,0:T(8,128)}, f32[16,2560]{1,0:T(8,128)}, /*i...) custom-call(s32[1]{0:T(128)} %bitcast.place, f32[256,2560]{1,0:T(8,128)} %spectra.1, ...), custom_call_target="tpu_custom_call" | custom-call | flops 5242880 | bytes 5242880 | tf_op jit(solution)/shard_map/local_tree/pallas_call | solution.py:159
  17.2 6.3 %all-to-all-start = ((f32[8,16,2560]{2,1,0:T(8,128)}), f32[8,16,2560]{2,1,0:T(8,128)S(1)}, u32[]{:S(2)}, u32[]{:S(2)}) async-start(f32[8,16,2560]{2,1,0:T(8,128)} %bitcast.46), calls=%async_computation | async-start | bytes 2621440 | tf_op jit(solution)/shard_map/all_to_all | solution.py:411
  24.4 1.5 %collective-permute-start.1 = (f32[16,2560]{1,0:T(8,128)}, f32[16,2560]{1,0:T(8,128)S(1)}, u32[]{:S(2)}, u32[]{:S(2)}) collective-permute-start(f32[16,2560]{1,0:T(8,128)} %get-tuple-element.32), channel_id=1, source_target_pairs={{0,2},{2,0},{4,6},{6,4},{8,10},{10,8},{12,14},{14,12},{1,3},{3,1},... | collective-permute-start | bytes 491528 | tf_op jit(solution)/shard_map/ppermute | solution.py:415
  26.5 1.5 collective-permute-start.3
  28.0 2.4 %collective-permute-start.4 = (f32[16,2560]{1,0:T(8,128)}, f32[16,2560]{1,0:T(8,128)S(1)}, u32[]{:S(2)}, u32[]{:S(2)}) collective-permute-start(f32[16,2560]{1,0:T(8,128)} %get-tuple-element.35), channel_id=1, source_target_pairs={{0,8},{2,10},{4,12},{6,14},{8,0},{10,2},{12,4},{14,6},{1,9},{3,11}... | collective-permute-start | bytes 491528 | tf_op jit(solution)/shard_map/ppermute | solution.py:415
  30.3 1.5 collective-permute-start.5
  31.8 1.6 %bitcast_dynamic-update-slice_fusion = f32[8,16,1920]{2,1,0:T(8,128)} fusion(f32[16,2560]{1,0:T(8,128)} %get-tuple-element.31.refs_0_), kind=kLoop, calls=%fused_computation.14 | loop fusion | bytes 245760
  33.4 5.5 %collective-permute-done.1.refs_1_ = f32[16,2560]{1,0:T(8,128)S(1)} collective-permute-done((f32[16,2560]{1,0:T(8,128)}, f32[16,2560]{1,0:T(8,128)S(1)}, u32[]{:S(2)}, u32[]{:S(2)}) %collective-permute-start.1) | collective-permute-done | bytes 163872 | tf_op jit(solution)/shard_map/ppermute | solution.py:415
  38.9 1.5 collective-permute-start.6
  41.0 12.8 %all-to-all-done = f32[8,16,2560]{2,1,0:T(8,128)S(1)} async-done(((f32[8,16,2560]{2,1,0:T(8,128)}), f32[8,16,2560]{2,1,0:T(8,128)S(1)}, u32[]{:S(2)}, u32[]{:S(2)}) %all-to-all-start) | async-done | bytes 1310752 | tf_op jit(solution)/shard_map/all_to_all | solution.py:411
  56.0 1.7 %collective-permute-start.7 = (f32[16,2560]{1,0:T(8,128)}, f32[16,2560]{1,0:T(8,128)S(1)}, u32[]{:S(2)}, u32[]{:S(2)}) collective-permute-start(f32[16,2560]{1,0:T(8,128)} %get-tuple-element.38), channel_id=1, source_target_pairs={{0,14},{2,12},{4,10},{6,8},{8,6},{10,4},{12,2},{14,0},{1,15},{3,13... | collective-permute-start | bytes 491528 | tf_op jit(solution)/shard_map/ppermute | solution.py:415
  58.3 13.0 %collective-permute-done.4.refs_4_ = f32[16,2560]{1,0:T(8,128)S(1)} collective-permute-done((f32[16,2560]{1,0:T(8,128)}, f32[16,2560]{1,0:T(8,128)S(1)}, u32[]{:S(2)}, u32[]{:S(2)}) %collective-permute-start.4) | collective-permute-done | bytes 163872 | tf_op jit(solution)/shard_map/ppermute | solution.py:415
  72.0 4.3 %cross_tree.3 = f32[128,2688]{1,0:T(8,128)} custom-call(s32[1]{0:T(128)} %bitcast.place, s32[128,128]{1,0:T(8,128)S(1)} %bitcast.42, f32[128,1920]{1,0:T(8,128)S(1)} %collective-permute-done.12.rim, f32[128,2560]{1,0:T(8,128)S(1)} %bitcast.40), custom_call_target="tpu_custom_call" | custom-call | flops 1310720 | bytes 2621440 | tf_op jit(solution)/shard_map/cross_tree/pallas_call | solution.py:264
  76.3 6.4 %all-to-all-start.1 = ((f32[8,16,2688]{2,1,0:T(8,128)}), f32[8,16,2688]{2,1,0:T(8,128)S(1)}, u32[]{:S(2)}, u32[]{:S(2)}) async-start(f32[8,16,2688]{2,1,0:T(8,128)} %bitcast.15), calls=%async_computation.1 | async-start | bytes 2752512 | tf_op jit(solution)/shard_map/all_to_all | solution.py:411
  84.7 1.5 collective-permute-start.8
  86.1 3.2 %collective-permute-done.8.rim = f32[8,16,1920]{2,1,0:T(8,128)S(1)} collective-permute-done((f32[8,16,1920]{2,1,0:T(8,128)}, f32[8,16,1920]{2,1,0:T(8,128)S(1)}, u32[]{:S(2)}, u32[]{:S(2)}) %collective-permute-start.8) | collective-permute-done | bytes 983072 | tf_op jit(solution)/shard_map/ppermute | solution.py:406
  90.2 6.9 %cross_tree.2 = (f32[16,2688]{1,0:T(8,128)S(1)}, f32[16,2688]{1,0:T(8,128)S(1)}, f32[16,2688]{1,0:T(8,128)S(1)}, f32[16,2688]{1,0:T(8,128)S(1)}, f32[16,2688]{1,...) custom-call(s32[1]{0:T(128)} %bitcast.place, s32[128,128]{1,0:T(8,128)S(1)} %bitcast.43, ...), custom_call_target="tpu_custom_call" | custom-call | flops 1310720 | bytes 2621440 | tf_op jit(solution)/shard_map/cross_tree/pallas_call | solution.py:264
  97.2 1.5 %collective-permute-start.9 = (f32[16,2688]{1,0:T(8,128)S(1)}, f32[16,2688]{1,0:T(8,128)S(1)}, u32[]{:S(2)}, u32[]{:S(2)}) collective-permute-start(f32[16,2688]{1,0:T(8,128)S(1)} %get-tuple-element.40), channel_id=1, source_target_pairs={{0,2},{2,0},{4,6},{6,4},{8,10},{10,8},{12,14},{14,12},{1,3},{3,1},... | collective-permute-start | bytes 516104 | tf_op jit(solution)/shard_map/ppermute | solution.py:415
  99.3 1.5 collective-permute-start.11
  100.7 2.4 %collective-permute-start.13 = (f32[16,2688]{1,0:T(8,128)S(1)}, f32[16,2688]{1,0:T(8,128)S(1)}, u32[]{:S(2)}, u32[]{:S(2)}) collective-permute-start(f32[16,2688]{1,0:T(8,128)S(1)} %get-tuple-element.47), channel_id=1, source_target_pairs={{0,8},{2,10},{4,12},{6,14},{8,0},{10,2},{12,4},{14,6},{1,9},{3,11}... | collective-permute-start | bytes 516104 | tf_op jit(solution)/shard_map/ppermute | solution.py:415
  104.6 2.9 %collective-permute-done.9.refs_1_ = f32[16,2688]{1,0:T(8,128)S(1)} collective-permute-done((f32[16,2688]{1,0:T(8,128)S(1)}, f32[16,2688]{1,0:T(8,128)S(1)}, u32[]{:S(2)}, u32[]{:S(2)}) %collective-permute-start.9) | collective-permute-done | bytes 172064 | tf_op jit(solution)/shard_map/ppermute | solution.py:415
  107.5 3.8 %collective-permute-done.10.refs_2_ = f32[16,2688]{1,0:T(8,128)S(1)} collective-permute-done((f32[16,2688]{1,0:T(8,128)S(1)}, f32[16,2688]{1,0:T(8,128)S(1)}, u32[]{:S(2)}, u32[]{:S(2)}) %collective-permute-start.10) | collective-permute-done | bytes 172064 | tf_op jit(solution)/shard_map/ppermute | solution.py:415
  111.3 2.9 %collective-permute-start.16 = (f32[16,2688]{1,0:T(8,128)S(1)}, f32[16,2688]{1,0:T(8,128)S(1)}, u32[]{:S(2)}, u32[]{:S(2)}) collective-permute-start(f32[16,2688]{1,0:T(8,128)S(1)} %get-tuple-element.54), channel_id=1, source_target_pairs={{0,14},{2,12},{4,10},{6,8},{8,6},{10,4},{12,2},{14,0},{1,15},{3,13... | collective-permute-start | bytes 516104 | tf_op jit(solution)/shard_map/ppermute | solution.py:415
  114.2 1.9 %collective-permute-done.11.refs_3_ = f32[16,2688]{1,0:T(8,128)S(1)} collective-permute-done((f32[16,2688]{1,0:T(8,128)S(1)}, f32[16,2688]{1,0:T(8,128)S(1)}, u32[]{:S(2)}, u32[]{:S(2)}) %collective-permute-start.11) | collective-permute-done | bytes 172064 | tf_op jit(solution)/shard_map/ppermute | solution.py:415
  116.1 5.7 %box_filters.5 = (f32[8,256,2560]{2,1,0:T(8,128)}, f32[8,128]{1,0:T(8,128)S(1)}) custom-call(s32[1]{0:T(128)} %bitcast.place, s32[8]{0:T(128)S(1)} %copy-done.1, f32[8]{0:T(128)S(1)} %multiply_rsqrt_fusion.scale, f32[8,128]{1,0:T(8,128)S(1)} %broadcast_in_dim.7.earlier, f32[16,2688]{1,0:T(8,128)S(1)} %get-tuple-element.39.refs_0_, ...), custom_call_target="tpu_custom_call" | custom-call | flops 10485760 | bytes 5898240 | tf_op jit(solution)/shard_map/box_filters/pallas_call | solution.py:375
  121.8 8.4 %box_filters.6 = (f32[8,256,2560]{2,1,0:T(8,128)}, f32[8,128]{1,0:T(8,128)S(1)}) custom-call(s32[1]{0:T(128)} %bitcast.place, s32[8]{0:T(128)S(1)} %copy-done.1, f32[8]{0:T(128)S(1)} %multiply_rsqrt_fusion.scale, f32[8,128]{1,0:T(8,128)S(1)} %get-tuple-element.43.earlier, f32[128,2688]{1,0:T(8,128)S(1)} %bitcast.41, ...), custom_call_target="tpu_custom_call", output_to_operand_aliasing={{0}: (5, {})} | custom-call | flops 20971520 | bytes 11796480 | tf_op jit(solution)/shard_map/box_filters/pallas_call | solution.py:375
  130.3 1.5 %collective-permute-done.13.refs_0_ = f32[16,2688]{1,0:T(8,128)S(1)} collective-permute-done((f32[16,2688]{1,0:T(8,128)S(1)}, f32[16,2688]{1,0:T(8,128)S(1)}, u32[]{:S(2)}, u32[]{:S(2)}) %collective-permute-start.13) | collective-permute-done | bytes 172064 | tf_op jit(solution)/shard_map/ppermute | solution.py:415
  131.8 3.7 %collective-permute-done.14.refs_1_ = f32[16,2688]{1,0:T(8,128)S(1)} collective-permute-done((f32[16,2688]{1,0:T(8,128)S(1)}, f32[16,2688]{1,0:T(8,128)S(1)}, u32[]{:S(2)}, u32[]{:S(2)}) %collective-permute-start.14) | collective-permute-done | bytes 172064 | tf_op jit(solution)/shard_map/ppermute | solution.py:415
  135.5 3.7 %box_filters.7 = (f32[8,256,2560]{2,1,0:T(8,128)}, f32[8,128]{1,0:T(8,128)S(1)}) custom-call(s32[1]{0:T(128)} %bitcast.place, s32[8]{0:T(128)S(1)} %copy-done.1, f32[8]{0:T(128)S(1)} %multiply_rsqrt_fusion.scale, f32[8,128]{1,0:T(8,128)S(1)} %get-tuple-element.46.earlier, ...), custom_call_target="tpu_custom_call", output_to_operand_aliasing={{0}: (6, {})} | custom-call | flops 5242880 | bytes 2949120 | tf_op jit(solution)/shard_map/box_filters/pallas_call | solution.py:375
  139.2 2.0 %collective-permute-done.15.refs_0_ = f32[16,2688]{1,0:T(8,128)S(1)} collective-permute-done((f32[16,2688]{1,0:T(8,128)S(1)}, f32[16,2688]{1,0:T(8,128)S(1)}, u32[]{:S(2)}, u32[]{:S(2)}) %collective-permute-start.15) | collective-permute-done | bytes 172064 | tf_op jit(solution)/shard_map/ppermute | solution.py:415
  141.2 2.7 %box_filters.8 = (f32[8,256,2560]{2,1,0:T(8,128)}, f32[8,128]{1,0:T(8,128)S(1)}) custom-call(s32[1]{0:T(128)} %bitcast.place, s32[8]{0:T(128)S(1)} %copy-done.1, f32[8]{0:T(128)S(1)} %multiply_rsqrt_fusion.scale, f32[8,128]{1,0:T(8,128)S(1)} %get-tuple-element.50.earlier, ...), custom_call_target="tpu_custom_call", output_to_operand_aliasing={{0}: (5, {})} | custom-call | flops 2621440 | bytes 1474560 | tf_op jit(solution)/shard_map/box_filters/pallas_call | solution.py:375
  144.7 3.3 %box_filters.9 = (f32[8,256,2560]{2,1,0:T(8,128)}, f32[8,128]{1,0:T(8,128)}) custom-call(s32[1]{0:T(128)} %bitcast.place, s32[8]{0:T(128)S(1)} %copy-done.1, f32[8]{0:T(128)S(1)} %multiply_rsqrt_fusion.scale, f32[8,128]{1,0:T(8,128)S(1)} %get-tuple-element.53.earlier, ...), custom_call_target="tpu_custom_call", output_to_operand_aliasing={{0}: (5, {})} | custom-call | flops 2621440 | bytes 1474560 | tf_op jit(solution)/shard_map/box_filters/pallas_call | solution.py:375
  (35 shorter events, 16.6 us)
Async XLA Ops:
  0.0 114.2 %copy-start.1 = (s32[8]{0:T(128)S(1)}, s32[8]{0:T(128)}, u32[]{:S(2)}) copy-start(s32[8]{0:T(128)} %widths.9) | copy-start | bytes 100
  1.0 3.6 %collective-permute-start = (f32[256,256]{1,0:T(8,128)S(1)}, f32[256,256]{1,0:T(8,128)S(1)}, u32[]{:S(2)}, u32[]{:S(2)}) collective-permute-start(f32[256,256]{1,0:T(8,128)S(1)} %slice.30), channel_id=1, source_target_pairs={{1,0},{3,2},{5,4},{7,6},{9,8},{11,10},{13,12},{15,14},{17,16},{19,... | collective-permute-start | bytes 786440 | tf_op jit(solution)/shard_map/ppermute | solution.py:406
  4.6 0.7 copy-start.2
  17.2 36.5 %all-to-all-start = ((f32[8,16,2560]{2,1,0:T(8,128)}), f32[8,16,2560]{2,1,0:T(8,128)S(1)}, u32[]{:S(2)}, u32[]{:S(2)}) async-start(f32[8,16,2560]{2,1,0:T(8,128)} %bitcast.46), calls=%async_computation | async-start | bytes 2621440 | tf_op jit(solution)/shard_map/all_to_all | solution.py:411
  24.4 14.4 %collective-permute-start.1 = (f32[16,2560]{1,0:T(8,128)}, f32[16,2560]{1,0:T(8,128)S(1)}, u32[]{:S(2)}, u32[]{:S(2)}) collective-permute-start(f32[16,2560]{1,0:T(8,128)} %get-tuple-element.32), channel_id=1, source_target_pairs={{0,2},{2,0},{4,6},{6,4},{8,10},{10,8},{12,14},{14,12},{1,3},{3,1},... | collective-permute-start | bytes 491528 | tf_op jit(solution)/shard_map/ppermute | solution.py:415
  26.0 27.9 %collective-permute-start.2 = (f32[16,2560]{1,0:T(8,128)}, f32[16,2560]{1,0:T(8,128)S(1)}, u32[]{:S(2)}, u32[]{:S(2)}) collective-permute-start(f32[16,2560]{1,0:T(8,128)} %get-tuple-element.33), channel_id=1, source_target_pairs={{0,4},{2,6},{4,0},{6,2},{8,12},{10,14},{12,8},{14,10},{1,5},{3,7},... | collective-permute-start | bytes 491528 | tf_op jit(solution)/shard_map/ppermute | solution.py:415
  26.5 29.4 %collective-permute-start.3 = (f32[16,2560]{1,0:T(8,128)}, f32[16,2560]{1,0:T(8,128)S(1)}, u32[]{:S(2)}, u32[]{:S(2)}) collective-permute-start(f32[16,2560]{1,0:T(8,128)} %get-tuple-element.34), channel_id=1, source_target_pairs={{0,6},{2,4},{4,2},{6,0},{8,14},{10,12},{12,10},{14,8},{1,7},{3,5},... | collective-permute-start | bytes 491528 | tf_op jit(solution)/shard_map/ppermute | solution.py:415
  28.0 43.3 %collective-permute-start.4 = (f32[16,2560]{1,0:T(8,128)}, f32[16,2560]{1,0:T(8,128)S(1)}, u32[]{:S(2)}, u32[]{:S(2)}) collective-permute-start(f32[16,2560]{1,0:T(8,128)} %get-tuple-element.35), channel_id=1, source_target_pairs={{0,8},{2,10},{4,12},{6,14},{8,0},{10,2},{12,4},{14,6},{1,9},{3,11}... | collective-permute-start | bytes 491528 | tf_op jit(solution)/shard_map/ppermute | solution.py:415
  30.3 52.3 %collective-permute-start.5 = (f32[16,2560]{1,0:T(8,128)}, f32[16,2560]{1,0:T(8,128)S(1)}, u32[]{:S(2)}, u32[]{:S(2)}) collective-permute-start(f32[16,2560]{1,0:T(8,128)} %get-tuple-element.36), channel_id=1, source_target_pairs={{0,10},{2,8},{4,14},{6,12},{8,2},{10,0},{12,6},{14,4},{1,11},{3,9}... | collective-permute-start | bytes 491528 | tf_op jit(solution)/shard_map/ppermute | solution.py:415
  38.9 44.4 %collective-permute-start.6 = (f32[16,2560]{1,0:T(8,128)}, f32[16,2560]{1,0:T(8,128)S(1)}, u32[]{:S(2)}, u32[]{:S(2)}) collective-permute-start(f32[16,2560]{1,0:T(8,128)} %get-tuple-element.37), channel_id=1, source_target_pairs={{0,12},{2,14},{4,8},{6,10},{8,4},{10,6},{12,0},{14,2},{1,13},{3,15... | collective-permute-start | bytes 491528 | tf_op jit(solution)/shard_map/ppermute | solution.py:415
  53.9 18.1 %collective-permute-start.12 = (f32[128,1920]{1,0:T(8,128)S(1)}, f32[128,1920]{1,0:T(8,128)S(1)}, u32[]{:S(2)}, u32[]{:S(2)}) collective-permute-start(f32[128,1920]{1,0:T(8,128)S(1)} %slice.47), channel_id=1, source_target_pairs={{1,0},{3,2},{5,4},{7,6},{9,8},{11,10},{13,12},{15,14},{17,16},{19,... | collective-permute-start | bytes 2949128 | tf_op jit(solution)/shard_map/ppermute | solution.py:406
  56.0 28.0 %collective-permute-start.7 = (f32[16,2560]{1,0:T(8,128)}, f32[16,2560]{1,0:T(8,128)S(1)}, u32[]{:S(2)}, u32[]{:S(2)}) collective-permute-start(f32[16,2560]{1,0:T(8,128)} %get-tuple-element.38), channel_id=1, source_target_pairs={{0,14},{2,12},{4,10},{6,8},{8,6},{10,4},{12,2},{14,0},{1,15},{3,13... | collective-permute-start | bytes 491528 | tf_op jit(solution)/shard_map/ppermute | solution.py:415
  76.3 45.5 %all-to-all-start.1 = ((f32[8,16,2688]{2,1,0:T(8,128)}), f32[8,16,2688]{2,1,0:T(8,128)S(1)}, u32[]{:S(2)}, u32[]{:S(2)}) async-start(f32[8,16,2688]{2,1,0:T(8,128)} %bitcast.15), calls=%async_computation.1 | async-start | bytes 2752512 | tf_op jit(solution)/shard_map/all_to_all | solution.py:411
  84.7 4.7 %collective-permute-start.8 = (f32[8,16,1920]{2,1,0:T(8,128)}, f32[8,16,1920]{2,1,0:T(8,128)S(1)}, u32[]{:S(2)}, u32[]{:S(2)}) collective-permute-start(f32[8,16,1920]{2,1,0:T(8,128)} %fusion), channel_id=1, source_target_pairs={{1,0},{3,2},{5,4},{7,6},{9,8},{11,10},{13,12},{15,14},{17,16},{19,... | collective-permute-start | bytes 2949128 | tf_op jit(solution)/shard_map/ppermute | solution.py:406
  89.3 0.9 copy-start
  97.2 10.3 %collective-permute-start.9 = (f32[16,2688]{1,0:T(8,128)S(1)}, f32[16,2688]{1,0:T(8,128)S(1)}, u32[]{:S(2)}, u32[]{:S(2)}) collective-permute-start(f32[16,2688]{1,0:T(8,128)S(1)} %get-tuple-element.40), channel_id=1, source_target_pairs={{0,2},{2,0},{4,6},{6,4},{8,10},{10,8},{12,14},{14,12},{1,3},{3,1},... | collective-permute-start | bytes 516104 | tf_op jit(solution)/shard_map/ppermute | solution.py:415
  98.7 12.6 %collective-permute-start.10 = (f32[16,2688]{1,0:T(8,128)S(1)}, f32[16,2688]{1,0:T(8,128)S(1)}, u32[]{:S(2)}, u32[]{:S(2)}) collective-permute-start(f32[16,2688]{1,0:T(8,128)S(1)} %get-tuple-element.41), channel_id=1, source_target_pairs={{0,4},{2,6},{4,0},{6,2},{8,12},{10,14},{12,8},{14,10},{1,5},{3,7},... | collective-permute-start | bytes 516104 | tf_op jit(solution)/shard_map/ppermute | solution.py:415
  99.3 16.8 %collective-permute-start.11 = (f32[16,2688]{1,0:T(8,128)S(1)}, f32[16,2688]{1,0:T(8,128)S(1)}, u32[]{:S(2)}, u32[]{:S(2)}) collective-permute-start(f32[16,2688]{1,0:T(8,128)S(1)} %get-tuple-element.42), channel_id=1, source_target_pairs={{0,6},{2,4},{4,2},{6,0},{8,14},{10,12},{12,10},{14,8},{1,7},{3,5},... | collective-permute-start | bytes 516104 | tf_op jit(solution)/shard_map/ppermute | solution.py:415
  100.7 31.1 %collective-permute-start.13 = (f32[16,2688]{1,0:T(8,128)S(1)}, f32[16,2688]{1,0:T(8,128)S(1)}, u32[]{:S(2)}, u32[]{:S(2)}) collective-permute-start(f32[16,2688]{1,0:T(8,128)S(1)} %get-tuple-element.47), channel_id=1, source_target_pairs={{0,8},{2,10},{4,12},{6,14},{8,0},{10,2},{12,4},{14,6},{1,9},{3,11}... | collective-permute-start | bytes 516104 | tf_op jit(solution)/shard_map/ppermute | solution.py:415
  103.1 32.4 %collective-permute-start.14 = (f32[16,2688]{1,0:T(8,128)S(1)}, f32[16,2688]{1,0:T(8,128)S(1)}, u32[]{:S(2)}, u32[]{:S(2)}) collective-permute-start(f32[16,2688]{1,0:T(8,128)S(1)} %get-tuple-element.48), channel_id=1, source_target_pairs={{0,10},{2,8},{4,14},{6,12},{8,2},{10,0},{12,6},{14,4},{1,11},{3,9}... | collective-permute-start | bytes 516104 | tf_op jit(solution)/shard_map/ppermute | solution.py:415
  107.5 33.8 %collective-permute-start.15 = (f32[16,2688]{1,0:T(8,128)S(1)}, f32[16,2688]{1,0:T(8,128)S(1)}, u32[]{:S(2)}, u32[]{:S(2)}) collective-permute-start(f32[16,2688]{1,0:T(8,128)S(1)} %get-tuple-element.51), channel_id=1, source_target_pairs={{0,12},{2,14},{4,8},{6,10},{8,4},{10,6},{12,0},{14,2},{1,13},{3,15... | collective-permute-start | bytes 516104 | tf_op jit(solution)/shard_map/ppermute | solution.py:415
  111.3 33.4 %collective-permute-start.16 = (f32[16,2688]{1,0:T(8,128)S(1)}, f32[16,2688]{1,0:T(8,128)S(1)}, u32[]{:S(2)}, u32[]{:S(2)}) collective-permute-start(f32[16,2688]{1,0:T(8,128)S(1)} %get-tuple-element.54), channel_id=1, source_target_pairs={{0,14},{2,12},{4,10},{6,8},{8,6},{10,4},{12,2},{14,0},{1,15},{3,13... | collective-permute-start | bytes 516104 | tf_op jit(solution)/shard_map/ppermute | solution.py:415

commit v5 on v4

--- a/solution.py
+++ b/solution.py
@@ -255,7 +255,7 @@
         store.wait()
 
 
-def cross_tree(position, table, parts, rim, rows, freq_count):
+def cross_tree(position, table, parts, rim, rows, freq_count, width):
     count = len(parts)
     size, span = parts[0].shape
     group = size * count
@@ -263,13 +263,13 @@
     hbm = pl.BlockSpec(memory_space=pl.ANY)
     return pl.pallas_call(
         functools.partial(cross_tree_kernel, rows, freq_count, count),
-        out_shape=[jax.ShapeDtypeStruct((size, span + LANES), jnp.float32)] * count,
+        out_shape=[jax.ShapeDtypeStruct((size, width), jnp.float32)] * count,
         in_specs=[pl.BlockSpec(memory_space=pltpu.SMEM)] + [hbm] * (2 + count),
         out_specs=[pl.BlockSpec(memory_space=pltpu.HBM if count == 1 else pl.ANY)] * count,
         scratch_shapes=[
             pltpu.VMEM((group, total), jnp.float32),
             pltpu.VMEM((group, total), jnp.float32),
-            pltpu.VMEM((group, span + LANES), jnp.float32),
+            pltpu.VMEM((group, width), jnp.float32),
             pltpu.VMEM((freq_count.bit_length() - 1, group, LANES), jnp.int32),
             pltpu.VMEM((group, LANES), jnp.int32),
             pltpu.SemaphoreType.DMA((1 + 2 * count,)),
@@ -291,13 +291,21 @@
         pieces = refs[:count]
         starts = [jnp.bitwise_xor(place[0], mask) * share for mask in masks]
     else:
-        pieces = [refs[0].at[pl.ds(n * share, share), :] for n in range(count)]
+        pieces, edges = [
+            [ref.at[pl.ds(n * share, share), :] for n in range(count)] for ref in refs[:2]
+        ]
         starts = [n * share for n in range(count)]
     blocks = out.shape[2] // LANES
     filters = out.shape[0]
-    loads = [pltpu.make_async_copy(pieces[n], values.at[n], in_sem.at[n]) for n in range(count)]
-    for load in loads:
-        load.start()
+    loads = []
+    for n in range(count):
+        whole_piece = values.at[n]
+        if not masks:
+            whole_piece = values.at[n, :, pl.ds(0, blocks * LANES)]
+            edge = values.at[n, :, pl.ds(blocks * LANES, LANES)]
+            pltpu.make_async_copy(edges[n], edge, in_sem.at[count + n]).start()
+        loads.append(pltpu.make_async_copy(pieces[n], whole_piece, in_sem.at[n]))
+        loads[n].start()
     row = lax.broadcasted_iota(jnp.int32, (2 * LANES, 2 * LANES), 0) & (LANES - 1)
     col = lax.broadcasted_iota(jnp.int32, (2 * LANES, 2 * LANES), 1)
     ones = ((row < col) | (col >= LANES)).astype(jnp.bfloat16)
@@ -307,6 +315,9 @@
     for n in range(count):
         slot = n % 2
         loads[n].wait()
+        if not masks:
+            edge = values.at[n, :, pl.ds(blocks * LANES, LANES)]
+            pltpu.make_async_copy(edges[n], edge, in_sem.at[count + n]).wait()
         for j in range(blocks + 1):
             exact = values[n, :, block_of(j)]
             high = exact.astype(jnp.bfloat16)
@@ -358,8 +369,9 @@
             copy.wait()
 
 
-def box_filters(position, widths, scale, earlier, parts, masks, result, rows, base):
+def box_filters(position, widths, scale, earlier, parts, masks, edge, result, rows, base):
     size, reach = parts[0].shape
+    reach += LANES if edge is not None else 0
     share = size if masks else max(n for n in (16, 32) if size % n == 0)
     count = len(parts) * size // share
     span = reach - LANES
@@ -368,6 +380,7 @@
     hbm = pl.BlockSpec(memory_space=pl.ANY)
     smem = pl.BlockSpec(memory_space=pltpu.SMEM)
     operands = [position, widths, scale, earlier, *parts]
+    operands += [] if edge is None else [edge]
     aliases = {}
     if result is not None:
         aliases = {len(operands): 0}
@@ -387,7 +400,7 @@
             pltpu.VMEM((blocks + 1, share, LANES), jnp.float32),
             pltpu.VMEM((blocks + 1, share, LANES), jnp.float32),
             pltpu.VMEM((2, filters, share, span), jnp.float32),
-            pltpu.SemaphoreType.DMA((count,)),
+            pltpu.SemaphoreType.DMA((2 * count,)),
             pltpu.SemaphoreType.DMA((2, filters)),
         ],
         compiler_params=pltpu.CompilerParams(vmem_limit_bytes=FILTER_VMEM),
@@ -432,7 +445,6 @@
     rim = passed_along(spectra[:, :local_rim], "tm", -1)
     table = jnp.pad(delays.T, ((0, 0), (0, LANES - delays.shape[0])))
     scale = 1.0 / jnp.sqrt(widths.astype(jnp.float32) * channels)
-    reach = channels - rows + LANES
     chunks = chunks_of(rows, freq_count)
     made = local_tree(position, spectra, rim, table, chunks, freq_count)
     tables = {}
@@ -448,10 +460,12 @@
         made = made[count:]
     back = []
     for (base, _, count), parts in zip(chunks, arrived):
-        edges = [part[:, :reach] for part in parts]
+        extra = LANES if count > 1 else 0
+        edges = [part[:, : channels - rows + extra] for part in parts]
         rim = passed_along(jnp.stack(edges) if count > 1 else edges[0], "tm", -1)
-        back.append(cross_tree(position, tables[base], parts, rim, rows, freq_count))
+        back.append(cross_tree(position, tables[base], parts, rim, rows, freq_count, span + extra))
     back = [exchanged(parts, freq_count) for parts in back]
+    edge = passed_along(back[1][0][:, :LANES], "tm", -1)
     result, mark = None, jnp.zeros((SUBLANES, LANES), jnp.float32)
     half = freq_count // 2
     turns = [(0, range(half)), (1, ()), (0, range(half, freq_count - 2))]
@@ -460,7 +474,16 @@
         base, parts = chunks[chunk][0], back[chunk]
         some = [parts[mask] for mask in masks] or parts
         result, mark = box_filters(
-            position, widths, scale, mark, some, tuple(masks), result, rows, base
+            position,
+            widths,
+            scale,
+            mark,
+            some,
+            tuple(masks),
+            None if masks else edge,
+            result,
+            rows,
+            base,
         )
     return result
 

time: 151 us -> 150 us (level)
  the two profiles are of different devices: /device:TPU:10 before, /device:TPU:0 now
where the time goes in v5:
time: 150 us; the launch traced here: 149 us
  waiting for transfers between devices  49.9 us (33%)
  Pallas kernels  45.8 us (31%)
  starting transfers between devices  41.1 us (27%)
  local copies, waits for them, and re-layouts  12 us (8%)
    all_to_all x2, waiting for transfers between devices, exchanged(): return [lax.all_to_all(parts[0], 'freq', 0, 0, tiled=True)]  25.7 us
    ppermute x14, starting transfers between devices, exchanged(): result[mask] = lax.ppermute(parts[mask], 'freq', pairs)  24.9 us
    pallas_call x5, Pallas kernels, box_filters(): pl.pallas_call(functools.partial(filter_kernel, base, tuple(masks)), out_...  23.6 us
    ppermute x14, waiting for transfers between devices, exchanged(): result[mask] = lax.ppermute(parts[mask], 'freq', pairs)  20.8 us
    pallas_call x1, Pallas kernels, local_tree(): pl.pallas_call(functools.partial(local_tree_kernel, tuple(chunks), freq_c...  11.9 us
    all_to_all x2, starting transfers between devices, exchanged(): return [lax.all_to_all(parts[0], 'freq', 0, 0, tiled=True)]  10.9 us
    pallas_call x2, Pallas kernels, cross_tree(): pl.pallas_call(functools.partial(cross_tree_kernel, rows, freq_count, cou...  10.3 us
    unnamed x14, local copies, waits for them, and re-layouts  8.36 us
  transfers between devices with their start and end apart: 20, of which 6 were waited for; matrix products, arithmetic and copies ran while one was open for 6% of the time, Pallas kernels for 21%

profile of v5, /device:TPU:0, one launch (start us, length us, event | category | flops | bytes accessed | tf_op | source)
XLA Modules:
  0.0 149.2 jit_solution(8104313358166569444)
XLA Ops:
  1.0 1.3 collective-permute-start
  5.3 11.9 %local_tree.1 = (f32[16,2560]{1,0:T(8,128)}, f32[16,2560]{1,0:T(8,128)}, f32[16,2560]{1,0:T(8,128)}, f32[16,2560]{1,0:T(8,128)}, f32[16,2560]{1,0:T(8,128)}, /*i...) custom-call(s32[1]{0:T(128)} %bitcast.place, f32[256,2560]{1,0:T(8,128)} %spectra.1, ...), custom_call_target="tpu_custom_call" | custom-call | flops 5242880 | bytes 5242880 | tf_op jit(solution)/shard_map/local_tree/pallas_call | solution.py:159
  17.2 7.3 %all-to-all-start = ((f32[8,16,2560]{2,1,0:T(8,128)}), f32[8,16,2560]{2,1,0:T(8,128)S(1)}, u32[]{:S(2)}, u32[]{:S(2)}) async-start(f32[8,16,2560]{2,1,0:T(8,128)} %bitcast.47), calls=%async_computation | async-start | bytes 2621440 | tf_op jit(solution)/shard_map/all_to_all | solution.py:424
  25.4 2.1 %collective-permute-start.1 = (f32[16,2560]{1,0:T(8,128)}, f32[16,2560]{1,0:T(8,128)S(1)}, u32[]{:S(2)}, u32[]{:S(2)}) collective-permute-start(f32[16,2560]{1,0:T(8,128)} %get-tuple-element.32), channel_id=1, source_target_pairs={{0,2},{2,0},{4,6},{6,4},{8,10},{10,8},{12,14},{14,12},{1,3},{3,1},... | collective-permute-start | bytes 491528 | tf_op jit(solution)/shard_map/ppermute | solution.py:428
  27.5 1.5 collective-permute-start.2
  29.0 2.8 %collective-permute-start.4 = (f32[16,2560]{1,0:T(8,128)}, f32[16,2560]{1,0:T(8,128)S(1)}, u32[]{:S(2)}, u32[]{:S(2)}) collective-permute-start(f32[16,2560]{1,0:T(8,128)} %get-tuple-element.35), channel_id=1, source_target_pairs={{0,8},{2,10},{4,12},{6,14},{8,0},{10,2},{12,4},{14,6},{1,9},{3,11}... | collective-permute-start | bytes 491528 | tf_op jit(solution)/shard_map/ppermute | solution.py:428
  31.9 1.5 collective-permute-start.5
  33.3 1.6 %bitcast_dynamic-update-slice_fusion = f32[8,16,1920]{2,1,0:T(8,128)} fusion(f32[16,2560]{1,0:T(8,128)} %get-tuple-element.31.refs_0_), kind=kLoop, calls=%fused_computation.14 | loop fusion | bytes 245760
  34.9 5.8 %collective-permute-done.1.refs_1_ = f32[16,2560]{1,0:T(8,128)S(1)} collective-permute-done((f32[16,2560]{1,0:T(8,128)}, f32[16,2560]{1,0:T(8,128)S(1)}, u32[]{:S(2)}, u32[]{:S(2)}) %collective-permute-start.1) | collective-permute-done | bytes 163872 | tf_op jit(solution)/shard_map/ppermute | solution.py:428
  40.7 2.6 %collective-permute-start.6 = (f32[16,2560]{1,0:T(8,128)}, f32[16,2560]{1,0:T(8,128)S(1)}, u32[]{:S(2)}, u32[]{:S(2)}) collective-permute-start(f32[16,2560]{1,0:T(8,128)} %get-tuple-element.37), channel_id=1, source_target_pairs={{0,12},{2,14},{4,8},{6,10},{8,4},{10,6},{12,0},{14,2},{1,13},{3,15... | collective-permute-start | bytes 491528 | tf_op jit(solution)/shard_map/ppermute | solution.py:428
  43.9 13.8 %all-to-all-done = f32[8,16,2560]{2,1,0:T(8,128)S(1)} async-done(((f32[8,16,2560]{2,1,0:T(8,128)}), f32[8,16,2560]{2,1,0:T(8,128)S(1)}, u32[]{:S(2)}, u32[]{:S(2)}) %all-to-all-start) | async-done | bytes 1310752 | tf_op jit(solution)/shard_map/all_to_all | solution.py:424
  57.7 1.3 collective-permute-start.12
  59.7 1.9 %collective-permute-start.7 = (f32[16,2560]{1,0:T(8,128)}, f32[16,2560]{1,0:T(8,128)S(1)}, u32[]{:S(2)}, u32[]{:S(2)}) collective-permute-start(f32[16,2560]{1,0:T(8,128)} %get-tuple-element.38), channel_id=1, source_target_pairs={{0,14},{2,12},{4,10},{6,8},{8,6},{10,4},{12,2},{14,0},{1,15},{3,13... | collective-permute-start | bytes 491528 | tf_op jit(solution)/shard_map/ppermute | solution.py:428
  62.3 12.9 %collective-permute-done.4.refs_4_ = f32[16,2560]{1,0:T(8,128)S(1)} collective-permute-done((f32[16,2560]{1,0:T(8,128)}, f32[16,2560]{1,0:T(8,128)S(1)}, u32[]{:S(2)}, u32[]{:S(2)}) %collective-permute-start.4) | collective-permute-done | bytes 163872 | tf_op jit(solution)/shard_map/ppermute | solution.py:428
  75.9 4.2 %cross_tree.3 = f32[128,2560]{1,0:T(8,128)} custom-call(s32[1]{0:T(128)} %bitcast.place, s32[128,128]{1,0:T(8,128)S(1)} %bitcast.43, f32[128,1792]{1,0:T(8,128)S(1)} %collective-permute-done.12.rim, f32[128,2560]{1,0:T(8,128)S(1)} %bitcast.40), custom_call_target="tpu_custom_call" | custom-call | flops 1310720 | bytes 2621440 | tf_op jit(solution)/shard_map/cross_tree/pallas_call | solution.py:264
  80.0 3.6 %all-to-all-start.1 = ((f32[8,16,2560]{2,1,0:T(8,128)}), f32[8,16,2560]{2,1,0:T(8,128)S(1)}, u32[]{:S(2)}, u32[]{:S(2)}) async-start(f32[8,16,2560]{2,1,0:T(8,128)} %bitcast.15), calls=%async_computation.1 | async-start | bytes 2621440 | tf_op jit(solution)/shard_map/all_to_all | solution.py:424
  85.6 1.3 collective-permute-start.8
  86.9 3.4 %collective-permute-done.8.rim = f32[8,16,1920]{2,1,0:T(8,128)S(1)} collective-permute-done((f32[8,16,1920]{2,1,0:T(8,128)}, f32[8,16,1920]{2,1,0:T(8,128)S(1)}, u32[]{:S(2)}, u32[]{:S(2)}) %collective-permute-start.8) | collective-permute-done | bytes 983072 | tf_op jit(solution)/shard_map/ppermute | solution.py:419
  91.2 6.2 %cross_tree.2 = (f32[16,2688]{1,0:T(8,128)S(1)}, f32[16,2688]{1,0:T(8,128)}, f32[16,2688]{1,0:T(8,128)}, f32[16,2688]{1,0:T(8,128)}, f32[16,2688]{1,0:T(8,128)S(...) custom-call(s32[1]{0:T(128)} %bitcast.place, s32[128,128]{1,0:T(8,128)S(1)} %bitcast.44, ...), custom_call_target="tpu_custom_call" | custom-call | flops 1310720 | bytes 2621440 | tf_op jit(solution)/shard_map/cross_tree/pallas_call | solution.py:264
  97.4 2.0 %collective-permute-start.9 = (f32[16,2688]{1,0:T(8,128)}, f32[16,2688]{1,0:T(8,128)S(1)}, u32[]{:S(2)}, u32[]{:S(2)}) collective-permute-start(f32[16,2688]{1,0:T(8,128)} %get-tuple-element.40), channel_id=1, source_target_pairs={{0,2},{2,0},{4,6},{6,4},{8,10},{10,8},{12,14},{14,12},{1,3},{3,1},... | collective-permute-start | bytes 516104 | tf_op jit(solution)/shard_map/ppermute | solution.py:428
  99.3 1.5 collective-permute-start.10
  100.9 2.8 %collective-permute-start.14 = (f32[16,2688]{1,0:T(8,128)S(1)}, f32[16,2688]{1,0:T(8,128)S(1)}, u32[]{:S(2)}, u32[]{:S(2)}) collective-permute-start(f32[16,2688]{1,0:T(8,128)S(1)} %get-tuple-element.47), channel_id=1, source_target_pairs={{0,8},{2,10},{4,12},{6,14},{8,0},{10,2},{12,4},{14,6},{1,9},{3,11}... | collective-permute-start | bytes 516104 | tf_op jit(solution)/shard_map/ppermute | solution.py:428
  103.7 1.4 collective-permute-start.15
  105.2 11.9 %all-to-all-done.1 = f32[8,16,2560]{2,1,0:T(8,128)S(1)} async-done(((f32[8,16,2560]{2,1,0:T(8,128)}), f32[8,16,2560]{2,1,0:T(8,128)S(1)}, u32[]{:S(2)}, u32[]{:S(2)}) %all-to-all-start.1) | async-done | bytes 1310752 | tf_op jit(solution)/shard_map/all_to_all | solution.py:424
  118.2 3.5 %collective-permute-start.17 = (f32[16,2688]{1,0:T(8,128)S(1)}, f32[16,2688]{1,0:T(8,128)S(1)}, u32[]{:S(2)}, u32[]{:S(2)}) collective-permute-start(f32[16,2688]{1,0:T(8,128)S(1)} %get-tuple-element.54), channel_id=1, source_target_pairs={{0,14},{2,12},{4,10},{6,8},{8,6},{10,4},{12,2},{14,0},{1,15},{3,13... | collective-permute-start | bytes 516104 | tf_op jit(solution)/shard_map/ppermute | solution.py:428
  121.7 1.5 collective-permute-start.13
  123.2 5.7 %box_filters.5 = (f32[8,256,2560]{2,1,0:T(8,128)}, f32[8,128]{1,0:T(8,128)S(1)}) custom-call(s32[1]{0:T(128)} %bitcast.place, s32[8]{0:T(128)S(1)} %copy-done.1, f32[8]{0:T(128)S(1)} %multiply_rsqrt_fusion.scale, f32[8,128]{1,0:T(8,128)S(1)} %broadcast_in_dim.7.earlier, f32[16,2688]{1,0:T(8,128)S(1)} %get-tuple-element.39.refs_0_, ...), custom_call_target="tpu_custom_call" | custom-call | flops 10485760 | bytes 5898240 | tf_op jit(solution)/shard_map/box_filters/pallas_call | solution.py:388
  129.0 8.2 %box_filters.6 = (f32[8,256,2560]{2,1,0:T(8,128)}, f32[8,128]{1,0:T(8,128)S(1)}) custom-call(s32[1]{0:T(128)} %bitcast.place, s32[8]{0:T(128)S(1)} %copy-done.1, f32[8]{0:T(128)S(1)} %multiply_rsqrt_fusion.scale, f32[8,128]{1,0:T(8,128)S(1)} %get-tuple-element.43.earlier, f32[128,2560]{1,0:T(8,128)S(1)} %bitcast.42, ...), custom_call_target="tpu_custom_call", output_to_operand_aliasing={{0}: (6, {})} | custom-call | flops 20971520 | bytes 11796480 | tf_op jit(solution)/shard_map/box_filters/pallas_call | solution.py:388
  137.2 2.1 %collective-permute-done.15.refs_1_ = f32[16,2688]{1,0:T(8,128)S(1)} collective-permute-done((f32[16,2688]{1,0:T(8,128)S(1)}, f32[16,2688]{1,0:T(8,128)S(1)}, u32[]{:S(2)}, u32[]{:S(2)}) %collective-permute-start.15) | collective-permute-done | bytes 172064 | tf_op jit(solution)/shard_map/ppermute | solution.py:428
  139.3 3.7 %box_filters.7 = (f32[8,256,2560]{2,1,0:T(8,128)}, f32[8,128]{1,0:T(8,128)S(1)}) custom-call(s32[1]{0:T(128)} %bitcast.place, s32[8]{0:T(128)S(1)} %copy-done.1, f32[8]{0:T(128)S(1)} %multiply_rsqrt_fusion.scale, f32[8,128]{1,0:T(8,128)S(1)} %get-tuple-element.46.earlier, ...), custom_call_target="tpu_custom_call", output_to_operand_aliasing={{0}: (6, {})} | custom-call | flops 5242880 | bytes 2949120 | tf_op jit(solution)/shard_map/box_filters/pallas_call | solution.py:388
  143.0 2.7 %box_filters.8 = (f32[8,256,2560]{2,1,0:T(8,128)}, f32[8,128]{1,0:T(8,128)S(1)}) custom-call(s32[1]{0:T(128)} %bitcast.place, s32[8]{0:T(128)S(1)} %copy-done.1, f32[8]{0:T(128)S(1)} %multiply_rsqrt_fusion.scale, f32[8,128]{1,0:T(8,128)S(1)} %get-tuple-element.50.earlier, ...), custom_call_target="tpu_custom_call", output_to_operand_aliasing={{0}: (5, {})} | custom-call | flops 2621440 | bytes 1474560 | tf_op jit(solution)/shard_map/box_filters/pallas_call | solution.py:388
  145.7 3.3 %box_filters.9 = (f32[8,256,2560]{2,1,0:T(8,128)}, f32[8,128]{1,0:T(8,128)}) custom-call(s32[1]{0:T(128)} %bitcast.place, s32[8]{0:T(128)S(1)} %copy-done.1, f32[8]{0:T(128)S(1)} %multiply_rsqrt_fusion.scale, f32[8,128]{1,0:T(8,128)S(1)} %get-tuple-element.53.earlier, ...), custom_call_target="tpu_custom_call", output_to_operand_aliasing={{0}: (5, {})} | custom-call | flops 2621440 | bytes 1474560 | tf_op jit(solution)/shard_map/box_filters/pallas_call | solution.py:388
  (38 shorter events, 11.8 us)
Async XLA Ops:
  0.0 123.2 %copy-start.1 = (s32[8]{0:T(128)S(1)}, s32[8]{0:T(128)}, u32[]{:S(2)}) copy-start(s32[8]{0:T(128)} %widths.9) | copy-start | bytes 100
  1.0 3.6 %collective-permute-start = (f32[256,256]{1,0:T(8,128)S(1)}, f32[256,256]{1,0:T(8,128)S(1)}, u32[]{:S(2)}, u32[]{:S(2)}) collective-permute-start(f32[256,256]{1,0:T(8,128)S(1)} %slice.33), channel_id=1, source_target_pairs={{1,0},{3,2},{5,4},{7,6},{9,8},{11,10},{13,12},{15,14},{17,16},{19,... | collective-permute-start | bytes 786440 | tf_op jit(solution)/shard_map/ppermute | solution.py:419
  4.6 0.7 copy-start.2
  17.2 40.4 %all-to-all-start = ((f32[8,16,2560]{2,1,0:T(8,128)}), f32[8,16,2560]{2,1,0:T(8,128)S(1)}, u32[]{:S(2)}, u32[]{:S(2)}) async-start(f32[8,16,2560]{2,1,0:T(8,128)} %bitcast.47), calls=%async_computation | async-start | bytes 2621440 | tf_op jit(solution)/shard_map/all_to_all | solution.py:424
  25.4 15.3 %collective-permute-start.1 = (f32[16,2560]{1,0:T(8,128)}, f32[16,2560]{1,0:T(8,128)S(1)}, u32[]{:S(2)}, u32[]{:S(2)}) collective-permute-start(f32[16,2560]{1,0:T(8,128)} %get-tuple-element.32), channel_id=1, source_target_pairs={{0,2},{2,0},{4,6},{6,4},{8,10},{10,8},{12,14},{14,12},{1,3},{3,1},... | collective-permute-start | bytes 491528 | tf_op jit(solution)/shard_map/ppermute | solution.py:428
  27.5 30.2 %collective-permute-start.2 = (f32[16,2560]{1,0:T(8,128)}, f32[16,2560]{1,0:T(8,128)S(1)}, u32[]{:S(2)}, u32[]{:S(2)}) collective-permute-start(f32[16,2560]{1,0:T(8,128)} %get-tuple-element.33), channel_id=1, source_target_pairs={{0,4},{2,6},{4,0},{6,2},{8,12},{10,14},{12,8},{14,10},{1,5},{3,7},... | collective-permute-start | bytes 491528 | tf_op jit(solution)/shard_map/ppermute | solution.py:428
  29.0 30.7 %collective-permute-start.3 = (f32[16,2560]{1,0:T(8,128)}, f32[16,2560]{1,0:T(8,128)S(1)}, u32[]{:S(2)}, u32[]{:S(2)}) collective-permute-start(f32[16,2560]{1,0:T(8,128)} %get-tuple-element.34), channel_id=1, source_target_pairs={{0,6},{2,4},{4,2},{6,0},{8,14},{10,12},{12,10},{14,8},{1,7},{3,5},... | collective-permute-start | bytes 491528 | tf_op jit(solution)/shard_map/ppermute | solution.py:428
  29.0 46.2 %collective-permute-start.4 = (f32[16,2560]{1,0:T(8,128)}, f32[16,2560]{1,0:T(8,128)S(1)}, u32[]{:S(2)}, u32[]{:S(2)}) collective-permute-start(f32[16,2560]{1,0:T(8,128)} %get-tuple-element.35), channel_id=1, source_target_pairs={{0,8},{2,10},{4,12},{6,14},{8,0},{10,2},{12,4},{14,6},{1,9},{3,11}... | collective-permute-start | bytes 491528 | tf_op jit(solution)/shard_map/ppermute | solution.py:428
  31.9 51.8 %collective-permute-start.5 = (f32[16,2560]{1,0:T(8,128)}, f32[16,2560]{1,0:T(8,128)S(1)}, u32[]{:S(2)}, u32[]{:S(2)}) collective-permute-start(f32[16,2560]{1,0:T(8,128)} %get-tuple-element.36), channel_id=1, source_target_pairs={{0,10},{2,8},{4,14},{6,12},{8,2},{10,0},{12,6},{14,4},{1,11},{3,9}... | collective-permute-start | bytes 491528 | tf_op jit(solution)/shard_map/ppermute | solution.py:428
  40.7 43.6 %collective-permute-start.6 = (f32[16,2560]{1,0:T(8,128)}, f32[16,2560]{1,0:T(8,128)S(1)}, u32[]{:S(2)}, u32[]{:S(2)}) collective-permute-start(f32[16,2560]{1,0:T(8,128)} %get-tuple-element.37), channel_id=1, source_target_pairs={{0,12},{2,14},{4,8},{6,10},{8,4},{10,6},{12,0},{14,2},{1,13},{3,15... | collective-permute-start | bytes 491528 | tf_op jit(solution)/shard_map/ppermute | solution.py:428
  57.7 18.1 %collective-permute-start.12 = (f32[128,1792]{1,0:T(8,128)S(1)}, f32[128,1792]{1,0:T(8,128)S(1)}, u32[]{:S(2)}, u32[]{:S(2)}) collective-permute-start(f32[128,1792]{1,0:T(8,128)S(1)} %slice.51), channel_id=1, source_target_pairs={{1,0},{3,2},{5,4},{7,6},{9,8},{11,10},{13,12},{15,14},{17,16},{19,... | collective-permute-start | bytes 2752520 | tf_op jit(solution)/shard_map/ppermute | solution.py:419
  59.7 25.3 %collective-permute-start.7 = (f32[16,2560]{1,0:T(8,128)}, f32[16,2560]{1,0:T(8,128)S(1)}, u32[]{:S(2)}, u32[]{:S(2)}) collective-permute-start(f32[16,2560]{1,0:T(8,128)} %get-tuple-element.38), channel_id=1, source_target_pairs={{0,14},{2,12},{4,10},{6,8},{8,6},{10,4},{12,2},{14,0},{1,15},{3,13... | collective-permute-start | bytes 491528 | tf_op jit(solution)/shard_map/ppermute | solution.py:428
  80.0 37.0 %all-to-all-start.1 = ((f32[8,16,2560]{2,1,0:T(8,128)}), f32[8,16,2560]{2,1,0:T(8,128)S(1)}, u32[]{:S(2)}, u32[]{:S(2)}) async-start(f32[8,16,2560]{2,1,0:T(8,128)} %bitcast.15), calls=%async_computation.1 | async-start | bytes 2621440 | tf_op jit(solution)/shard_map/all_to_all | solution.py:424
  85.6 4.7 %collective-permute-start.8 = (f32[8,16,1920]{2,1,0:T(8,128)}, f32[8,16,1920]{2,1,0:T(8,128)S(1)}, u32[]{:S(2)}, u32[]{:S(2)}) collective-permute-start(f32[8,16,1920]{2,1,0:T(8,128)} %fusion), channel_id=1, source_target_pairs={{1,0},{3,2},{5,4},{7,6},{9,8},{11,10},{13,12},{15,14},{17,16},{19,... | collective-permute-start | bytes 2949128 | tf_op jit(solution)/shard_map/ppermute | solution.py:419
  90.3 0.9 copy-start
  97.4 19.7 %collective-permute-start.9 = (f32[16,2688]{1,0:T(8,128)}, f32[16,2688]{1,0:T(8,128)S(1)}, u32[]{:S(2)}, u32[]{:S(2)}) collective-permute-start(f32[16,2688]{1,0:T(8,128)} %get-tuple-element.40), channel_id=1, source_target_pairs={{0,2},{2,0},{4,6},{6,4},{8,10},{10,8},{12,14},{14,12},{1,3},{3,1},... | collective-permute-start | bytes 516104 | tf_op jit(solution)/shard_map/ppermute | solution.py:428
  99.3 18.9 %collective-permute-start.10 = (f32[16,2688]{1,0:T(8,128)}, f32[16,2688]{1,0:T(8,128)S(1)}, u32[]{:S(2)}, u32[]{:S(2)}) collective-permute-start(f32[16,2688]{1,0:T(8,128)} %get-tuple-element.41), channel_id=1, source_target_pairs={{0,4},{2,6},{4,0},{6,2},{8,12},{10,14},{12,8},{14,10},{1,5},{3,7},... | collective-permute-start | bytes 516104 | tf_op jit(solution)/shard_map/ppermute | solution.py:428
  100.8 20.9 %collective-permute-start.11 = (f32[16,2688]{1,0:T(8,128)}, f32[16,2688]{1,0:T(8,128)S(1)}, u32[]{:S(2)}, u32[]{:S(2)}) collective-permute-start(f32[16,2688]{1,0:T(8,128)} %get-tuple-element.42), channel_id=1, source_target_pairs={{0,6},{2,4},{4,2},{6,0},{8,14},{10,12},{12,10},{14,8},{1,7},{3,5},... | collective-permute-start | bytes 516104 | tf_op jit(solution)/shard_map/ppermute | solution.py:428
  100.9 36.3 %collective-permute-start.14 = (f32[16,2688]{1,0:T(8,128)S(1)}, f32[16,2688]{1,0:T(8,128)S(1)}, u32[]{:S(2)}, u32[]{:S(2)}) collective-permute-start(f32[16,2688]{1,0:T(8,128)S(1)} %get-tuple-element.47), channel_id=1, source_target_pairs={{0,8},{2,10},{4,12},{6,14},{8,0},{10,2},{12,4},{14,6},{1,9},{3,11}... | collective-permute-start | bytes 516104 | tf_op jit(solution)/shard_map/ppermute | solution.py:428
  103.7 35.5 %collective-permute-start.15 = (f32[16,2688]{1,0:T(8,128)S(1)}, f32[16,2688]{1,0:T(8,128)S(1)}, u32[]{:S(2)}, u32[]{:S(2)}) collective-permute-start(f32[16,2688]{1,0:T(8,128)S(1)} %get-tuple-element.48), channel_id=1, source_target_pairs={{0,10},{2,8},{4,14},{6,12},{8,2},{10,0},{12,6},{14,4},{1,11},{3,9}... | collective-permute-start | bytes 516104 | tf_op jit(solution)/shard_map/ppermute | solution.py:428
  117.1 25.9 %collective-permute-start.16 = (f32[16,2688]{1,0:T(8,128)S(1)}, f32[16,2688]{1,0:T(8,128)S(1)}, u32[]{:S(2)}, u32[]{:S(2)}) collective-permute-start(f32[16,2688]{1,0:T(8,128)S(1)} %get-tuple-element.51), channel_id=1, source_target_pairs={{0,12},{2,14},{4,8},{6,10},{8,4},{10,6},{12,0},{14,2},{1,13},{3,15... | collective-permute-start | bytes 516104 | tf_op jit(solution)/shard_map/ppermute | solution.py:428
  118.2 27.5 %collective-permute-start.17 = (f32[16,2688]{1,0:T(8,128)S(1)}, f32[16,2688]{1,0:T(8,128)S(1)}, u32[]{:S(2)}, u32[]{:S(2)}) collective-permute-start(f32[16,2688]{1,0:T(8,128)S(1)} %get-tuple-element.54), channel_id=1, source_target_pairs={{0,14},{2,12},{4,10},{6,8},{8,6},{10,4},{12,2},{14,0},{1,15},{3,13... | collective-permute-start | bytes 516104 | tf_op jit(solution)/shard_map/ppermute | solution.py:428
  121.7 7.2 %collective-permute-start.13 = (f32[128,128]{1,0:T(8,128)S(1)}, f32[128,128]{1,0:T(8,128)S(1)}, u32[]{:S(2)}, u32[]{:S(2)}) collective-permute-start(f32[128,128]{1,0:T(8,128)S(1)} %slice.52), channel_id=1, source_target_pairs={{1,0},{3,2},{5,4},{7,6},{9,8},{11,10},{13,12},{15,14},{17,16},{19,... | collective-permute-start | bytes 196616 | tf_op jit(solution)/shard_map/ppermute | solution.py:419
